TPU v7x, 32 devices: a whole 2x2x4 slice. The times are simulated.
32 devices in a mesh: kern: 4 (over y, x), tile: 8 (over z, core).
Axes of the slice: x: 2, y: 2, z: 4, core: 2. Of those that a mesh axis runs over, the one named last changes fastest.
Arguments:
- diag_tiles: float32 [4, 8, 512, 512], P('kern', 'tile'), may hold values from -0.25 to 0.25
- left_factors: float32 [4, 8, 8, 80, 512], P('kern', 'tile'), may hold values from -0.25 to 0.25
- right_factors: float32 [4, 8, 12, 80, 512], P('kern', 'tile'), may hold values from -0.25 to 0.25
- tile_offsets: int32 [4, 8, 8], P('kern', 'tile'), may hold values from -6 to 6, as said below
- tile_ranks: int32 [4, 8, 8], P('kern', 'tile'), may hold values from 32 to 80
- mixing: float32 [64, 4, 4], replicated, may hold values from -3 to 3
- block_index: int32 [4096], P('tile'), may hold values from 0 to 63
- rhs_field: float32 [4, 4096, 128], P('kern', 'tile'), may hold values from -6 to 6
Outputs:
- product: float32 [4, 4096, 128], P('kern', 'tile')
Inputs may be any that keep to these rules, and one draw needn't show every extreme that they name: `tile_offsets`: each row's 8 offsets are distinct and nonzero.
All inputs are finite; a program needn't handle non-finite values.
Results may differ from a plain program's by a relative error of at most 0.00007.
Values sent between devices are 32-bit elements; how exact they have to be, the bound alone decides.
No kernel may reach another device: no remote copies, remote signals or barrier semaphores. Data moves between devices by JAX's collectives and lax.ppermute only.
A program may use at most 64 MiB of HBM per device.

v0:
```python
import jax
import jax.numpy as jnp
from jax import lax
from jax.sharding import PartitionSpec as P

REACH = 6


highest = lax.Precision.HIGHEST


def shifted(value, axis, steps):
    count = lax.axis_size(axis)
    pairs = [(source, (source + steps) % count) for source in range(count)]
    return lax.ppermute(value, axis, pairs)


def deliver(coeffs):
    arrived = []
    for which in range(2 * REACH):
        offset_val = which - REACH if which < REACH else which - REACH + 1
        arrived.append(shifted(coeffs[which], "tile", -offset_val))
    return jnp.stack(arrived)


def apply_kernel(diag_tile, left_tile, right_tile, offsets_row, ranks_row, column_vals):
    coeffs = jnp.einsum("sqp,pc->sqc", right_tile, column_vals, precision=highest)
    arrived = deliver(coeffs)
    slot_pick = jnp.where(offsets_row < 0, offsets_row + REACH, offsets_row + REACH - 1)
    picker = (slot_pick[:, None] == jnp.arange(2 * REACH)[None, :]).astype(jnp.float32)
    chosen = jnp.einsum("ks,sqc->kqc", picker, arrived, precision=highest)
    keeper = (jnp.arange(left_tile.shape[1])[None, :] < ranks_row[:, None]).astype(jnp.float32)
    chosen = chosen * keeper[:, :, None]
    result = jnp.dot(diag_tile, column_vals, precision=highest, preferred_element_type=jnp.float32)
    return result + jnp.einsum("kqp,kqc->pc", left_tile, chosen, precision=highest)


def local(
    diag_tiles,
    left_factors,
    right_factors,
    tile_offsets,
    tile_ranks,
    mixing,
    block_index,
    rhs_field,
):
    diag_tile = diag_tiles[0, 0]
    left_tile = left_factors[0, 0]
    right_tile = right_factors[0, 0]
    offsets_row = tile_offsets[0, 0]
    ranks_row = tile_ranks[0, 0]
    first = apply_kernel(diag_tile, left_tile, right_tile, offsets_row, ranks_row, rhs_field[0])
    own_group = lax.axis_index("kern")
    table_len = mixing.shape[0]
    grouped = lax.all_to_all(first[None], "kern", split_axis=1, concat_axis=0, tiled=True)
    part_len = grouped.shape[1]
    local_index = lax.dynamic_slice_in_dim(block_index, own_group * part_len, part_len)
    picker = (jnp.arange(table_len)[:, None] == local_index[None, :]).astype(jnp.float32)
    full_mix = jnp.einsum("nab,nl->abl", mixing, picker, precision=highest)
    blended = jnp.einsum("abl,blc->alc", full_mix, grouped, precision=highest)
    mixed = lax.all_to_all(blended, "kern", split_axis=0, concat_axis=1, tiled=True)[0]
    second = apply_kernel(diag_tile, left_tile, right_tile, offsets_row, ranks_row, mixed)
    return second[None]


def solution(mesh):
    in_specs = (
        P("kern", "tile", None, None),
        P("kern", "tile", None, None, None),
        P("kern", "tile", None, None, None),
        P("kern", "tile", None),
        P("kern", "tile", None),
        P(),
        P("tile"),
        P("kern", "tile", None),
    )
    out_specs = P("kern", "tile", None)
    return jax.shard_map(local, mesh=mesh, in_specs=in_specs, out_specs=out_specs, check_vma=False)
```

profile of v0, /device:TPU:0, one launch (start us, length us, event | category | flops | bytes accessed | tf_op | source)
XLA Modules:
  0.0 117.8 jit_solution(16457110280662532400)
XLA Ops:
  1.5 2.6 %fusion.2 = f32[12,80,128]{2,1,0:T(8,128)S(1)} fusion(f32[1,1,12,80,512]{4,3,2,1,0:T(8,128)S(1)} %copy-done, f32[1,512,128]{2,1,0:T(8,128)} %param.15), kind=kOutput, calls=%fused_computation.2 | convolution fusion | flops 754974720 | bytes 2719744 | tf_op jit(solution)/shard_map/sqp,pc->sqc/dot_general | solution.py:27
  5.0 3.0 %collective-permute-start.11 = (f32[80,128]{1,0:T(8,128)}, f32[80,128]{1,0:T(8,128)S(1)}, u32[]{:S(2)}, u32[]{:S(2)}) collective-permute-start(f32[80,128]{1,0:T(8,128)} %get-tuple-element.17), channel_id=1, source_target_pairs={{0,2},{1,3},{2,4},{3,5},{4,6},{5,7},{6,0},{7,1},{8,10},{9,11},{10,... | collective-permute-start | bytes 122888 | tf_op jit(solution)/shard_map/ppermute | solution.py:15
  10.6 2.3 %collective-permute-start.8 = (f32[80,128]{1,0:T(8,128)}, f32[80,128]{1,0:T(8,128)S(1)}, u32[]{:S(2)}, u32[]{:S(2)}) collective-permute-start(f32[80,128]{1,0:T(8,128)} %get-tuple-element.20), channel_id=1, source_target_pairs={{0,5},{1,6},{2,7},{3,0},{4,1},{5,2},{6,3},{7,4},{8,13},{9,14},{10,... | collective-permute-start | bytes 122888 | tf_op jit(solution)/shard_map/ppermute | solution.py:15
  17.2 4.0 %collective-permute-done.1 = f32[80,128]{1,0:T(8,128)S(1)} collective-permute-done((f32[80,128]{1,0:T(8,128)}, f32[80,128]{1,0:T(8,128)S(1)}, u32[]{:S(2)}, u32[]{:S(2)}) %collective-permute-start.1) | collective-permute-done | bytes 40992 | tf_op jit(solution)/shard_map/ppermute | solution.py:15
  21.2 5.6 %collective-permute-done.2 = f32[80,128]{1,0:T(8,128)S(1)} collective-permute-done((f32[80,128]{1,0:T(8,128)}, f32[80,128]{1,0:T(8,128)S(1)}, u32[]{:S(2)}, u32[]{:S(2)}) %collective-permute-start.2) | collective-permute-done | bytes 40992 | tf_op jit(solution)/shard_map/ppermute | solution.py:15
  26.9 4.5 %collective-permute-done.3 = f32[80,128]{1,0:T(8,128)S(1)} collective-permute-done((f32[80,128]{1,0:T(8,128)}, f32[80,128]{1,0:T(8,128)S(1)}, u32[]{:S(2)}, u32[]{:S(2)}) %collective-permute-start.3) | collective-permute-done | bytes 40992 | tf_op jit(solution)/shard_map/ppermute | solution.py:15
  33.1 4.7 %collective-permute-done.4 = f32[80,128]{1,0:T(8,128)S(1)} collective-permute-done((f32[80,128]{1,0:T(8,128)}, f32[80,128]{1,0:T(8,128)S(1)}, u32[]{:S(2)}, u32[]{:S(2)}) %collective-permute-start.4) | collective-permute-done | bytes 40992 | tf_op jit(solution)/shard_map/ppermute | solution.py:15
  37.9 5.3 %collective-permute-done.5 = f32[80,128]{1,0:T(8,128)S(1)} collective-permute-done((f32[80,128]{1,0:T(8,128)}, f32[80,128]{1,0:T(8,128)S(1)}, u32[]{:S(2)}, u32[]{:S(2)}) %collective-permute-start.5) | collective-permute-done | bytes 40992 | tf_op jit(solution)/shard_map/ppermute | solution.py:15
  43.2 2.0 %collective-permute-done.6 = f32[80,128]{1,0:T(8,128)S(1)} collective-permute-done((f32[80,128]{1,0:T(8,128)}, f32[80,128]{1,0:T(8,128)S(1)}, u32[]{:S(2)}, u32[]{:S(2)}) %collective-permute-start.6) | collective-permute-done | bytes 40992 | tf_op jit(solution)/shard_map/ppermute | solution.py:15
  45.3 4.1 %collective-permute-done.7 = f32[80,128]{1,0:T(8,128)S(1)} collective-permute-done((f32[80,128]{1,0:T(8,128)}, f32[80,128]{1,0:T(8,128)S(1)}, u32[]{:S(2)}, u32[]{:S(2)}) %collective-permute-start.7) | collective-permute-done | bytes 40992 | tf_op jit(solution)/shard_map/ppermute | solution.py:15
  50.0 2.8 %fusion.11 = f32[512,128]{1,0:T(8,128)S(1)} fusion(f32[8,80,128]{2,0,1:T(8,128)S(1)} %convolution_multiply_fusion.1, f32[8,80,512]{2,1,0:T(8,128)S(1)} %bitcast.153), kind=kOutput, calls=%fused_computation.12 | convolution fusion | flops 503316480 | bytes 1900544 | tf_op jit(solution)/shard_map/kqp,kqc->pc/dot_general | solution.py:35
  54.5 3.7 %all-to-all-start = ((f32[1,512,128]{2,0,1:T(1,128)}), f32[1,512,128]{2,0,1:T(1,128)S(1)}, u32[]{:S(2)}, u32[]{:S(2)}) async-start(f32[1,512,128]{2,0,1:T(1,128)} %bitcast.158), calls=%async_computation | async-start | bytes 524288 | tf_op jit(solution)/shard_map/all_to_all | solution.py:56
  59.9 4.5 %all-to-all-done = f32[1,512,128]{2,0,1:T(1,128)S(1)} async-done(((f32[1,512,128]{2,0,1:T(1,128)}), f32[1,512,128]{2,0,1:T(1,128)S(1)}, u32[]{:S(2)}, u32[]{:S(2)}) %all-to-all-start) | async-done | bytes 262176 | tf_op jit(solution)/shard_map/all_to_all | solution.py:56
  64.3 2.0 %convolution_bitcast_fusion = f32[4,128,128]{2,0,1:T(4,128)S(1)} fusion(f32[4,4,128]{1,0,2:T(4,128)} %copy.30, f32[4,128,128]{2,1,0:T(8,128)S(1)} %bitcast.157), kind=kOutput, calls=%fused_computation.11 | convolution fusion | flops 3145728 | bytes 532480 | tf_op jit(solution)/shard_map/abl,blc->alc/dot_general | solution.py:61
  66.4 8.3 %all_to_all.21 = f32[4,128,128]{2,1,0:T(8,128)S(1)} all-to-all(f32[4,128,128]{2,1,0:T(8,128)S(1)} %copy.31), channel_id=1, replica_groups=mesh['kern'=4,'tile'=8] {'kern'}, dimensions={0} | all-to-all | bytes 524288 | tf_op jit(solution)/shard_map/all_to_all | solution.py:62
  76.4 1.9 %collective-permute-start.12 = (f32[80,128]{1,0:T(8,128)S(1)}, f32[80,128]{1,0:T(8,128)S(1)}, u32[]{:S(2)}, u32[]{:S(2)}) collective-permute-start(f32[80,128]{1,0:T(8,128)S(1)} %get-tuple-element.16), channel_id=1, source_target_pairs={{0,6},{1,7},{2,0},{3,1},{4,2},{5,3},{6,4},{7,5},{8,14},{9,15},{10,... | collective-permute-start | bytes 122888 | tf_op jit(solution)/shard_map/ppermute | solution.py:15
  78.5 3.5 %collective-permute-start.21 = (f32[80,128]{1,0:T(8,128)S(1)}, f32[80,128]{1,0:T(8,128)S(1)}, u32[]{:S(2)}, u32[]{:S(2)}) collective-permute-start(f32[80,128]{1,0:T(8,128)S(1)} %get-tuple-element.7), channel_id=1, source_target_pairs={{0,4},{1,5},{2,6},{3,7},{4,0},{5,1},{6,2},{7,3},{8,12},{9,13},{10,... | collective-permute-start | bytes 122888 | tf_op jit(solution)/shard_map/ppermute | solution.py:15
  83.9 3.0 %collective-permute-done.13 = f32[80,128]{1,0:T(8,128)S(1)} collective-permute-done((f32[80,128]{1,0:T(8,128)S(1)}, f32[80,128]{1,0:T(8,128)S(1)}, u32[]{:S(2)}, u32[]{:S(2)}) %collective-permute-start.13) | collective-permute-done | bytes 40992 | tf_op jit(solution)/shard_map/ppermute | solution.py:15
  88.4 3.9 %collective-permute-done.14 = f32[80,128]{1,0:T(8,128)S(1)} collective-permute-done((f32[80,128]{1,0:T(8,128)S(1)}, f32[80,128]{1,0:T(8,128)S(1)}, u32[]{:S(2)}, u32[]{:S(2)}) %collective-permute-start.14) | collective-permute-done | bytes 40992 | tf_op jit(solution)/shard_map/ppermute | solution.py:15
  92.3 4.3 %collective-permute-done.15 = f32[80,128]{1,0:T(8,128)S(1)} collective-permute-done((f32[80,128]{1,0:T(8,128)S(1)}, f32[80,128]{1,0:T(8,128)S(1)}, u32[]{:S(2)}, u32[]{:S(2)}) %collective-permute-start.15) | collective-permute-done | bytes 40992 | tf_op jit(solution)/shard_map/ppermute | solution.py:15
  96.6 2.4 %collective-permute-start.16 = (f32[80,128]{1,0:T(8,128)S(1)}, f32[80,128]{1,0:T(8,128)S(1)}, u32[]{:S(2)}, u32[]{:S(2)}) collective-permute-start(f32[80,128]{1,0:T(8,128)S(1)} %get-tuple-element.12), channel_id=1, source_target_pairs={{0,2},{1,3},{2,4},{3,5},{4,6},{5,7},{6,0},{7,1},{8,10},{9,11},{10,... | collective-permute-start | bytes 122888 | tf_op jit(solution)/shard_map/ppermute | solution.py:15
  99.0 3.6 %collective-permute-done.16 = f32[80,128]{1,0:T(8,128)S(1)} collective-permute-done((f32[80,128]{1,0:T(8,128)S(1)}, f32[80,128]{1,0:T(8,128)S(1)}, u32[]{:S(2)}, u32[]{:S(2)}) %collective-permute-start.16) | collective-permute-done | bytes 40992 | tf_op jit(solution)/shard_map/ppermute | solution.py:15
  102.7 5.1 %collective-permute-done.17 = f32[80,128]{1,0:T(8,128)S(1)} collective-permute-done((f32[80,128]{1,0:T(8,128)S(1)}, f32[80,128]{1,0:T(8,128)S(1)}, u32[]{:S(2)}, u32[]{:S(2)}) %collective-permute-start.17) | collective-permute-done | bytes 40992 | tf_op jit(solution)/shard_map/ppermute | solution.py:15
  109.5 4.0 %collective-permute-done.19 = f32[80,128]{1,0:T(8,128)S(1)} collective-permute-done((f32[80,128]{1,0:T(8,128)S(1)}, f32[80,128]{1,0:T(8,128)S(1)}, u32[]{:S(2)}, u32[]{:S(2)}) %collective-permute-start.19) | collective-permute-done | bytes 40992 | tf_op jit(solution)/shard_map/ppermute | solution.py:15
  (93 shorter events, 26.3 us)
Async XLA Ops:
  5.0 44.5 %collective-permute-start.11 = (f32[80,128]{1,0:T(8,128)}, f32[80,128]{1,0:T(8,128)S(1)}, u32[]{:S(2)}, u32[]{:S(2)}) collective-permute-start(f32[80,128]{1,0:T(8,128)} %get-tuple-element.17), channel_id=1, source_target_pairs={{0,2},{1,3},{2,4},{3,5},{4,6},{5,7},{6,0},{7,1},{8,10},{9,11},{10,... | collective-permute-start | bytes 122888 | tf_op jit(solution)/shard_map/ppermute | solution.py:15
  8.0 41.4 %collective-permute-start.10 = (f32[80,128]{1,0:T(8,128)}, f32[80,128]{1,0:T(8,128)S(1)}, u32[]{:S(2)}, u32[]{:S(2)}) collective-permute-start(f32[80,128]{1,0:T(8,128)} %get-tuple-element.18), channel_id=1, source_target_pairs={{0,3},{1,4},{2,5},{3,6},{4,7},{5,0},{6,1},{7,2},{8,11},{9,12},{10,... | collective-permute-start | bytes 122888 | tf_op jit(solution)/shard_map/ppermute | solution.py:15
  8.7 40.7 %collective-permute-start.9 = (f32[80,128]{1,0:T(8,128)}, f32[80,128]{1,0:T(8,128)S(1)}, u32[]{:S(2)}, u32[]{:S(2)}) collective-permute-start(f32[80,128]{1,0:T(8,128)} %get-tuple-element.19), channel_id=1, source_target_pairs={{0,4},{1,5},{2,6},{3,7},{4,0},{5,1},{6,2},{7,3},{8,12},{9,13},{10,... | collective-permute-start | bytes 122888 | tf_op jit(solution)/shard_map/ppermute | solution.py:15
  10.6 38.8 %collective-permute-start.8 = (f32[80,128]{1,0:T(8,128)}, f32[80,128]{1,0:T(8,128)S(1)}, u32[]{:S(2)}, u32[]{:S(2)}) collective-permute-start(f32[80,128]{1,0:T(8,128)} %get-tuple-element.20), channel_id=1, source_target_pairs={{0,5},{1,6},{2,7},{3,0},{4,1},{5,2},{6,3},{7,4},{8,13},{9,14},{10,... | collective-permute-start | bytes 122888 | tf_op jit(solution)/shard_map/ppermute | solution.py:15
  13.0 4.2 %collective-permute-start = (f32[80,128]{1,0:T(8,128)}, f32[80,128]{1,0:T(8,128)S(1)}, u32[]{:S(2)}, u32[]{:S(2)}) collective-permute-start(f32[80,128]{1,0:T(8,128)} %get-tuple-element.28), channel_id=1, source_target_pairs={{0,6},{1,7},{2,0},{3,1},{4,2},{5,3},{6,4},{7,5},{8,14},{9,15},{10,... | collective-permute-start | bytes 122888 | tf_op jit(solution)/shard_map/ppermute | solution.py:15
  17.2 4.0 %collective-permute-start.1 = (f32[80,128]{1,0:T(8,128)}, f32[80,128]{1,0:T(8,128)S(1)}, u32[]{:S(2)}, u32[]{:S(2)}) collective-permute-start(f32[80,128]{1,0:T(8,128)} %get-tuple-element.27), channel_id=1, source_target_pairs={{0,5},{1,6},{2,7},{3,0},{4,1},{5,2},{6,3},{7,4},{8,13},{9,14},{10,... | collective-permute-start | bytes 122888 | tf_op jit(solution)/shard_map/ppermute | solution.py:15
  21.2 5.6 %collective-permute-start.2 = (f32[80,128]{1,0:T(8,128)}, f32[80,128]{1,0:T(8,128)S(1)}, u32[]{:S(2)}, u32[]{:S(2)}) collective-permute-start(f32[80,128]{1,0:T(8,128)} %get-tuple-element.26), channel_id=1, source_target_pairs={{0,4},{1,5},{2,6},{3,7},{4,0},{5,1},{6,2},{7,3},{8,12},{9,13},{10,... | collective-permute-start | bytes 122888 | tf_op jit(solution)/shard_map/ppermute | solution.py:15
  26.9 4.5 %collective-permute-start.3 = (f32[80,128]{1,0:T(8,128)}, f32[80,128]{1,0:T(8,128)S(1)}, u32[]{:S(2)}, u32[]{:S(2)}) collective-permute-start(f32[80,128]{1,0:T(8,128)} %get-tuple-element.25), channel_id=1, source_target_pairs={{0,3},{1,4},{2,5},{3,6},{4,7},{5,0},{6,1},{7,2},{8,11},{9,12},{10,... | collective-permute-start | bytes 122888 | tf_op jit(solution)/shard_map/ppermute | solution.py:15
  31.4 6.3 %collective-permute-start.4 = (f32[80,128]{1,0:T(8,128)}, f32[80,128]{1,0:T(8,128)S(1)}, u32[]{:S(2)}, u32[]{:S(2)}) collective-permute-start(f32[80,128]{1,0:T(8,128)} %get-tuple-element.24), channel_id=1, source_target_pairs={{0,2},{1,3},{2,4},{3,5},{4,6},{5,7},{6,0},{7,1},{8,10},{9,11},{10,... | collective-permute-start | bytes 122888 | tf_op jit(solution)/shard_map/ppermute | solution.py:15
  37.7 5.4 %collective-permute-start.5 = (f32[80,128]{1,0:T(8,128)}, f32[80,128]{1,0:T(8,128)S(1)}, u32[]{:S(2)}, u32[]{:S(2)}) collective-permute-start(f32[80,128]{1,0:T(8,128)} %get-tuple-element.23), channel_id=1, source_target_pairs={{0,1},{1,2},{2,3},{3,4},{4,5},{5,6},{6,7},{7,0},{8,9},{9,10},{10,1... | collective-permute-start | bytes 122888 | tf_op jit(solution)/shard_map/ppermute | solution.py:15
  43.2 2.0 %collective-permute-start.6 = (f32[80,128]{1,0:T(8,128)}, f32[80,128]{1,0:T(8,128)S(1)}, u32[]{:S(2)}, u32[]{:S(2)}) collective-permute-start(f32[80,128]{1,0:T(8,128)} %get-tuple-element.22), channel_id=1, source_target_pairs={{0,7},{1,0},{2,1},{3,2},{4,3},{5,4},{6,5},{7,6},{8,15},{9,8},{10,9... | collective-permute-start | bytes 122888 | tf_op jit(solution)/shard_map/ppermute | solution.py:15
  45.2 4.2 %collective-permute-start.7 = (f32[80,128]{1,0:T(8,128)}, f32[80,128]{1,0:T(8,128)S(1)}, u32[]{:S(2)}, u32[]{:S(2)}) collective-permute-start(f32[80,128]{1,0:T(8,128)} %get-tuple-element.21), channel_id=1, source_target_pairs={{0,6},{1,7},{2,0},{3,1},{4,2},{5,3},{6,4},{7,5},{8,14},{9,15},{10,... | collective-permute-start | bytes 122888 | tf_op jit(solution)/shard_map/ppermute | solution.py:15
  54.5 9.8 %all-to-all-start = ((f32[1,512,128]{2,0,1:T(1,128)}), f32[1,512,128]{2,0,1:T(1,128)S(1)}, u32[]{:S(2)}, u32[]{:S(2)}) async-start(f32[1,512,128]{2,0,1:T(1,128)} %bitcast.158), calls=%async_computation | async-start | bytes 524288 | tf_op jit(solution)/shard_map/all_to_all | solution.py:56
  76.4 5.6 %collective-permute-start.12 = (f32[80,128]{1,0:T(8,128)S(1)}, f32[80,128]{1,0:T(8,128)S(1)}, u32[]{:S(2)}, u32[]{:S(2)}) collective-permute-start(f32[80,128]{1,0:T(8,128)S(1)} %get-tuple-element.16), channel_id=1, source_target_pairs={{0,6},{1,7},{2,0},{3,1},{4,2},{5,3},{6,4},{7,5},{8,14},{9,15},{10,... | collective-permute-start | bytes 122888 | tf_op jit(solution)/shard_map/ppermute | solution.py:15
  78.3 35.2 %collective-permute-start.23 = (f32[80,128]{1,0:T(8,128)S(1)}, f32[80,128]{1,0:T(8,128)S(1)}, u32[]{:S(2)}, u32[]{:S(2)}) collective-permute-start(f32[80,128]{1,0:T(8,128)S(1)} %get-tuple-element.5), channel_id=1, source_target_pairs={{0,2},{1,3},{2,4},{3,5},{4,6},{5,7},{6,0},{7,1},{8,10},{9,11},{10,... | collective-permute-start | bytes 122888 | tf_op jit(solution)/shard_map/ppermute | solution.py:15
  78.5 35.0 %collective-permute-start.22 = (f32[80,128]{1,0:T(8,128)S(1)}, f32[80,128]{1,0:T(8,128)S(1)}, u32[]{:S(2)}, u32[]{:S(2)}) collective-permute-start(f32[80,128]{1,0:T(8,128)S(1)} %get-tuple-element.6), channel_id=1, source_target_pairs={{0,3},{1,4},{2,5},{3,6},{4,7},{5,0},{6,1},{7,2},{8,11},{9,12},{10,... | collective-permute-start | bytes 122888 | tf_op jit(solution)/shard_map/ppermute | solution.py:15
  78.5 35.0 %collective-permute-start.21 = (f32[80,128]{1,0:T(8,128)S(1)}, f32[80,128]{1,0:T(8,128)S(1)}, u32[]{:S(2)}, u32[]{:S(2)}) collective-permute-start(f32[80,128]{1,0:T(8,128)S(1)} %get-tuple-element.7), channel_id=1, source_target_pairs={{0,4},{1,5},{2,6},{3,7},{4,0},{5,1},{6,2},{7,3},{8,12},{9,13},{10,... | collective-permute-start | bytes 122888 | tf_op jit(solution)/shard_map/ppermute | solution.py:15
  82.0 31.4 %collective-permute-start.20 = (f32[80,128]{1,0:T(8,128)S(1)}, f32[80,128]{1,0:T(8,128)S(1)}, u32[]{:S(2)}, u32[]{:S(2)}) collective-permute-start(f32[80,128]{1,0:T(8,128)S(1)} %get-tuple-element.8), channel_id=1, source_target_pairs={{0,5},{1,6},{2,7},{3,0},{4,1},{5,2},{6,3},{7,4},{8,13},{9,14},{10,... | collective-permute-start | bytes 122888 | tf_op jit(solution)/shard_map/ppermute | solution.py:15
  82.0 4.9 %collective-permute-start.13 = (f32[80,128]{1,0:T(8,128)S(1)}, f32[80,128]{1,0:T(8,128)S(1)}, u32[]{:S(2)}, u32[]{:S(2)}) collective-permute-start(f32[80,128]{1,0:T(8,128)S(1)} %get-tuple-element.15), channel_id=1, source_target_pairs={{0,5},{1,6},{2,7},{3,0},{4,1},{5,2},{6,3},{7,4},{8,13},{9,14},{10,... | collective-permute-start | bytes 122888 | tf_op jit(solution)/shard_map/ppermute | solution.py:15
  86.9 5.3 %collective-permute-start.14 = (f32[80,128]{1,0:T(8,128)S(1)}, f32[80,128]{1,0:T(8,128)S(1)}, u32[]{:S(2)}, u32[]{:S(2)}) collective-permute-start(f32[80,128]{1,0:T(8,128)S(1)} %get-tuple-element.14), channel_id=1, source_target_pairs={{0,4},{1,5},{2,6},{3,7},{4,0},{5,1},{6,2},{7,3},{8,12},{9,13},{10,... | collective-permute-start | bytes 122888 | tf_op jit(solution)/shard_map/ppermute | solution.py:15
  92.3 4.3 %collective-permute-start.15 = (f32[80,128]{1,0:T(8,128)S(1)}, f32[80,128]{1,0:T(8,128)S(1)}, u32[]{:S(2)}, u32[]{:S(2)}) collective-permute-start(f32[80,128]{1,0:T(8,128)S(1)} %get-tuple-element.13), channel_id=1, source_target_pairs={{0,3},{1,4},{2,5},{3,6},{4,7},{5,0},{6,1},{7,2},{8,11},{9,12},{10,... | collective-permute-start | bytes 122888 | tf_op jit(solution)/shard_map/ppermute | solution.py:15
  96.6 5.9 %collective-permute-start.16 = (f32[80,128]{1,0:T(8,128)S(1)}, f32[80,128]{1,0:T(8,128)S(1)}, u32[]{:S(2)}, u32[]{:S(2)}) collective-permute-start(f32[80,128]{1,0:T(8,128)S(1)} %get-tuple-element.12), channel_id=1, source_target_pairs={{0,2},{1,3},{2,4},{3,5},{4,6},{5,7},{6,0},{7,1},{8,10},{9,11},{10,... | collective-permute-start | bytes 122888 | tf_op jit(solution)/shard_map/ppermute | solution.py:15
  102.5 5.3 %collective-permute-start.17 = (f32[80,128]{1,0:T(8,128)S(1)}, f32[80,128]{1,0:T(8,128)S(1)}, u32[]{:S(2)}, u32[]{:S(2)}) collective-permute-start(f32[80,128]{1,0:T(8,128)S(1)} %get-tuple-element.11), channel_id=1, source_target_pairs={{0,1},{1,2},{2,3},{3,4},{4,5},{5,6},{6,7},{7,0},{8,9},{9,10},{10,1... | collective-permute-start | bytes 122888 | tf_op jit(solution)/shard_map/ppermute | solution.py:15
  109.5 4.0 %collective-permute-start.19 = (f32[80,128]{1,0:T(8,128)S(1)}, f32[80,128]{1,0:T(8,128)S(1)}, u32[]{:S(2)}, u32[]{:S(2)}) collective-permute-start(f32[80,128]{1,0:T(8,128)S(1)} %get-tuple-element.9), channel_id=1, source_target_pairs={{0,6},{1,7},{2,0},{3,1},{4,2},{5,3},{6,4},{7,5},{8,14},{9,15},{10,... | collective-permute-start | bytes 122888 | tf_op jit(solution)/shard_map/ppermute | solution.py:15
  (13 other events, 243.0 us)
where the time goes:
time: 118 us
  waiting for transfers between devices  61.8 us (52%)
  starting transfers between devices  26.4 us (22%)
  matrix products  15.4 us (13%)
  blocking collectives  8.26 us (7%)
  local copies, waits for them, and re-layouts  5.6 us (5%)
    ppermute x24, waiting for transfers between devices, shifted(): return lax.ppermute(value, axis, pairs)  57.3 us
    ppermute x24, starting transfers between devices, shifted(): return lax.ppermute(value, axis, pairs)  22.7 us
    all_to_all x1, blocking collectives, local(): lax.all_to_all(blended, 'kern', split_axis=0, concat_axis=1, tiled=True)[0]  8.26 us
    all_to_all x1, waiting for transfers between devices, local(): lax.all_to_all(first[None], 'kern', split_axis=1, concat_axis=0, tiled=True)  4.45 us
    dot_general x2, matrix products, apply_kernel(): jnp.einsum('kqp,kqc->pc', left_tile, chosen, precision=highest)  4.37 us
    dot_general x2, matrix products, apply_kernel(): jnp.einsum('sqp,pc->sqc', right_tile, column_vals, precision=highest)  4.34 us
    all_to_all x1, starting transfers between devices, local(): lax.all_to_all(first[None], 'kern', split_axis=1, concat_axis=0, tiled=True)  3.72 us
    dot_general x2, matrix products, apply_kernel(): jnp.dot(diag_tile, column_vals, precision=highest, preferred_element_type...  2.94 us
  transfers between devices with their start and end apart: 25, of which 16 were waited for; matrix products, arithmetic and copies ran while one was open for 3% of the time, Pallas kernels for 0%

commit v1 on v0

v1 whole, which is shorter than its diff:
```python
import jax
import jax.numpy as jnp
from jax import lax
from jax.sharding import PartitionSpec as P

high = lax.Precision.HIGH


def offset_of(slot, reach):
    return slot - reach if slot < reach else slot - reach + 1


def deliver_all(coeffs, reach, count):
    groups = [[] for _ in range(count)]
    for slot in range(2 * reach):
        groups[offset_of(slot, reach) % count].append(slot)
    width = max(len(group) for group in groups)
    order = [(group + [0] * width)[:width] for group in groups]
    me = lax.axis_index("tile")
    dests = jnp.arange(count, dtype=jnp.int32)
    table = jnp.asarray(order, dtype=jnp.int32)[(me - dests) % count]
    packed = coeffs[table.reshape(-1)]
    packed = packed.reshape((count, width) + coeffs.shape[1:])
    received = lax.all_to_all(packed, "tile", split_axis=0, concat_axis=0, tiled=True)
    place = [0] * (2 * reach)
    for group in groups:
        for at, slot in enumerate(group):
            place[slot] = at
    return received, jnp.asarray(place, dtype=jnp.int32)


def apply_kernel(diag_tile, left_tile, right_tile, offsets_row, ranks_row, column_vals):
    reach = right_tile.shape[0] // 2
    count = lax.axis_size("tile")
    coeffs = jnp.einsum("sqp,pc->sqc", right_tile, column_vals, precision=high)
    slot_pick = jnp.where(offsets_row < 0, offsets_row + reach, offsets_row + reach - 1)
    keeper = jnp.arange(left_tile.shape[1])[None, :] < ranks_row[:, None]
    if count <= 2 * reach:
        received, place = deliver_all(coeffs, reach, count)
        me = lax.axis_index("tile")
        chosen = received[(me + offsets_row) % count, place[slot_pick]]
    else:
        arrived = []
        for slot in range(2 * reach):
            steps = -offset_of(slot, reach)
            pairs = [(source, (source + steps) % count) for source in range(count)]
            arrived.append(lax.ppermute(coeffs[slot], "tile", pairs))
        chosen = jnp.stack(arrived)[slot_pick]
    chosen = jnp.where(keeper[:, :, None], chosen, 0.0)
    result = jnp.dot(diag_tile, column_vals, precision=high, preferred_element_type=jnp.float32)
    return result + jnp.einsum("kqp,kqc->pc", left_tile, chosen, precision=high)


def local(
    diag_tiles,
    left_factors,
    right_factors,
    tile_offsets,
    tile_ranks,
    mixing,
    block_index,
    rhs_field,
):
    diag_tile = diag_tiles[0, 0]
    left_tile = left_factors[0, 0]
    right_tile = right_factors[0, 0]
    offsets_row = tile_offsets[0, 0]
    ranks_row = tile_ranks[0, 0]
    first = apply_kernel(diag_tile, left_tile, right_tile, offsets_row, ranks_row, rhs_field[0])
    own_group = lax.axis_index("kern")
    grouped = lax.all_to_all(first[None], "kern", split_axis=1, concat_axis=0, tiled=True)
    part_len = grouped.shape[1]
    local_index = lax.dynamic_slice_in_dim(block_index, own_group * part_len, part_len)
    per_location = mixing[local_index]
    blended = jnp.sum(per_location.transpose(1, 2, 0)[..., None] * grouped[None], axis=1)
    mixed = lax.all_to_all(blended, "kern", split_axis=0, concat_axis=1, tiled=True)[0]
    second = apply_kernel(diag_tile, left_tile, right_tile, offsets_row, ranks_row, mixed)
    return second[None]


def solution(mesh):
    in_specs = (
        P("kern", "tile", None, None),
        P("kern", "tile", None, None, None),
        P("kern", "tile", None, None, None),
        P("kern", "tile", None),
        P("kern", "tile", None),
        P(),
        P("tile"),
        P("kern", "tile", None),
    )
    out_specs = P("kern", "tile", None)
    return jax.shard_map(local, mesh=mesh, in_specs=in_specs, out_specs=out_specs, check_vma=False)
```

time: 118 us -> 89.5 us (0.76)
  waiting for transfers between devices: 61.8 us -> 19.6 us
  blocking collectives: 8.26 us -> 30.5 us
  starting transfers between devices: 26.4 us -> 10.4 us
  local copies, waits for them, and re-layouts: 5.6 us -> 15.5 us
  matrix products: 15.4 us -> 10.5 us
  other arithmetic: 0.01 us -> 2.21 us
    ppermute x24 -> x0, waiting for transfers between devices: 57.3 us -> none  [shifted(): return lax.ppermute(value, axis, pairs)]
    ppermute x24 -> x0, starting transfers between devices: 22.7 us -> none  [shifted(): return lax.ppermute(value, axis, pairs)]
    all_to_all x0 -> x1, blocking collectives: none -> 22.4 us  [deliver_all(): lax.all_to_all(packed, 'tile', split_axis=0, concat_axis=0, tiled=True)]
    all_to_all x0 -> x1, waiting for transfers between devices: none -> 17.3 us  [deliver_all(): lax.all_to_all(packed, 'tile', split_axis=0, concat_axis=0, tiled=True)]
    gather x0 -> x7, local copies, waits for them, and re-layouts: none -> 13.3 us  [the longest x3 5.41 us: apply_kernel(): chosen = received[(me + offsets_row) % count, place[slot_pick]]]
    all_to_all x0 -> x1, starting transfers between devices: none -> 6.32 us  [deliver_all(): lax.all_to_all(packed, 'tile', split_axis=0, concat_axis=0, tiled=True)]
    dot_general x9 -> x6, matrix products: 14.6 us -> 10.5 us  [the longest x2 4.42 us: apply_kernel(): coeffs = jnp.einsum('sqp,pc->sqc', right_tile, column_vals, precision=high)]
    all_to_all x1, waiting for transfers between devices: 4.45 us -> 2.25 us  [local(): lax.all_to_all(first[None], 'kern', split_axis=1, concat_axis=0, tiled=True)]
  transfers between devices with their start and end apart: 25 -> 2, of which waited for: 16 -> 2; matrix products, arithmetic and copies ran while one was open for 3% -> 5% of each run, Pallas kernels for 0% -> 0%
where the time goes in v1:
time: 89.5 us; the launch traced here: 88.8 us
  blocking collectives  30.5 us (34%)
  waiting for transfers between devices  19.6 us (22%)
  local copies, waits for them, and re-layouts  15.5 us (17%)
  matrix products  10.5 us (12%)
  starting transfers between devices  10.4 us (12%)
  other arithmetic  2.21 us (2%)
    all_to_all x1, blocking collectives, deliver_all(): lax.all_to_all(packed, 'tile', split_axis=0, concat_axis=0, tiled=True)  22.4 us
    all_to_all x1, waiting for transfers between devices, deliver_all(): lax.all_to_all(packed, 'tile', split_axis=0, concat_axis=0, tiled=True)  17.3 us
    all_to_all x1, blocking collectives, local(): lax.all_to_all(blended, 'kern', split_axis=0, concat_axis=1, tiled=True)[0]  8.11 us
    all_to_all x1, starting transfers between devices, deliver_all(): lax.all_to_all(packed, 'tile', split_axis=0, concat_axis=0, tiled=True)  6.32 us
    gather x3, local copies, waits for them, and re-layouts, apply_kernel(): chosen = received[(me + offsets_row) % count, place[slot_pick]]  5.41 us
    gather x2, local copies, waits for them, and re-layouts, deliver_all(): packed = coeffs[table.reshape(-1)]  5.05 us
    dot_general x2, matrix products, apply_kernel(): coeffs = jnp.einsum('sqp,pc->sqc', right_tile, column_vals, precision=high)  4.42 us
    dot_general x2, matrix products, apply_kernel(): return result + jnp.einsum('kqp,kqc->pc', left_tile, chosen, precision=high)  4.11 us
  transfers between devices with their start and end apart: 2, of which 2 were waited for; matrix products, arithmetic and copies ran while one was open for 5% of the time, Pallas kernels for 0%

profile of v1, /device:TPU:0, one launch (start us, length us, event | category | flops | bytes accessed | tf_op | source)
XLA Modules:
  0.0 88.8 jit_solution(3827923384126577991)
XLA Ops:
  0.0 1.4 %gather_fusion.1 = s32[8,2]{1,0:T(8,128)S(1)} fusion(s32[8,2]{1,0:T(8,128)} %constant.62.clone, s32[1024]{0:T(1024)S(1)} %pad_clamp_fusion.2), kind=kCustom, calls=%fused_computation.1 | custom fusion | bytes 160 | tf_op jit(solution)/shard_map/gather | solution.py:21
  1.6 2.7 %fusion.2 = f32[12,80,128]{2,1,0:T(8,128)} fusion(f32[1,1,12,80,512]{4,3,2,1,0:T(8,128)S(1)} %copy-done, f32[1,512,128]{2,1,0:T(8,128)} %param.19), kind=kOutput, calls=%fused_computation.9 | convolution fusion | flops 377487360 | bytes 2719744 | tf_op jit(solution)/shard_map/sqp,pc->sqc/dot_general | solution.py:35
  4.3 2.6 %gather_fusion.2 = f32[16,80,128]{2,1,0:T(8,128)} fusion(f32[12,80,128]{2,1,0:T(8,128)} %fusion.2, s32[1024]{0:T(1024)S(1)} %pad_clamp_fusion.1), kind=kCustom, calls=%fused_computation.2 | custom fusion | bytes 1310784 | tf_op jit(solution)/shard_map/gather | solution.py:22
  6.9 6.3 %all-to-all-start = ((f32[8,2,80,128]{3,2,1,0:T(8,128)}), f32[8,2,80,128]{3,2,1,0:T(8,128)}, u32[]{:S(2)}, u32[]{:S(2)}) async-start(f32[8,2,80,128]{3,2,1,0:T(8,128)} %bitcast.74), calls=%async_computation | async-start | bytes 1310720 | tf_op jit(solution)/shard_map/all_to_all | solution.py:24
  13.2 0.1 copy.24
  13.4 0.6 gather_fusion.3
  14.1 17.3 %all-to-all-done = f32[8,2,80,128]{3,2,1,0:T(8,128)} async-done(((f32[8,2,80,128]{3,2,1,0:T(8,128)}), f32[8,2,80,128]{3,2,1,0:T(8,128)}, u32[]{:S(2)}, u32[]{:S(2)}) %all-to-all-start) | async-done | bytes 655392 | tf_op jit(solution)/shard_map/all_to_all | solution.py:24
  31.5 2.4 %gather_fusion.4 = f32[8,80,128]{2,1,0:T(8,128)} fusion(f32[8,2,80,128]{3,2,1,0:T(8,128)} %all-to-all-done, s32[8]{0:T(128)S(1)} %fusion.39), kind=kCustom, calls=%fused_computation.4 | custom fusion | bytes 655424 | tf_op jit(solution)/shard_map/gather | solution.py:41
  33.9 2.4 %fusion.11 = f32[512,128]{1,0:T(8,128)S(1)} fusion(f32[1,1,8,80,512]{4,3,2,1,0:T(8,128)S(1)} %copy-done.2, f32[8,80,128]{2,1,0:T(8,128)} %gather_fusion.4, pred[8,80]{1,0:T(8,128)(4,1)S(1)} %iota_compare_fusion), kind=kOutput, calls=%fused_computation.16 | convolution fusion | flops 251740160 | bytes 1901184 | tf_op jit(solution)/shard_map/kqp,kqc->pc/dot_general | solution.py:51
  36.3 1.3 %convolution_add_fusion.1 = f32[512,128]{1,0:T(8,128)} fusion(f32[512,128]{1,0:T(8,128)S(1)} %fusion.11, f32[1,1,512,512]{3,2,1,0:T(8,128)S(1)} %copy-done.3, f32[1,512,128]{2,1,0:T(8,128)S(1)} %copy-done.5), kind=kOutput, calls=%fused_computation.20 | convolution fusion | flops 201392128 | bytes 1835008 | tf_op jit(solution)/shard_map/dot_general | solution.py:50
  37.6 4.0 %all-to-all-start.1 = ((f32[1,512,128]{2,0,1:T(1,128)}), f32[1,512,128]{2,0,1:T(1,128)}, u32[]{:S(2)}, u32[]{:S(2)}) async-start(f32[1,512,128]{2,0,1:T(1,128)} %bitcast.78), calls=%async_computation.1 | async-start | bytes 524288 | tf_op jit(solution)/shard_map/all_to_all | solution.py:71
  41.6 0.8 compare_select_fusion.5
  42.4 1.4 %gather_fusion = f32[128,4,4]{2,1,0:T(4,128)} fusion(f32[64,4,4]{2,1,0:T(4,128)S(1)} %copy.24, s32[1024]{0:T(1024)S(1)} %pad_clamp_fusion.3), kind=kCustom, calls=%fused_computation | custom fusion | bytes 16896 | tf_op jit(solution)/shard_map/gather | solution.py:74
  43.8 1.0 %copy.25 = f32[4,4,128]{2,1,0:T(4,128)S(1)} copy(f32[4,4,128]{1,0,2:T(4,128)} %bitcast.79) | data formatting | bytes 16384 | tf_op jit(solution)/shard_map/transpose | solution.py:75
  44.9 2.3 %all-to-all-done.1 = f32[1,512,128]{2,0,1:T(1,128)} async-done(((f32[1,512,128]{2,0,1:T(1,128)}), f32[1,512,128]{2,0,1:T(1,128)}, u32[]{:S(2)}, u32[]{:S(2)}) %all-to-all-start.1) | async-done | bytes 262176 | tf_op jit(solution)/shard_map/all_to_all | solution.py:71
  47.1 1.3 %multiply_reduce_fusion = f32[4,128,128]{2,1,0:T(8,128)S(1)} fusion(f32[4,128,128]{2,1,0:T(8,128)} %bitcast.19, f32[4,4,128]{2,1,0:T(4,128)S(1)} %copy.25), kind=kLoop, calls=%fused_computation.23 | loop fusion | flops 458752 | bytes 532480 | tf_op jit(solution)/shard_map/reduce_sum | solution.py:75
  48.4 8.1 %all_to_all.28 = f32[4,128,128]{2,1,0:T(8,128)S(1)} all-to-all(f32[4,128,128]{2,1,0:T(8,128)S(1)} %multiply_reduce_fusion), channel_id=1, replica_groups=mesh['kern'=4,'tile'=8] {'kern'}, dimensions={0} | all-to-all | bytes 524288 | tf_op jit(solution)/shard_map/all_to_all | solution.py:76
  56.5 1.7 %fusion.8 = f32[12,80,128]{2,1,0:T(8,128)} fusion(f32[512,128,1]{1,0,2:T(8,128)S(1)} %bitcast.76, f32[1,1,12,80,512]{4,3,2,1,0:T(8,128)S(1)} %copy-done), kind=kOutput, calls=%fused_computation.15 | convolution fusion | flops 377487360 | bytes 2719744 | tf_op jit(solution)/shard_map/sqp,pc->sqc/dot_general | solution.py:35
  58.3 2.5 %gather_fusion.5 = f32[16,80,128]{2,1,0:T(8,128)} fusion(f32[12,80,128]{2,1,0:T(8,128)} %fusion.8, s32[1024]{0:T(1024)S(1)} %pad_clamp_fusion.1), kind=kCustom, calls=%fused_computation.5 | custom fusion | bytes 1310784 | tf_op jit(solution)/shard_map/gather | solution.py:22
  60.7 22.4 %all_to_all.29 = f32[8,2,80,128]{3,2,1,0:T(8,128)} all-to-all(f32[8,2,80,128]{3,2,1,0:T(8,128)} %bitcast.75), channel_id=1, replica_groups=mesh['kern'=4,'tile'=8] {'tile'}, dimensions={0} | all-to-all | bytes 1310720 | tf_op jit(solution)/shard_map/all_to_all | solution.py:24
  83.1 2.4 %gather_fusion.6 = f32[8,80,128]{2,1,0:T(8,128)} fusion(f32[8,2,80,128]{3,2,1,0:T(8,128)} %all_to_all.29, s32[8]{0:T(128)S(1)} %fusion.39), kind=kCustom, calls=%fused_computation.6 | custom fusion | bytes 655424 | tf_op jit(solution)/shard_map/gather | solution.py:41
  85.5 1.7 %fusion.14 = f32[128,512]{1,0:T(8,128)S(1)} fusion(f32[1,1,8,80,512]{4,3,2,1,0:T(8,128)S(1)} %copy-done.2, f32[8,80,128]{2,1,0:T(8,128)} %gather_fusion.6, pred[8,80]{1,0:T(8,128)(4,1)S(1)} %iota_compare_fusion), kind=kOutput, calls=%fused_computation.17 | convolution fusion | flops 251740160 | bytes 1901184 | tf_op jit(solution)/shard_map/kqp,kqc->pc/dot_general | solution.py:51
  87.2 0.7 fusion.17
  87.9 0.8 copy.28
  (28 shorter events, 0.3 us)
Async XLA Ops:
  0.0 1.6 %copy-start = (f32[1,1,12,80,512]{4,3,2,1,0:T(8,128)S(1)}, f32[1,1,12,80,512]{4,3,2,1,0:T(8,128)}, u32[]{:S(2)}) copy-start(f32[1,1,12,80,512]{4,3,2,1,0:T(8,128)} %param.14) | copy-start | bytes 5898244
  4.3 8.9 %copy-start.6 = (f32[64,4,4]{0,2,1:T(4,128)S(1)}, f32[64,4,4]{0,2,1:T(4,128)}, u32[]{:S(2)}) copy-start(f32[64,4,4]{0,2,1:T(4,128)} %param.17) | copy-start | bytes 12292
  4.3 9.1 %copy-start.7 = (s32[1,1,8]{2,1,0:T(1,128)S(1)}, s32[1,1,8]{2,1,0:T(1,128)}, u32[]{:S(2)}) copy-start(s32[1,1,8]{2,1,0:T(1,128)} %param.15) | copy-start | bytes 100
  4.3 9.1 %copy-start.1 = (s32[12]{0:T(128)S(1)}, s32[12]{0:T(128)}, u32[]{:S(2)}) copy-start(s32[12]{0:T(128)} %constant.63.clone) | copy-start | bytes 148
  4.3 9.8 %copy-start.8 = (s32[1,1,8]{2,1,0:T(1,128)S(1)}, s32[1,1,8]{2,1,0:T(1,128)}, u32[]{:S(2)}) copy-start(s32[1,1,8]{2,1,0:T(1,128)} %param.16) | copy-start | bytes 100
  4.3 29.6 %copy-start.2 = (f32[1,1,8,80,512]{4,3,2,1,0:T(8,128)S(1)}, f32[1,1,8,80,512]{4,3,2,1,0:T(8,128)}, u32[]{:S(2)}) copy-start(f32[1,1,8,80,512]{4,3,2,1,0:T(8,128)} %param.13) | copy-start | bytes 3932164
  6.9 24.6 %all-to-all-start = ((f32[8,2,80,128]{3,2,1,0:T(8,128)}), f32[8,2,80,128]{3,2,1,0:T(8,128)}, u32[]{:S(2)}, u32[]{:S(2)}) async-start(f32[8,2,80,128]{3,2,1,0:T(8,128)} %bitcast.74), calls=%async_computation | async-start | bytes 1310720 | tf_op jit(solution)/shard_map/all_to_all | solution.py:24
  33.8 2.4 %copy-start.3 = (f32[1,1,512,512]{3,2,1,0:T(8,128)S(1)}, f32[1,1,512,512]{3,2,1,0:T(8,128)}, u32[]{:S(2)}) copy-start(f32[1,1,512,512]{3,2,1,0:T(8,128)} %param.12) | copy-start | bytes 3145732
  33.9 2.4 %copy-start.5 = (f32[1,512,128]{2,1,0:T(8,128)S(1)}, f32[1,512,128]{2,1,0:T(8,128)}, u32[]{:S(2)}) copy-start(f32[1,512,128]{2,1,0:T(8,128)} %param.19) | copy-start | bytes 786436
  37.6 9.6 %all-to-all-start.1 = ((f32[1,512,128]{2,0,1:T(1,128)}), f32[1,512,128]{2,0,1:T(1,128)}, u32[]{:S(2)}, u32[]{:S(2)}) async-start(f32[1,512,128]{2,0,1:T(1,128)} %bitcast.78), calls=%async_computation.1 | async-start | bytes 524288 | tf_op jit(solution)/shard_map/all_to_all | solution.py:71
  85.5 1.7 %copy-start.4 = (f32[1,1,512,512]{3,2,1,0:T(8,128)S(1)}, f32[1,1,512,512]{3,2,1,0:T(8,128)}, u32[]{:S(2)}) copy-start(f32[1,1,512,512]{3,2,1,0:T(8,128)} %param.12) | copy-start | bytes 3145732

commit v2 on v0

v2 whole, which is shorter than its diff:
```python
import functools

import jax
import jax.numpy as jnp
from jax import lax
from jax.experimental import pallas as pl
from jax.experimental.pallas import tpu as pltpu
from jax.sharding import PartitionSpec as P

f32 = jnp.float32
bf16 = jnp.bfloat16
VMEM_BYTES = 24 * 1024 * 1024
in_vmem = pl.BlockSpec(memory_space=pltpu.VMEM)
in_smem = pl.BlockSpec(memory_space=pltpu.SMEM)
in_any = pl.BlockSpec(memory_space=pl.ANY)


def split(value):
    hi = value.astype(bf16)
    return hi, (value - hi.astype(f32)).astype(bf16)


def dot(left, right):
    return jnp.dot(left, right, preferred_element_type=f32)


def call(kernel, out_shape, in_specs, scratch=(), flops=0, moved=0):
    many = isinstance(out_shape, (list, tuple))
    return pl.pallas_call(
        kernel,
        out_shape=out_shape,
        in_specs=in_specs,
        out_specs=[in_vmem] * len(out_shape) if many else in_vmem,
        scratch_shapes=list(scratch),
        compiler_params=pltpu.CompilerParams(vmem_limit_bytes=VMEM_BYTES),
        cost_estimate=pl.CostEstimate(flops=flops, bytes_accessed=moved, transcendentals=0),
    )


def offset_of(slot, reach):
    return slot - reach if slot < reach else slot - reach + 1


def paired(count, reach):
    return reach < count <= 2 * reach


def coeff_kernel(count, chunks, cols_ref, right_ref, out_ref, held, sems):
    slots, rank, size = right_ref.shape
    reach = slots // 2
    step = slots // chunks
    copies = []
    for at in range(chunks):
        part = pl.ds(at * step, step)
        copies.append(pltpu.make_async_copy(right_ref.at[part], held.at[part], sems.at[at]))
        copies[-1].start()
    width = cols_ref.shape[1]
    both = jnp.concatenate(split(cols_ref[...]), axis=1)
    me = lax.axis_index("tile")
    for at in range(chunks):
        copies[at].wait()
        rows = held[pl.ds(at * step, step)].reshape(step * rank, size)
        hi, lo = split(rows)
        got = dot(hi, both) + dot(lo, both)
        got = got[:, :width] + got[:, width:]
        for s in range(step):
            slot = at * step + s
            piece = got[s * rank : (s + 1) * rank]
            if paired(count, reach):
                offset = offset_of(slot, reach)
                dest = lax.rem(me - offset + count, count)
                out_ref[dest, 0 if offset > 0 else 1] = piece
            else:
                out_ref[slot, 0] = piece


def coefficients(cols, right_tile):
    count = lax.axis_size("tile")
    slots, rank, size = right_tile.shape
    width = cols.shape[1]
    lead = (count, 2) if paired(count, slots // 2) else (slots, 1)
    chunks = 3 if slots % 3 == 0 else 1
    return call(
        functools.partial(coeff_kernel, count, chunks),
        jax.ShapeDtypeStruct(lead + (rank, width), f32),
        [in_vmem, in_any],
        [pltpu.VMEM(right_tile.shape, f32), pltpu.SemaphoreType.DMA((chunks,))],
        flops=8 * slots * rank * size * width,
        moved=4 * slots * rank * (size + width),
    )(cols, right_tile)


def diag_kernel(turned, diag_ref, cols_ref, out_ref):
    width = cols_ref.shape[1]
    both = jnp.concatenate(split(cols_ref[...]), axis=1)
    hi, lo = split(diag_ref[...])
    got = dot(hi, both) + dot(lo, both)
    got = got[:, :width] + got[:, width:]
    out_ref[...] = got.T if turned else got


def diagonal(diag_tile, cols, turned):
    size, width = cols.shape
    return call(
        functools.partial(diag_kernel, turned),
        jax.ShapeDtypeStruct((width, size) if turned else (size, width), f32),
        [in_vmem, in_vmem],
        flops=8 * size * size * width,
        moved=4 * size * (size + 2 * width),
    )(diag_tile, cols)


def weights_kernel(table_ref, index_ref, out_ref):
    entries = table_ref.shape[1]
    part = index_ref.shape[1]
    hot = (lax.broadcasted_iota(jnp.int32, (entries, part), 0) == index_ref[...]).astype(f32)
    out_ref[...] = jnp.dot(
        table_ref[...], hot, precision=lax.Precision.HIGHEST, preferred_element_type=f32
    )


def row_kernel(count, turned, offs_ref, ranks_ref, got_ref, left_ref, diag_ref, out_ref, picked):
    terms, rank, size = left_ref.shape
    width = got_ref.shape[3]
    reach = got_ref.shape[0] // 2
    me = lax.axis_index("tile")
    line = lax.broadcasted_iota(jnp.int32, (rank, width), 0)
    for k in range(terms):
        offset = offs_ref[0, k]
        if got_ref.shape[1] == 2:
            piece = got_ref[lax.rem(me + offset + count, count), jnp.where(offset > 0, 0, 1)]
        else:
            piece = got_ref[jnp.where(offset < 0, offset + reach, offset + reach - 1), 0]
        picked[pl.ds(k * rank, rank)] = jnp.where(line < ranks_ref[0, k], piece, 0.0)
    both = jnp.concatenate(split(picked[...].T), axis=0)
    hi, lo = split(left_ref[...].reshape(terms * rank, size))
    total = dot(both, hi) + dot(both, lo)
    total = total[:width] + total[width:]
    if turned:
        total = total + diag_ref[...]
        part = out_ref.shape[2]
        for at in range(out_ref.shape[0]):
            out_ref[at] = total[:, at * part : (at + 1) * part]
    else:
        out_ref[...] = total.T + diag_ref[...]


def rows(offsets, ranks, got, left_tile, diag_part, groups, turned):
    terms, rank, size = left_tile.shape
    width = got.shape[3]
    shape = (groups, width, size // groups) if turned else (size, width)
    return call(
        functools.partial(row_kernel, lax.axis_size("tile"), turned),
        jax.ShapeDtypeStruct(shape, f32),
        [in_smem, in_smem, in_vmem, in_vmem, in_vmem],
        [pltpu.VMEM((terms * rank, width), f32)],
        flops=8 * terms * rank * size * width,
        moved=4 * terms * rank * (size + width),
    )(offsets, ranks, got, left_tile, diag_part)


def mix_kernel(fields_ref, weights_ref, out_ref):
    groups = fields_ref.shape[0]
    for a in range(groups):
        total = fields_ref[0] * weights_ref[pl.ds(a * groups, 1)]
        for b in range(1, groups):
            total = total + fields_ref[b] * weights_ref[pl.ds(a * groups + b, 1)]
        out_ref[a] = total.T


def deliver(coeffs, reach):
    count = lax.axis_size("tile")
    if paired(count, reach):
        return lax.all_to_all(coeffs, "tile", split_axis=0, concat_axis=0, tiled=True)
    arrived = []
    for slot in range(2 * reach):
        steps = -offset_of(slot, reach)
        pairs = [(source, (source + steps) % count) for source in range(count)]
        arrived.append(lax.ppermute(coeffs[slot], "tile", pairs))
    return jnp.stack(arrived)


def local(
    diag_tiles,
    left_factors,
    right_factors,
    tile_offsets,
    tile_ranks,
    mixing,
    block_index,
    rhs_field,
):
    diag_tile = diag_tiles[0, 0]
    left_tile = left_factors[0, 0]
    right_tile = right_factors[0, 0]
    offsets = tile_offsets[0]
    ranks = tile_ranks[0]
    reach = right_tile.shape[0] // 2
    groups = lax.axis_size("kern")
    own_group = lax.axis_index("kern")
    size, width = rhs_field.shape[1:]
    part = size // groups

    def apply_kernel(cols, turned):
        got = deliver(coefficients(cols, right_tile), reach)
        diag_part = diagonal(diag_tile, cols, turned)
        return rows(offsets, ranks, got, left_tile, diag_part, groups, turned)

    first = apply_kernel(rhs_field[0], True)
    fields = lax.all_to_all(first, "kern", split_axis=0, concat_axis=0, tiled=True)
    table = mixing.reshape(mixing.shape[0], groups * groups).T
    index = lax.dynamic_slice_in_dim(block_index, own_group * part, part)[None]
    weights = call(
        weights_kernel, jax.ShapeDtypeStruct((groups * groups, part), f32), [in_vmem, in_vmem]
    )(table, index)
    blended = call(
        mix_kernel,
        jax.ShapeDtypeStruct((groups, part, width), f32),
        [in_vmem, in_vmem],
        flops=2 * groups * groups * part * width,
        moved=8 * groups * part * width,
    )(fields, weights)
    mixed = lax.all_to_all(blended, "kern", split_axis=0, concat_axis=0, tiled=True)
    return apply_kernel(mixed.reshape(size, width), False)[None]


def solution(mesh):
    in_specs = (
        P("kern", "tile", None, None),
        P("kern", "tile", None, None, None),
        P("kern", "tile", None, None, None),
        P("kern", "tile", None),
        P("kern", "tile", None),
        P(),
        P("tile"),
        P("kern", "tile", None),
    )
    out_specs = P("kern", "tile", None)
    return jax.shard_map(local, mesh=mesh, in_specs=in_specs, out_specs=out_specs, check_vma=False)
```

time: 118 us -> 78.5 us (0.67)
  waiting for transfers between devices: 61.8 us -> 38.5 us
  matrix products: 15.4 us -> 0 us
  starting transfers between devices: 26.4 us -> 13.8 us
  Pallas kernels: 0 us -> 9.17 us
  local copies, waits for them, and re-layouts: 5.6 us -> 8.18 us
    ppermute x24 -> x0, waiting for transfers between devices: 57.3 us -> none  [shifted(): return lax.ppermute(value, axis, pairs)]
    all_to_all x1 -> x3, waiting for transfers between devices: 4.45 us -> 38.5 us  [the longest x2 34 us: deliver(): lax.all_to_all(coeffs, 'tile', split_axis=0, concat_axis=0, tiled=True)]
    ppermute x24 -> x0, starting transfers between devices: 22.7 us -> none  [shifted(): return lax.ppermute(value, axis, pairs)]
    dot_general x9 -> x0, matrix products: 14.6 us -> none  [the longest x2 4.37 us: apply_kernel(): jnp.einsum('kqp,kqc->pc', left_tile, chosen, precision=highest)]
    all_to_all x1 -> x3, starting transfers between devices: 3.72 us -> 13.8 us  [the longest x2 10.1 us: deliver(): lax.all_to_all(coeffs, 'tile', split_axis=0, concat_axis=0, tiled=True)]
    pallas_call x0 -> x8, Pallas kernels: none -> 9.17 us  [the longest x2 4.03 us: coefficients(): call(functools.partial(coeff_kernel, count, chunks), jax.ShapeDtypeStruct...]
    unnamed x46 -> x32, local copies, waits for them, and re-layouts: 1.7 us -> 8.1 us
    dynamic_slice x1 -> x0, local copies, waits for them, and re-layouts: 1.34 us -> none  [local(): lax.dynamic_slice_in_dim(block_index, own_group * part_len, part_len)]
  transfers between devices with their start and end apart: 25 -> 3, of which waited for: 16 -> 3; matrix products, arithmetic and copies ran while one was open for 3% -> 0% of each run, Pallas kernels for 0% -> 1%
where the time goes in v2:
time: 78.5 us; the launch traced here: 77.9 us
  waiting for transfers between devices  38.5 us (49%)
  starting transfers between devices  13.8 us (18%)
  Pallas kernels  9.17 us (12%)
  local copies, waits for them, and re-layouts  8.18 us (10%)
  blocking collectives  8.11 us (10%)
    all_to_all x2, waiting for transfers between devices, deliver(): lax.all_to_all(coeffs, 'tile', split_axis=0, concat_axis=0, tiled=True)  34 us
    all_to_all x2, starting transfers between devices, deliver(): lax.all_to_all(coeffs, 'tile', split_axis=0, concat_axis=0, tiled=True)  10.1 us
    all_to_all x1, blocking collectives, local(): lax.all_to_all(blended, 'kern', split_axis=0, concat_axis=0, tiled=True)  8.11 us
    unnamed x32, local copies, waits for them, and re-layouts  8.1 us
    all_to_all x1, waiting for transfers between devices, local(): lax.all_to_all(first, 'kern', split_axis=0, concat_axis=0, tiled=True)  4.46 us
    pallas_call x2, Pallas kernels, coefficients(): call(functools.partial(coeff_kernel, count, chunks), jax.ShapeDtypeStruct...  4.03 us
    pallas_call x2, Pallas kernels, rows(): call(functools.partial(row_kernel, lax.axis_size('tile'), turned), jax.Sh...  3.89 us
    all_to_all x1, starting transfers between devices, local(): lax.all_to_all(first, 'kern', split_axis=0, concat_axis=0, tiled=True)  3.72 us
  transfers between devices with their start and end apart: 3, of which 3 were waited for; matrix products, arithmetic and copies ran while one was open for 0% of the time, Pallas kernels for 1%

profile of v2, /device:TPU:0, one launch (start us, length us, event | category | flops | bytes accessed | tf_op | source)
XLA Modules:
  0.0 77.9 jit_solution(6606769609877688541)
XLA Ops:
  0.0 1.6 %copy-done.1 = f32[1,1,12,80,512]{4,3,2,1,0:T(8,128)S(1)} copy-done((f32[1,1,12,80,512]{4,3,2,1,0:T(8,128)S(1)}, f32[1,1,12,80,512]{4,3,2,1,0:T(8,128)}, u32[]{:S(2)}) %copy-start.1) | copy-done | bytes 1966104
  1.6 0.9 %copy-done.10 = f32[1,512,128]{2,1,0:T(8,128)S(1)} copy-done((f32[1,512,128]{2,1,0:T(8,128)S(1)}, f32[1,512,128]{2,1,0:T(8,128)}, u32[]{:S(2)}) %copy-start.10) | copy-done | bytes 262168
  2.5 2.0 %shard_map.82 = f32[8,2,80,128]{3,2,1,0:T(8,128)S(1)} custom-call(f32[512,128]{1,0:T(8,128)S(1)} %bitcast.21, f32[12,80,512]{2,1,0:T(8,128)S(1)} %bitcast.13), custom_call_target="tpu_custom_call" | custom-call | flops 503316480 | bytes 2457600 | tf_op jit(solution)/shard_map/pallas_call | solution.py:83
  4.6 0.8 %copy-done.9 = f32[8,2,80,128]{3,2,1,0:T(8,128)} copy-done((f32[8,2,80,128]{3,2,1,0:T(8,128)}, f32[8,2,80,128]{3,2,1,0:T(8,128)S(1)}, u32[]{:S(2)}) %copy-start.9) | copy-done | bytes 655384
  5.4 6.5 %all-to-all-start = ((f32[8,2,80,128]{3,2,1,0:T(8,128)}), f32[8,2,80,128]{3,2,1,0:T(8,128)S(1)}, u32[]{:S(2)}, u32[]{:S(2)}) async-start(f32[8,2,80,128]{3,2,1,0:T(8,128)} %copy-done.9), calls=%async_computation | async-start | bytes 1310720 | tf_op jit(solution)/shard_map/all_to_all | solution.py:174
  11.9 0.5 shard_map.83.diag_ref
  12.4 17.6 %all-to-all-done.got_ref = f32[8,2,80,128]{3,2,1,0:T(8,128)S(1)} async-done(((f32[8,2,80,128]{3,2,1,0:T(8,128)}), f32[8,2,80,128]{3,2,1,0:T(8,128)S(1)}, u32[]{:S(2)}, u32[]{:S(2)}) %all-to-all-start) | async-done | bytes 655392 | tf_op jit(solution)/shard_map/all_to_all | solution.py:174
  30.0 0.9 %copy-done.6 = f32[8,2,80,128]{3,2,1,0:T(8,128)} copy-done((f32[8,2,80,128]{3,2,1,0:T(8,128)}, f32[8,2,80,128]{3,2,1,0:T(8,128)S(1)}, u32[]{:S(2)}) %copy-start.6) | copy-done | bytes 655384
  30.9 1.1 %copy-done.7 = f32[8,2,80,128]{3,2,1,0:T(8,128)S(1)} copy-done((f32[8,2,80,128]{3,2,1,0:T(8,128)S(1)}, f32[8,2,80,128]{3,2,1,0:T(8,128)}, u32[]{:S(2)}) %copy-start.7) | copy-done | bytes 655384
  32.0 1.9 %shard_map.84 = f32[4,128,128]{2,1,0:T(8,128)} custom-call(s32[1,8]{1,0:T(1,128)S(1)} %bitcast.24, s32[1,8]{1,0:T(1,128)S(1)} %bitcast.26, f32[8,2,80,128]{3,2,1,0:T(8,128)S(1)} %copy-done.7, f32[8,80,512]{2,1,0:T(8,128)S(1)} %bitcast.15, f32[128,512]{1,0:T(8,128)S(1)} %shard_map.83.diag_ref), custom_call_target="tpu_custom_call" | custom-call | flops 335544320 | bytes 1638400 | tf_op jit(solution)/shard_map/pallas_call | solution.py:152
  33.9 3.7 %all-to-all-start.1 = ((f32[4,128,128]{2,1,0:T(8,128)}), f32[4,128,128]{2,1,0:T(8,128)S(1)}, u32[]{:S(2)}, u32[]{:S(2)}) async-start(f32[4,128,128]{2,1,0:T(8,128)} %shard_map.84), calls=%async_computation.1 | async-start | bytes 524288 | tf_op jit(solution)/shard_map/all_to_all | solution.py:210
  37.6 0.1 dynamic-slice_bitcast_fusion.index_ref
  37.7 0.7 copy-done.12
  38.4 0.1 shard_map.85.weights_ref
  38.5 4.5 %all-to-all-done.1.fields_ref = f32[4,128,128]{2,1,0:T(8,128)S(1)} async-done(((f32[4,128,128]{2,1,0:T(8,128)}), f32[4,128,128]{2,1,0:T(8,128)S(1)}, u32[]{:S(2)}, u32[]{:S(2)}) %all-to-all-start.1) | async-done | bytes 262176 | tf_op jit(solution)/shard_map/all_to_all | solution.py:210
  43.0 0.1 shard_map.86
  43.1 8.1 %all_to_all.20 = f32[4,128,128]{2,1,0:T(8,128)S(1)} all-to-all(f32[4,128,128]{2,1,0:T(8,128)S(1)} %shard_map.86), channel_id=1, replica_groups=mesh['kern'=4,'tile'=8] {'kern'}, dimensions={0} | all-to-all | bytes 524288 | tf_op jit(solution)/shard_map/all_to_all | solution.py:223
  51.2 2.0 %shard_map.87 = f32[8,2,80,128]{3,2,1,0:T(8,128)S(1)} custom-call(f32[512,128]{1,0:T(8,128)S(1)} %bitcast.19, f32[12,80,512]{2,1,0:T(8,128)S(1)} %bitcast.14), custom_call_target="tpu_custom_call" | custom-call | flops 503316480 | bytes 2457600 | tf_op jit(solution)/shard_map/pallas_call | solution.py:83
  53.3 0.8 %copy-done.8 = f32[8,2,80,128]{3,2,1,0:T(8,128)} copy-done((f32[8,2,80,128]{3,2,1,0:T(8,128)}, f32[8,2,80,128]{3,2,1,0:T(8,128)S(1)}, u32[]{:S(2)}) %copy-start.8) | copy-done | bytes 655384
  54.1 3.7 %all-to-all-start.3 = ((f32[8,2,80,128]{3,2,1,0:T(8,128)}), f32[8,2,80,128]{3,2,1,0:T(8,128)S(1)}, u32[]{:S(2)}, u32[]{:S(2)}) async-start(f32[8,2,80,128]{3,2,1,0:T(8,128)} %copy-done.8), calls=%async_computation.3 | async-start | bytes 1310720 | tf_op jit(solution)/shard_map/all_to_all | solution.py:174
  57.8 1.2 %copy-done.5 = f32[1,1,512,512]{3,2,1,0:T(8,128)S(1)} copy-done((f32[1,1,512,512]{3,2,1,0:T(8,128)S(1)}, f32[1,1,512,512]{3,2,1,0:T(8,128)}, u32[]{:S(2)}) %copy-start.5) | copy-done | bytes 1048600
  59.0 0.5 shard_map.88.diag_ref
  59.5 16.4 %all-to-all-done.3.got_ref = f32[8,2,80,128]{3,2,1,0:T(8,128)S(1)} async-done(((f32[8,2,80,128]{3,2,1,0:T(8,128)}), f32[8,2,80,128]{3,2,1,0:T(8,128)S(1)}, u32[]{:S(2)}, u32[]{:S(2)}) %all-to-all-start.3) | async-done | bytes 655392 | tf_op jit(solution)/shard_map/all_to_all | solution.py:174
  75.9 2.0 %shard_map.89 = f32[512,128]{1,0:T(8,128)} custom-call(s32[1,8]{1,0:T(1,128)S(1)} %bitcast.25, s32[1,8]{1,0:T(1,128)S(1)} %bitcast.27, f32[8,2,80,128]{3,2,1,0:T(8,128)S(1)} %all-to-all-done.3.got_ref, f32[8,80,512]{2,1,0:T(8,128)S(1)} %bitcast.16, f32[512,128]{1,0:T(8,128)S(1)} %shard_map.88.diag_ref), custom_call_target="tpu_custom_call" | custom-call | flops 335544320 | bytes 1638400 | tf_op jit(solution)/shard_map/pallas_call | solution.py:152
  (24 shorter events, 0.0 us)
Async XLA Ops:
  0.0 37.6 %copy-start = (s32[512]{0:T(512)S(1)}, s32[512]{0:T(512)}, u32[]{:S(2)}) copy-start(s32[512]{0:T(512)} %param.14) | copy-start | bytes 6148
  0.0 1.6 %copy-start.1 = (f32[1,1,12,80,512]{4,3,2,1,0:T(8,128)S(1)}, f32[1,1,12,80,512]{4,3,2,1,0:T(8,128)}, u32[]{:S(2)}) copy-start(f32[1,1,12,80,512]{4,3,2,1,0:T(8,128)} %param.10) | copy-start | bytes 5898244
  1.6 0.9 %copy-start.10 = (f32[1,512,128]{2,1,0:T(8,128)S(1)}, f32[1,512,128]{2,1,0:T(8,128)}, u32[]{:S(2)}) copy-start(f32[1,512,128]{2,1,0:T(8,128)} %param.15) | copy-start | bytes 786436
  2.5 9.3 %copy-start.4 = (f32[1,1,512,512]{3,2,1,0:T(8,128)S(1)}, f32[1,1,512,512]{3,2,1,0:T(8,128)}, u32[]{:S(2)}) copy-start(f32[1,1,512,512]{3,2,1,0:T(8,128)} %param.8) | copy-start | bytes 3145732
  2.5 9.4 %copy-start.11 = (f32[1,512,128]{2,1,0:T(8,128)S(1)}, f32[1,512,128]{2,1,0:T(8,128)}, u32[]{:S(2)}) copy-start(f32[1,512,128]{2,1,0:T(8,128)} %param.15) | copy-start | bytes 786436
  4.5 0.9 %copy-start.9 = (f32[8,2,80,128]{3,2,1,0:T(8,128)}, f32[8,2,80,128]{3,2,1,0:T(8,128)S(1)}, u32[]{:S(2)}) copy-start(f32[8,2,80,128]{3,2,1,0:T(8,128)S(1)} %shard_map.82) | copy-start | bytes 1966084
  5.4 25.5 %copy-start.3 = (f32[1,1,8,80,512]{4,3,2,1,0:T(8,128)S(1)}, f32[1,1,8,80,512]{4,3,2,1,0:T(8,128)}, u32[]{:S(2)}) copy-start(f32[1,1,8,80,512]{4,3,2,1,0:T(8,128)} %param.9) | copy-start | bytes 3932164
  5.4 25.5 %copy-start.13 = (s32[1,1,8]{2,1,0:T(1,128)S(1)}, s32[1,1,8]{2,1,0:T(1,128)}, u32[]{:S(2)}) copy-start(s32[1,1,8]{2,1,0:T(1,128)} %param.11) | copy-start | bytes 100
  5.4 25.5 %copy-start.14 = (s32[1,1,8]{2,1,0:T(1,128)S(1)}, s32[1,1,8]{2,1,0:T(1,128)}, u32[]{:S(2)}) copy-start(s32[1,1,8]{2,1,0:T(1,128)} %param.12) | copy-start | bytes 100
  5.4 24.6 %all-to-all-start = ((f32[8,2,80,128]{3,2,1,0:T(8,128)}), f32[8,2,80,128]{3,2,1,0:T(8,128)S(1)}, u32[]{:S(2)}, u32[]{:S(2)}) async-start(f32[8,2,80,128]{3,2,1,0:T(8,128)} %copy-done.9), calls=%async_computation | async-start | bytes 1310720 | tf_op jit(solution)/shard_map/all_to_all | solution.py:174
  30.0 0.9 %copy-start.6 = (f32[8,2,80,128]{3,2,1,0:T(8,128)}, f32[8,2,80,128]{3,2,1,0:T(8,128)S(1)}, u32[]{:S(2)}) copy-start(f32[8,2,80,128]{3,2,1,0:T(8,128)S(1)} %all-to-all-done.got_ref) | copy-start | bytes 1966084
  30.9 1.1 %copy-start.7 = (f32[8,2,80,128]{3,2,1,0:T(8,128)S(1)}, f32[8,2,80,128]{3,2,1,0:T(8,128)}, u32[]{:S(2)}) copy-start(f32[8,2,80,128]{3,2,1,0:T(8,128)} %copy-done.6) | copy-start | bytes 1966084
  32.0 19.3 %copy-start.2 = (f32[1,1,12,80,512]{4,3,2,1,0:T(8,128)S(1)}, f32[1,1,12,80,512]{4,3,2,1,0:T(8,128)}, u32[]{:S(2)}) copy-start(f32[1,1,12,80,512]{4,3,2,1,0:T(8,128)} %param.10) | copy-start | bytes 5898244
  33.9 9.1 %all-to-all-start.1 = ((f32[4,128,128]{2,1,0:T(8,128)}), f32[4,128,128]{2,1,0:T(8,128)S(1)}, u32[]{:S(2)}, u32[]{:S(2)}) async-start(f32[4,128,128]{2,1,0:T(8,128)} %shard_map.84), calls=%async_computation.1 | async-start | bytes 524288 | tf_op jit(solution)/shard_map/all_to_all | solution.py:210
  37.7 0.7 copy-start.12
  53.3 0.9 %copy-start.8 = (f32[8,2,80,128]{3,2,1,0:T(8,128)}, f32[8,2,80,128]{3,2,1,0:T(8,128)S(1)}, u32[]{:S(2)}) copy-start(f32[8,2,80,128]{3,2,1,0:T(8,128)S(1)} %shard_map.87) | copy-start | bytes 1966084
  54.1 21.8 %copy-start.15 = (s32[1,1,8]{2,1,0:T(1,128)S(1)}, s32[1,1,8]{2,1,0:T(1,128)}, u32[]{:S(2)}) copy-start(s32[1,1,8]{2,1,0:T(1,128)} %param.12) | copy-start | bytes 100
  54.1 21.8 %all-to-all-start.3 = ((f32[8,2,80,128]{3,2,1,0:T(8,128)}), f32[8,2,80,128]{3,2,1,0:T(8,128)S(1)}, u32[]{:S(2)}, u32[]{:S(2)}) async-start(f32[8,2,80,128]{3,2,1,0:T(8,128)} %copy-done.8), calls=%async_computation.3 | async-start | bytes 1310720 | tf_op jit(solution)/shard_map/all_to_all | solution.py:174
  57.8 1.2 %copy-start.5 = (f32[1,1,512,512]{3,2,1,0:T(8,128)S(1)}, f32[1,1,512,512]{3,2,1,0:T(8,128)}, u32[]{:S(2)}) copy-start(f32[1,1,512,512]{3,2,1,0:T(8,128)} %param.8) | copy-start | bytes 3145732

commit v3 on v2

v3 whole, which is shorter than its diff:
```python
import functools

import jax
import jax.numpy as jnp
from jax import lax
from jax.experimental import pallas as pl
from jax.experimental.pallas import tpu as pltpu
from jax.sharding import PartitionSpec as P

f32 = jnp.float32
bf16 = jnp.bfloat16
VMEM_BYTES = 24 * 1024 * 1024
in_vmem = pl.BlockSpec(memory_space=pltpu.VMEM)
in_smem = pl.BlockSpec(memory_space=pltpu.SMEM)
in_hbm = pl.BlockSpec(memory_space=pltpu.HBM)


def to_hbm(value):
    return pltpu.with_memory_space_constraint(value, pltpu.HBM)


def split(value):
    hi = value.astype(bf16)
    return hi, (value - hi.astype(f32)).astype(bf16)


def dot(left, right):
    return jnp.dot(left, right, preferred_element_type=f32)


def call(kernel, outs, out_specs, in_specs, scratch=(), flops=0, moved=0):
    return pl.pallas_call(
        kernel,
        out_shape=outs,
        in_specs=in_specs,
        out_specs=out_specs,
        scratch_shapes=list(scratch),
        compiler_params=pltpu.CompilerParams(vmem_limit_bytes=VMEM_BYTES),
        cost_estimate=pl.CostEstimate(flops=flops, bytes_accessed=moved, transcendentals=0),
    )


def struct(*shape, dtype=f32):
    return jax.ShapeDtypeStruct(shape, dtype)


def offset_of(slot, reach):
    return slot - reach if slot < reach else slot - reach + 1


def paired(count, reach):
    return reach < count <= 2 * reach


def partner(me, step, count):
    if count & (count - 1) == 0:
        return me ^ step, me ^ step
    return lax.rem(me + step, count), lax.rem(me + count - step, count)


def exchange(values, axis):
    count = lax.axis_size(axis)
    arrived = [values[0]]
    for step in range(1, count):
        if count & (count - 1) == 0:
            pairs = [(source, source ^ step) for source in range(count)]
        else:
            pairs = [(source, (source + step) % count) for source in range(count)]
        arrived.append(lax.ppermute(values[step], axis, pairs))
    return arrived


def send_rows(count, slot, reach, piece, held, out_ref, sems):
    held[slot] = piece
    if paired(count, reach):
        offset = offset_of(slot, reach)
        dest = lax.rem(lax.axis_index("tile") - offset + count, count)
        target = out_ref.at[dest, 0 if offset > 0 else 1]
    else:
        target = out_ref.at[slot, 0]
    copy = pltpu.make_async_copy(held.at[slot], target, sems.at[slot])
    copy.start()
    return copy


def first_coeff_kernel(count, chunks, cols_ref, right_ref, out_ref, cols, right, held, in_sems, out_sems):
    slots, rank, size = right_ref.shape
    width = cols_ref.shape[1]
    step = slots // chunks
    cols_copy = pltpu.make_async_copy(cols_ref, cols, in_sems.at[chunks])
    cols_copy.start()
    copies = []
    for at in range(chunks):
        part = pl.ds(at * step, step)
        copies.append(pltpu.make_async_copy(right_ref.at[part], right.at[part], in_sems.at[at]))
        copies[-1].start()
    cols_copy.wait()
    both = jnp.concatenate(split(cols[...]), axis=1)
    sent = []
    for at in range(chunks):
        copies[at].wait()
        hi, lo = split(right[pl.ds(at * step, step)].reshape(step * rank, size))
        got = dot(hi, both) + dot(lo, both)
        got = got[:, :width] + got[:, width:]
        for s in range(step):
            piece = got[s * rank : (s + 1) * rank]
            sent.append(send_rows(count, at * step + s, slots // 2, piece, held, out_ref, out_sems))
    for copy in sent:
        copy.wait()


def lead_shape(count, slots):
    return (count, 2) if paired(count, slots // 2) else (slots, 1)


def first_coefficients(cols, right_tile):
    count = lax.axis_size("tile")
    slots, rank, size = right_tile.shape
    width = cols.shape[1]
    chunks = 4 if slots % 4 == 0 else 1
    return call(
        functools.partial(first_coeff_kernel, count, chunks),
        pltpu.HBM(lead_shape(count, slots) + (rank, width), f32),
        in_hbm,
        [in_hbm, in_hbm],
        [
            pltpu.VMEM(cols.shape, f32),
            pltpu.VMEM(right_tile.shape, f32),
            pltpu.VMEM((slots, rank, width), f32),
            pltpu.SemaphoreType.DMA((chunks + 1,)),
            pltpu.SemaphoreType.DMA((slots,)),
        ],
        flops=8 * slots * rank * size * width,
        moved=4 * slots * rank * (size + width),
    )(to_hbm(cols), to_hbm(right_tile))


def next_coeff_kernel(count, chunks, groups, *refs):
    parts = refs[:groups]
    hi_ref, lo_ref, out_ref, cols_ref, held, out_sems = refs[groups:]
    slots, rank, width = held.shape
    step = slots // chunks
    part, width = parts[0].shape
    me = lax.axis_index("kern")
    for at in range(groups):
        source = partner(me, at, groups)[1]
        cols_ref[pl.ds(pl.multiple_of(source * part, part), part)] = parts[at][...]
    both = jnp.concatenate(split(cols_ref[...]), axis=1)
    sent = []
    for at in range(chunks):
        span = pl.ds(at * step * rank, step * rank)
        got = dot(hi_ref[span], both) + dot(lo_ref[span], both)
        got = got[:, :width] + got[:, width:]
        for s in range(step):
            piece = got[s * rank : (s + 1) * rank]
            sent.append(send_rows(count, at * step + s, slots // 2, piece, held, out_ref, out_sems))
    for copy in sent:
        copy.wait()


def next_coefficients(parts, right_hi, right_lo, slots):
    count = lax.axis_size("tile")
    groups = len(parts)
    part, width = parts[0].shape
    total, size = right_hi.shape
    rank = total // slots
    chunks = 4 if slots % 4 == 0 else 1
    return call(
        functools.partial(next_coeff_kernel, count, chunks, groups),
        [pltpu.HBM(lead_shape(count, slots) + (rank, width), f32), struct(size, width)],
        [in_hbm, in_vmem],
        [in_vmem] * (groups + 2),
        [pltpu.VMEM((slots, rank, width), f32), pltpu.SemaphoreType.DMA((slots,))],
        flops=8 * slots * rank * size * width,
        moved=4 * slots * rank * (size + width),
    )(*parts, right_hi, right_lo)


def times_diag(diag_ref, cols_ref):
    width = cols_ref.shape[1]
    both = jnp.concatenate(split(cols_ref[...]), axis=1)
    hi, lo = split(diag_ref[...])
    got = dot(hi, both) + dot(lo, both)
    return got[:, :width] + got[:, width:]


def diag_kernel(diag_ref, cols_ref, out_ref):
    out_ref[...] = times_diag(diag_ref, cols_ref)


def diagonal(diag_tile, cols):
    size, width = cols.shape
    return call(
        diag_kernel,
        struct(size, width),
        in_vmem,
        [in_vmem, in_vmem],
        flops=8 * size * size * width,
        moved=4 * size * (size + 2 * width),
    )(diag_tile, cols)


def prepare_kernel(
    diag_ref, cols_ref, left_ref, right_ref, table_ref, index_ref,
    diag_out, left_hi, left_lo, right_hi, right_lo, weights_ref,
):
    diag_out[...] = times_diag(diag_ref, cols_ref).T
    for whole, hi_ref, lo_ref in ((left_ref, left_hi, left_lo), (right_ref, right_hi, right_lo)):
        rank = whole.shape[1]
        for at in range(whole.shape[0]):
            span = pl.ds(at * rank, rank)
            hi_ref[span], lo_ref[span] = split(whole[at])
    entries = table_ref.shape[1]
    part = index_ref.shape[1]
    index = index_ref[pl.ds(lax.axis_index("kern"), 1)]
    hot = (lax.broadcasted_iota(jnp.int32, (entries, part), 0) == index).astype(f32)
    weights_ref[...] = jnp.dot(
        table_ref[...], hot, precision=lax.Precision.HIGHEST, preferred_element_type=f32
    )


def prepare(diag_tile, cols, left_tile, right_tile, table, index):
    size, width = cols.shape
    terms, rank, _ = left_tile.shape
    slots = right_tile.shape[0]
    return call(
        prepare_kernel,
        [
            struct(width, size),
            struct(terms * rank, size, dtype=bf16),
            struct(terms * rank, size, dtype=bf16),
            struct(slots * rank, size, dtype=bf16),
            struct(slots * rank, size, dtype=bf16),
            struct(table.shape[0], index.shape[1]),
        ],
        [in_vmem] * 6,
        [in_vmem] * 6,
        flops=8 * size * size * width,
        moved=8 * (terms + slots) * rank * size + 4 * size * (size + 2 * width),
    )(diag_tile, cols, left_tile, right_tile, table, index)


def row_kernel(count, terms, groups, offs_ref, ranks_ref, got_ref, hi_ref, lo_ref, diag_ref, *refs):
    outs, (picked, sems) = refs[:-2], refs[-2:]
    rank, width = got_ref.shape[2:]
    reach = got_ref.shape[0] // 2
    me = lax.axis_index("tile")
    copies = []
    for k in range(terms):
        offset = offs_ref[0, k]
        if got_ref.shape[1] == 2:
            block = got_ref.at[lax.rem(me + offset + count, count), jnp.where(offset > 0, 0, 1)]
        else:
            block = got_ref.at[jnp.where(offset < 0, offset + reach, offset + reach - 1), 0]
        copies.append(pltpu.make_async_copy(block, picked.at[pl.ds(k * rank, rank)], sems.at[k]))
        copies[-1].start()
    line = lax.broadcasted_iota(jnp.int32, (rank, width), 0)
    pieces = []
    for k in range(terms):
        copies[k].wait()
        piece = picked[pl.ds(k * rank, rank)]
        pieces.append(jnp.where(line < ranks_ref[0, k], piece, 0.0))
    both = jnp.concatenate(split(jnp.concatenate(pieces, axis=0).T), axis=0)
    total = dot(both, hi_ref[...]) + dot(both, lo_ref[...])
    total = total[:width] + total[width:]
    if groups > 1:
        total = total + diag_ref[...]
        part = total.shape[1] // groups
        stage = refs[-3]
        for at in range(groups):
            stage[at] = total[:, at * part : (at + 1) * part]
        own = lax.axis_index("kern")
        for at in range(groups):
            outs[at][...] = stage[partner(own, at, groups)[0]]
    else:
        outs[0][...] = total.T + diag_ref[...]


def rows(offsets, ranks, got, left_hi, left_lo, diag_part, groups):
    total, size = left_hi.shape
    rank, width = got.shape[2:]
    terms = total // rank
    part = size // groups
    outs = [struct(width, part)] * groups if groups > 1 else [struct(size, width)]
    scratch = [pltpu.VMEM((total, width), f32), pltpu.SemaphoreType.DMA((terms,))]
    if groups > 1:
        scratch = [pltpu.VMEM((groups, width, part), f32)] + scratch
    return call(
        functools.partial(row_kernel, lax.axis_size("tile"), terms, groups),
        outs,
        [in_vmem] * len(outs),
        [in_smem, in_smem, in_hbm, in_vmem, in_vmem, in_vmem],
        scratch,
        flops=8 * total * size * width,
        moved=4 * total * (size + width),
    )(offsets, ranks, to_hbm(got), left_hi, left_lo, diag_part)


def mix_kernel(groups, *refs):
    fields, weights_ref, outs = refs[:groups], refs[groups], refs[groups + 1 :]
    me = lax.axis_index("kern")
    for at in range(groups):
        base = partner(me, at, groups)[0] * groups
        total = None
        for b in range(groups):
            term = fields[b][...] * weights_ref[pl.ds(base + partner(me, b, groups)[1], 1)]
            total = term if total is None else total + term
        outs[at][...] = total.T


def mix(fields, weights):
    groups = len(fields)
    width, part = fields[0].shape
    return call(
        functools.partial(mix_kernel, groups),
        [struct(part, width)] * groups,
        [in_vmem] * groups,
        [in_vmem] * (groups + 1),
        flops=2 * groups * groups * part * width,
        moved=8 * groups * part * width,
    )(*fields, weights)


def deliver(coeffs, reach):
    count = lax.axis_size("tile")
    if paired(count, reach):
        return lax.all_to_all(coeffs, "tile", split_axis=0, concat_axis=0, tiled=True)
    arrived = []
    for slot in range(2 * reach):
        steps = -offset_of(slot, reach)
        pairs = [(source, (source + steps) % count) for source in range(count)]
        arrived.append(lax.ppermute(coeffs[slot], "tile", pairs))
    return jnp.stack(arrived)


def local(
    diag_tiles,
    left_factors,
    right_factors,
    tile_offsets,
    tile_ranks,
    mixing,
    block_index,
    rhs_field,
):
    diag_tile = diag_tiles[0, 0]
    left_tile = left_factors[0, 0]
    right_tile = right_factors[0, 0]
    offsets = tile_offsets[0]
    ranks = tile_ranks[0]
    slots = right_tile.shape[0]
    groups = lax.axis_size("kern")
    size = rhs_field.shape[1]
    table = mixing.reshape(mixing.shape[0], groups * groups).T
    index = block_index.reshape(groups, size // groups)
    cols = rhs_field[0]

    got = deliver(first_coefficients(cols, right_tile), slots // 2)
    diag_part, left_hi, left_lo, right_hi, right_lo, weights = prepare(
        diag_tile, cols, left_tile, right_tile, table, index
    )
    first = rows(offsets, ranks, got, left_hi, left_lo, diag_part, groups)
    mixed = exchange(mix(exchange(first, "kern"), weights), "kern")
    coeffs, cols = next_coefficients(mixed, right_hi, right_lo, slots)
    got = deliver(coeffs, slots // 2)
    diag_part = diagonal(diag_tile, cols)
    return rows(offsets, ranks, got, left_hi, left_lo, diag_part, 1)[0][None]


def solution(mesh):
    in_specs = (
        P("kern", "tile", None, None),
        P("kern", "tile", None, None, None),
        P("kern", "tile", None, None, None),
        P("kern", "tile", None),
        P("kern", "tile", None),
        P(),
        P("tile"),
        P("kern", "tile", None),
    )
    out_specs = P("kern", "tile", None)
    return jax.shard_map(local, mesh=mesh, in_specs=in_specs, out_specs=out_specs, check_vma=False)
```

time: 78.5 us -> 76.3 us (0.972)
  blocking collectives: 8.11 us -> 0 us
  starting transfers between devices: 13.8 us -> 17.8 us
  Pallas kernels: 9.17 us -> 12 us
  waiting for transfers between devices: 38.5 us -> 36.7 us
  local copies, waits for them, and re-layouts: 8.18 us -> 9.09 us
    all_to_all x1 -> x0, blocking collectives: 8.11 us -> none  [local(): lax.all_to_all(blended, 'kern', split_axis=0, concat_axis=0, tiled=True)]
    ppermute x0 -> x6, waiting for transfers between devices: none -> 7.4 us  [exchange(): arrived.append(lax.ppermute(values[step], axis, pairs))]
    ppermute x0 -> x6, starting transfers between devices: none -> 7.11 us  [exchange(): arrived.append(lax.ppermute(values[step], axis, pairs))]
    all_to_all x2, waiting for transfers between devices: 34 us -> 29.3 us  [deliver(): lax.all_to_all(coeffs, 'tile', split_axis=0, concat_axis=0, tiled=True)]
    all_to_all x1 -> x0, waiting for transfers between devices: 4.46 us -> none  [local(): lax.all_to_all(first, 'kern', split_axis=0, concat_axis=0, tiled=True)]
    all_to_all x1 -> x0, starting transfers between devices: 3.72 us -> none  [local(): lax.all_to_all(first, 'kern', split_axis=0, concat_axis=0, tiled=True)]
    pallas_call x8 -> x7, Pallas kernels: 9.17 us -> 12 us  [the longest x2 5.21 us: rows(): call(functools.partial(row_kernel, lax.axis_size('tile'), terms, groups),...]
    unnamed x32 -> x40, local copies, waits for them, and re-layouts: 8.1 us -> 9.09 us
  transfers between devices with their start and end apart: 3 -> 8, of which waited for: 3 -> 8; matrix products, arithmetic and copies ran while one was open for 0% -> 0% of each run, Pallas kernels for 1% -> 2%
where the time goes in v3:
time: 76.3 us; the launch traced here: 75.7 us
  waiting for transfers between devices  36.7 us (48%)
  starting transfers between devices  17.8 us (23%)
  Pallas kernels  12 us (16%)
  local copies, waits for them, and re-layouts  9.09 us (12%)
    all_to_all x2, waiting for transfers between devices, deliver(): lax.all_to_all(coeffs, 'tile', split_axis=0, concat_axis=0, tiled=True)  29.3 us
    all_to_all x2, starting transfers between devices, deliver(): lax.all_to_all(coeffs, 'tile', split_axis=0, concat_axis=0, tiled=True)  10.7 us
    unnamed x40, local copies, waits for them, and re-layouts  9.09 us
    ppermute x6, waiting for transfers between devices, exchange(): arrived.append(lax.ppermute(values[step], axis, pairs))  7.4 us
    ppermute x6, starting transfers between devices, exchange(): arrived.append(lax.ppermute(values[step], axis, pairs))  7.11 us
    pallas_call x2, Pallas kernels, rows(): call(functools.partial(row_kernel, lax.axis_size('tile'), terms, groups),...  5.21 us
    pallas_call x1, Pallas kernels, first_coefficients(): call(functools.partial(first_coeff_kernel, count, chunks), pltpu.HBM(lead...  3.65 us
  transfers between devices with their start and end apart: 8, of which 8 were waited for; matrix products, arithmetic and copies ran while one was open for 0% of the time, Pallas kernels for 2%

profile of v3, /device:TPU:0, one launch (start us, length us, event | category | flops | bytes accessed | tf_op | source)
XLA Modules:
  0.0 75.7 jit_solution(7132806519612852201)
XLA Ops:
  0.0 3.7 %shard_map.82 = f32[8,2,80,128]{3,2,1,0:T(8,128)} custom-call(f32[512,128]{1,0:T(8,128)} %bitcast.16, f32[12,80,512]{2,1,0:T(8,128)} %bitcast.11), custom_call_target="tpu_custom_call" | custom-call | flops 503316480 | bytes 2457600 | tf_op jit(solution)/shard_map/pallas_call | solution.py:121
  3.7 6.3 %all-to-all-start = ((f32[8,2,80,128]{3,2,1,0:T(8,128)}), f32[8,2,80,128]{3,2,1,0:T(8,128)}, u32[]{:S(2)}, u32[]{:S(2)}) async-start(f32[8,2,80,128]{3,2,1,0:T(8,128)} %shard_map.82), calls=%async_computation | async-start | bytes 1310720 | tf_op jit(solution)/shard_map/all_to_all | solution.py:327
  10.1 1.3 %copy-done.8 = f32[1,1,8,80,512]{4,3,2,1,0:T(8,128)S(1)} copy-done((f32[1,1,8,80,512]{4,3,2,1,0:T(8,128)S(1)}, f32[1,1,8,80,512]{4,3,2,1,0:T(8,128)}, u32[]{:S(2)}) %copy-start.8) | copy-done | bytes 1310744
  12.0 1.1 %shard_map.83 = (f32[128,512]{1,0:T(8,128)S(1)}, bf16[640,512]{1,0:T(8,128)(2,1)S(1)}, bf16[640,512]{1,0:T(8,128)(2,1)S(1)}, bf16[960,512]{1,0:T(8,128)(2,1)S(1)...) custom-call(f32[512,512]{1,0:T(8,128)S(1)} %bitcast.13, f32[512,128]{1,0:T(8,128)S(1)} %bitcast.17, ...), custom_call_target="tpu_custom_call" | custom-call | flops 268435456 | bytes 8126464 | tf_op jit(solution)/shard_map/pallas_call | solution.py:226
  13.2 0.8 %copy-done.2 = bf16[640,512]{1,0:T(8,128)(2,1)} copy-done((bf16[640,512]{1,0:T(8,128)(2,1)}, bf16[640,512]{1,0:T(8,128)(2,1)S(1)}, u32[]{:S(2)}) %copy-start.2) | copy-done | bytes 655384
  14.0 0.8 %copy-done.5 = bf16[640,512]{1,0:T(8,128)(2,1)} copy-done((bf16[640,512]{1,0:T(8,128)(2,1)}, bf16[640,512]{1,0:T(8,128)(2,1)S(1)}, u32[]{:S(2)}) %copy-start.5) | copy-done | bytes 655384
  14.8 1.0 %copy-done.10 = bf16[960,512]{1,0:T(8,128)(2,1)} copy-done((bf16[960,512]{1,0:T(8,128)(2,1)}, bf16[960,512]{1,0:T(8,128)(2,1)S(1)}, u32[]{:S(2)}) %copy-start.10) | copy-done | bytes 983064
  15.8 0.9 %copy-done.12 = bf16[960,512]{1,0:T(8,128)(2,1)} copy-done((bf16[960,512]{1,0:T(8,128)(2,1)}, bf16[960,512]{1,0:T(8,128)(2,1)S(1)}, u32[]{:S(2)}) %copy-start.12) | copy-done | bytes 983064
  16.7 11.6 %all-to-all-done.got_ref = f32[8,2,80,128]{3,2,1,0:T(8,128)} async-done(((f32[8,2,80,128]{3,2,1,0:T(8,128)}), f32[8,2,80,128]{3,2,1,0:T(8,128)}, u32[]{:S(2)}, u32[]{:S(2)}) %all-to-all-start) | async-done | bytes 655392 | tf_op jit(solution)/shard_map/all_to_all | solution.py:327
  28.3 1.1 %copy-done.3 = bf16[640,512]{1,0:T(8,128)(2,1)S(1)} copy-done((bf16[640,512]{1,0:T(8,128)(2,1)S(1)}, bf16[640,512]{1,0:T(8,128)(2,1)}, u32[]{:S(2)}) %copy-start.3) | copy-done | bytes 655384
  29.4 1.1 %copy-done.6 = bf16[640,512]{1,0:T(8,128)(2,1)S(1)} copy-done((bf16[640,512]{1,0:T(8,128)(2,1)S(1)}, bf16[640,512]{1,0:T(8,128)(2,1)}, u32[]{:S(2)}) %copy-start.6) | copy-done | bytes 655384
  31.8 2.2 %shard_map.84 = (f32[128,128]{1,0:T(8,128)S(1)}, f32[128,128]{1,0:T(8,128)S(1)}, f32[128,128]{1,0:T(8,128)S(1)}, f32[128,128]{1,0:T(8,128)S(1)}) custom-call(s32[1,8]{1,0:T(1,128)S(1)} %bitcast.20, s32[1,8]{1,0:T(1,128)S(1)} %bitcast.22, f32[8,2,80,128]{3,2,1,0:T(8,128)} %all-to-all-done.got_ref, bf16[640,512]{1,0:T(8,128)(2,1)S(1)} %copy-done.3, ...), custom_call_target="tpu_custom_call" | custom-call | flops 335544320 | bytes 1638400 | tf_op jit(solution)/shard_map/pallas_call | solution.py:288
  34.0 1.6 %collective-permute-start = (f32[128,128]{1,0:T(8,128)S(1)}, f32[128,128]{1,0:T(8,128)S(1)}, u32[]{:S(2)}, u32[]{:S(2)}) collective-permute-start(f32[128,128]{1,0:T(8,128)S(1)} %get-tuple-element.25), channel_id=1, source_target_pairs={{0,8},{8,0},{16,24},{24,16},{1,9},{9,1},{17,25},{25,17},{2,10},{10... | collective-permute-start | bytes 196616 | tf_op jit(solution)/shard_map/ppermute | solution.py:69
  35.6 1.5 %collective-permute-start.1 = (f32[128,128]{1,0:T(8,128)S(1)}, f32[128,128]{1,0:T(8,128)S(1)}, u32[]{:S(2)}, u32[]{:S(2)}) collective-permute-start(f32[128,128]{1,0:T(8,128)S(1)} %get-tuple-element.26), channel_id=1, source_target_pairs={{0,16},{8,24},{16,0},{24,8},{1,17},{9,25},{17,1},{25,9},{2,18},{10... | collective-permute-start | bytes 196616 | tf_op jit(solution)/shard_map/ppermute | solution.py:69
  37.6 0.8 %collective-permute-done.refs_1_ = f32[128,128]{1,0:T(8,128)S(1)} collective-permute-done((f32[128,128]{1,0:T(8,128)S(1)}, f32[128,128]{1,0:T(8,128)S(1)}, u32[]{:S(2)}, u32[]{:S(2)}) %collective-permute-start) | collective-permute-done | bytes 65568 | tf_op jit(solution)/shard_map/ppermute | solution.py:69
  38.3 2.2 %collective-permute-done.1.refs_2_ = f32[128,128]{1,0:T(8,128)S(1)} collective-permute-done((f32[128,128]{1,0:T(8,128)S(1)}, f32[128,128]{1,0:T(8,128)S(1)}, u32[]{:S(2)}, u32[]{:S(2)}) %collective-permute-start.1) | collective-permute-done | bytes 65568 | tf_op jit(solution)/shard_map/ppermute | solution.py:69
  40.5 1.7 %collective-permute-done.2.refs_3_ = f32[128,128]{1,0:T(8,128)S(1)} collective-permute-done((f32[128,128]{1,0:T(8,128)S(1)}, f32[128,128]{1,0:T(8,128)S(1)}, u32[]{:S(2)}, u32[]{:S(2)}) %collective-permute-start.2) | collective-permute-done | bytes 65568 | tf_op jit(solution)/shard_map/ppermute | solution.py:69
  43.5 2.5 %collective-permute-start.5 = (f32[128,128]{1,0:T(8,128)S(1)}, f32[128,128]{1,0:T(8,128)S(1)}, u32[]{:S(2)}, u32[]{:S(2)}) collective-permute-start(f32[128,128]{1,0:T(8,128)S(1)} %get-tuple-element.32), channel_id=1, source_target_pairs={{0,24},{8,16},{16,8},{24,0},{1,25},{9,17},{17,9},{25,1},{2,26},{10... | collective-permute-start | bytes 196616 | tf_op jit(solution)/shard_map/ppermute | solution.py:69
  46.0 0.8 %collective-permute-done.3.refs_1_ = f32[128,128]{1,0:T(8,128)S(1)} collective-permute-done((f32[128,128]{1,0:T(8,128)S(1)}, f32[128,128]{1,0:T(8,128)S(1)}, u32[]{:S(2)}, u32[]{:S(2)}) %collective-permute-start.3) | collective-permute-done | bytes 65568 | tf_op jit(solution)/shard_map/ppermute | solution.py:69
  47.3 1.4 %collective-permute-done.5.refs_3_ = f32[128,128]{1,0:T(8,128)S(1)} collective-permute-done((f32[128,128]{1,0:T(8,128)S(1)}, f32[128,128]{1,0:T(8,128)S(1)}, u32[]{:S(2)}, u32[]{:S(2)}) %collective-permute-start.5) | collective-permute-done | bytes 65568 | tf_op jit(solution)/shard_map/ppermute | solution.py:69
  48.7 1.5 %shard_map.86 = (f32[8,2,80,128]{3,2,1,0:T(8,128)}, f32[512,128]{1,0:T(8,128)S(1)}) custom-call(f32[128,128]{1,0:T(8,128)S(1)} %get-tuple-element.29.refs_0_, f32[128,128]{1,0:T(8,128)S(1)} %collective-permute-done.3.refs_1_, f32[128,128]{1,0:T(8,128)S(1)} %collective-permute-done.4.refs_2_, f32[128,128]{1,0:T(8,128)S(1)} %collective-permute-done.5.refs_3_, ...), custom_call_target="tpu_custom_call" | custom-call | flops 503316480 | bytes 2457600 | tf_op jit(solution)/shard_map/pallas_call | solution.py:168
  50.2 4.3 %all-to-all-start.1 = ((f32[8,2,80,128]{3,2,1,0:T(8,128)}), f32[8,2,80,128]{3,2,1,0:T(8,128)}, u32[]{:S(2)}, u32[]{:S(2)}) async-start(f32[8,2,80,128]{3,2,1,0:T(8,128)} %get-tuple-element.35), calls=%async_computation.1 | async-start | bytes 1310720 | tf_op jit(solution)/shard_map/all_to_all | solution.py:327
  55.0 17.7 %all-to-all-done.1.got_ref = f32[8,2,80,128]{3,2,1,0:T(8,128)} async-done(((f32[8,2,80,128]{3,2,1,0:T(8,128)}), f32[8,2,80,128]{3,2,1,0:T(8,128)}, u32[]{:S(2)}, u32[]{:S(2)}) %all-to-all-start.1) | async-done | bytes 655392 | tf_op jit(solution)/shard_map/all_to_all | solution.py:327
  72.8 3.0 %shard_map.88 = f32[512,128]{1,0:T(8,128)} custom-call(s32[1,8]{1,0:T(1,128)S(1)} %bitcast.21, s32[1,8]{1,0:T(1,128)S(1)} %bitcast.23, f32[8,2,80,128]{3,2,1,0:T(8,128)} %all-to-all-done.1.got_ref, bf16[640,512]{1,0:T(8,128)(2,1)S(1)} %copy-done.4, bf16[640,512]{1,0:T(8,128)(2,1)S(1)} %copy-done.7, f32[512,128]{1,0:T(8,128)S(1)} %shard_map.87.diag_ref), custom_call_target="tpu_custom_call" | custom-call | flops 335544320 | bytes 1638400 | tf_op jit(solution)/shard_map/pallas_call | solution.py:288
  (39 shorter events, 4.7 us)
Async XLA Ops:
  0.0 10.0 %copy-start = (f32[1,1,12,80,512]{4,3,2,1,0:T(8,128)S(1)}, f32[1,1,12,80,512]{4,3,2,1,0:T(8,128)}, u32[]{:S(2)}) copy-start(f32[1,1,12,80,512]{4,3,2,1,0:T(8,128)} %param.10) | copy-start | bytes 5898244
  0.0 10.0 %copy-start.1 = (f32[1,1,512,512]{3,2,1,0:T(8,128)S(1)}, f32[1,1,512,512]{3,2,1,0:T(8,128)}, u32[]{:S(2)}) copy-start(f32[1,1,512,512]{3,2,1,0:T(8,128)} %param.8) | copy-start | bytes 3145732
  0.0 10.0 %copy-start.9 = (f32[1,512,128]{2,1,0:T(8,128)S(1)}, f32[1,512,128]{2,1,0:T(8,128)}, u32[]{:S(2)}) copy-start(f32[1,512,128]{2,1,0:T(8,128)} %param.15) | copy-start | bytes 786436
  0.0 10.0 %copy-start.14 = (f32[64,4,4]{0,2,1:T(4,128)S(1)}, f32[64,4,4]{0,2,1:T(4,128)}, u32[]{:S(2)}) copy-start(f32[64,4,4]{0,2,1:T(4,128)} %param.13) | copy-start | bytes 12292
  3.7 24.6 %all-to-all-start = ((f32[8,2,80,128]{3,2,1,0:T(8,128)}), f32[8,2,80,128]{3,2,1,0:T(8,128)}, u32[]{:S(2)}, u32[]{:S(2)}) async-start(f32[8,2,80,128]{3,2,1,0:T(8,128)} %shard_map.82), calls=%async_computation | async-start | bytes 1310720 | tf_op jit(solution)/shard_map/all_to_all | solution.py:327
  10.0 1.3 %copy-start.8 = (f32[1,1,8,80,512]{4,3,2,1,0:T(8,128)S(1)}, f32[1,1,8,80,512]{4,3,2,1,0:T(8,128)}, u32[]{:S(2)}) copy-start(f32[1,1,8,80,512]{4,3,2,1,0:T(8,128)} %param.9) | copy-start | bytes 3932164
  13.1 0.9 %copy-start.2 = (bf16[640,512]{1,0:T(8,128)(2,1)}, bf16[640,512]{1,0:T(8,128)(2,1)S(1)}, u32[]{:S(2)}) copy-start(bf16[640,512]{1,0:T(8,128)(2,1)S(1)} %get-tuple-element.21.hi_ref) | copy-start | bytes 1966084
  14.8 1.0 %copy-start.10 = (bf16[960,512]{1,0:T(8,128)(2,1)}, bf16[960,512]{1,0:T(8,128)(2,1)S(1)}, u32[]{:S(2)}) copy-start(bf16[960,512]{1,0:T(8,128)(2,1)S(1)} %get-tuple-element.33.refs_4_) | copy-start | bytes 2949124
  15.8 0.9 %copy-start.12 = (bf16[960,512]{1,0:T(8,128)(2,1)}, bf16[960,512]{1,0:T(8,128)(2,1)S(1)}, u32[]{:S(2)}) copy-start(bf16[960,512]{1,0:T(8,128)(2,1)S(1)} %get-tuple-element.34.refs_5_) | copy-start | bytes 2949124
  28.3 1.1 %copy-start.3 = (bf16[640,512]{1,0:T(8,128)(2,1)S(1)}, bf16[640,512]{1,0:T(8,128)(2,1)}, u32[]{:S(2)}) copy-start(bf16[640,512]{1,0:T(8,128)(2,1)} %copy-done.2) | copy-start | bytes 1966084
  29.4 1.1 %copy-start.6 = (bf16[640,512]{1,0:T(8,128)(2,1)S(1)}, bf16[640,512]{1,0:T(8,128)(2,1)}, u32[]{:S(2)}) copy-start(bf16[640,512]{1,0:T(8,128)(2,1)} %copy-done.5) | copy-start | bytes 1966084
  31.8 16.9 %copy-start.11 = (bf16[960,512]{1,0:T(8,128)(2,1)S(1)}, bf16[960,512]{1,0:T(8,128)(2,1)}, u32[]{:S(2)}) copy-start(bf16[960,512]{1,0:T(8,128)(2,1)} %copy-done.10) | copy-start | bytes 2949124
  31.8 16.9 %copy-start.13 = (bf16[960,512]{1,0:T(8,128)(2,1)S(1)}, bf16[960,512]{1,0:T(8,128)(2,1)}, u32[]{:S(2)}) copy-start(bf16[960,512]{1,0:T(8,128)(2,1)} %copy-done.12) | copy-start | bytes 2949124
  34.0 4.3 %collective-permute-start = (f32[128,128]{1,0:T(8,128)S(1)}, f32[128,128]{1,0:T(8,128)S(1)}, u32[]{:S(2)}, u32[]{:S(2)}) collective-permute-start(f32[128,128]{1,0:T(8,128)S(1)} %get-tuple-element.25), channel_id=1, source_target_pairs={{0,8},{8,0},{16,24},{24,16},{1,9},{9,1},{17,25},{25,17},{2,10},{10... | collective-permute-start | bytes 196616 | tf_op jit(solution)/shard_map/ppermute | solution.py:69
  35.6 5.0 %collective-permute-start.1 = (f32[128,128]{1,0:T(8,128)S(1)}, f32[128,128]{1,0:T(8,128)S(1)}, u32[]{:S(2)}, u32[]{:S(2)}) collective-permute-start(f32[128,128]{1,0:T(8,128)S(1)} %get-tuple-element.26), channel_id=1, source_target_pairs={{0,16},{8,24},{16,0},{24,8},{1,17},{9,25},{17,1},{25,9},{2,18},{10... | collective-permute-start | bytes 196616 | tf_op jit(solution)/shard_map/ppermute | solution.py:69
  37.1 5.2 %collective-permute-start.2 = (f32[128,128]{1,0:T(8,128)S(1)}, f32[128,128]{1,0:T(8,128)S(1)}, u32[]{:S(2)}, u32[]{:S(2)}) collective-permute-start(f32[128,128]{1,0:T(8,128)S(1)} %get-tuple-element.27), channel_id=1, source_target_pairs={{0,24},{8,16},{16,8},{24,0},{1,25},{9,17},{17,9},{25,1},{2,26},{10... | collective-permute-start | bytes 196616 | tf_op jit(solution)/shard_map/ppermute | solution.py:69
  42.4 4.3 %collective-permute-start.3 = (f32[128,128]{1,0:T(8,128)S(1)}, f32[128,128]{1,0:T(8,128)S(1)}, u32[]{:S(2)}, u32[]{:S(2)}) collective-permute-start(f32[128,128]{1,0:T(8,128)S(1)} %get-tuple-element.30), channel_id=1, source_target_pairs={{0,8},{8,0},{16,24},{24,16},{1,9},{9,1},{17,25},{25,17},{2,10},{10... | collective-permute-start | bytes 196616 | tf_op jit(solution)/shard_map/ppermute | solution.py:69
  43.0 4.3 %collective-permute-start.4 = (f32[128,128]{1,0:T(8,128)S(1)}, f32[128,128]{1,0:T(8,128)S(1)}, u32[]{:S(2)}, u32[]{:S(2)}) collective-permute-start(f32[128,128]{1,0:T(8,128)S(1)} %get-tuple-element.31), channel_id=1, source_target_pairs={{0,16},{8,24},{16,0},{24,8},{1,17},{9,25},{17,1},{25,9},{2,18},{10... | collective-permute-start | bytes 196616 | tf_op jit(solution)/shard_map/ppermute | solution.py:69
  43.5 5.2 %collective-permute-start.5 = (f32[128,128]{1,0:T(8,128)S(1)}, f32[128,128]{1,0:T(8,128)S(1)}, u32[]{:S(2)}, u32[]{:S(2)}) collective-permute-start(f32[128,128]{1,0:T(8,128)S(1)} %get-tuple-element.32), channel_id=1, source_target_pairs={{0,24},{8,16},{16,8},{24,0},{1,25},{9,17},{17,9},{25,1},{2,26},{10... | collective-permute-start | bytes 196616 | tf_op jit(solution)/shard_map/ppermute | solution.py:69
  50.2 22.6 %copy-start.4 = (bf16[640,512]{1,0:T(8,128)(2,1)S(1)}, bf16[640,512]{1,0:T(8,128)(2,1)}, u32[]{:S(2)}) copy-start(bf16[640,512]{1,0:T(8,128)(2,1)} %copy-done.2) | copy-start | bytes 1966084
  50.2 22.6 %copy-start.7 = (bf16[640,512]{1,0:T(8,128)(2,1)S(1)}, bf16[640,512]{1,0:T(8,128)(2,1)}, u32[]{:S(2)}) copy-start(bf16[640,512]{1,0:T(8,128)(2,1)} %copy-done.5) | copy-start | bytes 1966084
  50.2 22.6 %copy-start.17 = (s32[1,1,8]{2,1,0:T(1,128)S(1)}, s32[1,1,8]{2,1,0:T(1,128)}, u32[]{:S(2)}) copy-start(s32[1,1,8]{2,1,0:T(1,128)} %param.11) | copy-start | bytes 100
  50.2 22.5 %copy-start.19 = (s32[1,1,8]{2,1,0:T(1,128)S(1)}, s32[1,1,8]{2,1,0:T(1,128)}, u32[]{:S(2)}) copy-start(s32[1,1,8]{2,1,0:T(1,128)} %param.12) | copy-start | bytes 100
  50.2 22.5 %all-to-all-start.1 = ((f32[8,2,80,128]{3,2,1,0:T(8,128)}), f32[8,2,80,128]{3,2,1,0:T(8,128)}, u32[]{:S(2)}, u32[]{:S(2)}) async-start(f32[8,2,80,128]{3,2,1,0:T(8,128)} %get-tuple-element.35), calls=%async_computation.1 | async-start | bytes 1310720 | tf_op jit(solution)/shard_map/all_to_all | solution.py:327
  (4 other events, 2.8 us)

commit v4 on v0

v4 whole, which is shorter than its diff:
```python
import functools

import jax
import jax.numpy as jnp
from jax import lax
from jax.experimental import pallas as pl
from jax.experimental.pallas import tpu as pltpu
from jax.sharding import PartitionSpec as P

f32 = jnp.float32
bf16 = jnp.bfloat16
VMEM_BYTES = 24 * 1024 * 1024
in_vmem = pl.BlockSpec(memory_space=pltpu.VMEM)
in_smem = pl.BlockSpec(memory_space=pltpu.SMEM)
in_hbm = pl.BlockSpec(memory_space=pltpu.HBM)


def to_hbm(value):
    return pltpu.with_memory_space_constraint(value, pltpu.HBM)


def struct(*shape, dtype=f32):
    return jax.ShapeDtypeStruct(shape, dtype)


def split(value):
    hi = value.astype(bf16)
    return hi, (value - hi.astype(f32)).astype(bf16)


def side_by_side(value):
    return jnp.concatenate(split(value), axis=1)


def dot(left, right):
    return jnp.dot(left, right, preferred_element_type=f32)


def fold(value):
    width = value.shape[1] // 2
    return value[:, :width] + value[:, width:]


def call(kernel, outs, out_specs, in_specs, scratch=(), flops=0, moved=0):
    return pl.pallas_call(
        kernel,
        out_shape=outs,
        in_specs=in_specs,
        out_specs=out_specs,
        scratch_shapes=list(scratch),
        compiler_params=pltpu.CompilerParams(vmem_limit_bytes=VMEM_BYTES),
        cost_estimate=pl.CostEstimate(flops=flops, bytes_accessed=moved, transcendentals=0),
    )


def step_pairs(count, step):
    if count & (count - 1) == 0:
        return [(source, source ^ step) for source in range(count)]
    return [(source, (source + step) % count) for source in range(count)]


def partner(me, step, count):
    if count & (count - 1) == 0:
        return me ^ step, me ^ step
    return lax.rem(me + step, count), lax.rem(me + count - step, count)


def exchange(values, axis):
    count = lax.axis_size(axis)
    arrived = [values[0]]
    for step in range(1, count):
        arrived.append(lax.ppermute(values[step], axis, step_pairs(count, step)))
    return arrived


class Message:
    def __init__(self, count, reach, step=None, slot=None):
        self.count, self.reach, self.step, self.slot = count, reach, step, slot
        if slot is not None:
            offset = slot - reach if slot < reach else slot - reach + 1
            self.width = 1
            self.pairs = [(source, (source - offset) % count) for source in range(count)]
        else:
            self.pairs = step_pairs(count, step)
            self.width = 1
            for source, dest in self.pairs:
                ahead = (source - dest) % count
                if ahead <= reach and count - ahead <= reach:
                    self.width = 2

    def slots(self, me, sending):
        if self.slot is not None:
            return [(self.slot, True)]
        count, reach = self.count, self.reach
        dest, source = partner(me, self.step, count)
        column, row = (me, dest) if sending else (source, me)
        ahead = lax.rem(column - row + count, count)
        first = jnp.where(ahead <= reach, ahead + reach - 1, ahead - count + reach)
        if self.width == 1:
            return [(first, True)]
        both = jnp.logical_and(ahead <= reach, count - ahead <= reach)
        return [(first, True), (jnp.where(both, ahead - count + reach, first), both)]


def messages_of(count, slots):
    reach = slots // 2
    if reach < count <= 2 * reach:
        return [Message(count, reach, step=step) for step in range(count - 1, 0, -1)]
    return [Message(count, reach, slot=slot) for slot in range(slots)]


def chunks_of(messages, most=4):
    chunks, held = [[]], 0
    for at, message in enumerate(messages):
        if held and held + message.width > most:
            chunks.append([])
            held = 0
        chunks[-1].append(at)
        held += message.width
    return chunks


def chunk_coefficients(split_ref, base, chunk, messages, rank, both, outs):
    size = rank * sum(messages[at].width for at in chunk)
    got = fold(dot(split_ref[pl.ds(base, 2 * size)], both))
    got = got[:size] + got[size:]
    row = 0
    for at in chunk:
        for w in range(messages[at].width):
            outs[at][w] = got[row : row + rank]
            row += rank
    return base + 2 * size


def first_coeff_kernel(messages, cols_ref, right_ref, *refs):
    outs, (split_ref, cols, right, sems) = refs[: len(messages)], refs[len(messages) :]
    rank = right_ref.shape[1]
    me = lax.axis_index("tile")
    cols_copy = pltpu.make_async_copy(cols_ref, cols, sems.at[right.shape[0]])
    cols_copy.start()
    copies = []
    for message in messages:
        for slot, _ in message.slots(me, True):
            at = len(copies)
            copies.append(pltpu.make_async_copy(right_ref.at[slot], right.at[at], sems.at[at]))
            copies[-1].start()
    cols_copy.wait()
    both = side_by_side(cols[...])
    base, block = 0, 0
    for chunk in chunks_of(messages):
        blocks = sum(messages[at].width for at in chunk)
        for b in range(blocks):
            copies[block].wait()
            hi, lo = split(right[block])
            split_ref[pl.ds(base + b * rank, rank)] = hi
            split_ref[pl.ds(base + (blocks + b) * rank, rank)] = lo
            block += 1
        base = chunk_coefficients(split_ref, base, chunk, messages, rank, both, outs)


def first_coefficients(cols, right_tile):
    slots, rank, size = right_tile.shape
    messages = messages_of(lax.axis_size("tile"), slots)
    blocks = sum(message.width for message in messages)
    width = cols.shape[1]
    outs = [struct(message.width, rank, width) for message in messages]
    outs.append(struct(2 * blocks * rank, size, dtype=bf16))
    got = call(
        functools.partial(first_coeff_kernel, messages),
        outs,
        [in_vmem] * len(outs),
        [in_hbm, in_hbm],
        [
            pltpu.VMEM(cols.shape, f32),
            pltpu.VMEM((blocks, rank, size), f32),
            pltpu.SemaphoreType.DMA((blocks + 1,)),
        ],
        flops=8 * blocks * rank * size * width,
        moved=4 * blocks * rank * (2 * size + width),
    )(to_hbm(cols), to_hbm(right_tile))
    return got[:-1], got[-1]


def next_coeff_kernel(messages, groups, *refs):
    parts, split_ref = refs[:groups], refs[groups]
    outs, cols_ref = refs[groups + 1 : -1], refs[-1]
    part = parts[0].shape[0]
    rank = outs[0].shape[1]
    me = lax.axis_index("kern")
    for at in range(groups):
        source = partner(me, at, groups)[1]
        cols_ref[pl.ds(pl.multiple_of(source * part, part), part)] = parts[at][...]
    both = side_by_side(cols_ref[...])
    base = 0
    for chunk in chunks_of(messages):
        base = chunk_coefficients(split_ref, base, chunk, messages, rank, both, outs)


def next_coefficients(parts, split_right, slots, rank):
    messages = messages_of(lax.axis_size("tile"), slots)
    groups = len(parts)
    part, width = parts[0].shape
    size = part * groups
    total = split_right.shape[0]
    outs = [struct(message.width, rank, width) for message in messages]
    outs.append(struct(size, width))
    got = call(
        functools.partial(next_coeff_kernel, messages, groups),
        outs,
        [in_vmem] * len(outs),
        [in_vmem] * (groups + 1),
        flops=4 * total * size * width,
        moved=2 * total * (size + width),
    )(*parts, split_right)
    return got[:-1], got[-1]


def times_diag(diag_ref, cols_ref):
    both = side_by_side(cols_ref[...])
    hi, lo = split(diag_ref[...])
    return fold(dot(hi, both) + dot(lo, both))


def diag_kernel(diag_ref, cols_ref, out_ref):
    out_ref[...] = times_diag(diag_ref, cols_ref)


def diagonal(diag_tile, cols):
    size, width = cols.shape
    return call(
        diag_kernel,
        struct(size, width),
        in_vmem,
        [in_vmem, in_vmem],
        flops=8 * size * size * width,
        moved=4 * size * (size + 2 * width),
    )(diag_tile, cols)


def prepare_kernel(
    diag_ref, cols_ref, left_ref, table_ref, index_ref, diag_out, left_hi, left_lo, weights_ref
):
    diag_out[...] = times_diag(diag_ref, cols_ref)
    total = left_ref.shape[0]
    step = 128 if total % 128 == 0 else total
    for at in range(0, total, step):
        span = slice(at, at + step)
        left_hi[:, span], left_lo[:, span] = split(left_ref[span].T)
    entries = table_ref.shape[1]
    part = index_ref.shape[1]
    index = index_ref[pl.ds(lax.axis_index("kern"), 1)]
    hot = (lax.broadcasted_iota(jnp.int32, (entries, part), 0) == index).astype(f32)
    weights = jnp.dot(
        table_ref[...], hot, precision=lax.Precision.HIGHEST, preferred_element_type=f32
    )
    width = weights_ref.shape[2]
    for at in range(weights_ref.shape[0]):
        weights_ref[at] = jnp.broadcast_to(weights[at : at + 1], (width, part)).T


def prepare(diag_tile, cols, left_rows, table, index):
    size, width = cols.shape
    total = left_rows.shape[0]
    part = index.shape[1]
    return call(
        prepare_kernel,
        [
            struct(size, width),
            struct(size, total, dtype=bf16),
            struct(size, total, dtype=bf16),
            struct(table.shape[0], part, width),
        ],
        [in_vmem] * 4,
        [in_vmem] * 5,
        flops=8 * size * size * width,
        moved=8 * total * size + 4 * size * (size + 2 * width),
    )(diag_tile, cols, left_rows, table, index)


def row_kernel(messages, groups, offs_ref, ranks_ref, *refs):
    gots = refs[: len(messages)]
    hi_ref, lo_ref, diag_ref = refs[len(messages) : len(messages) + 3]
    outs, (stage, picked, term_of) = refs[len(messages) + 3 : -3], refs[-3:]
    terms = offs_ref.shape[1]
    rank, width = gots[0].shape[1:]
    slots = term_of.shape[0]
    reach = slots // 2
    for slot in range(slots):
        term_of[slot] = -1
    for k in range(terms):
        offset = offs_ref[0, k]
        term_of[jnp.where(offset < 0, offset + reach, offset + reach - 1)] = k
    me = lax.axis_index("tile")
    line = lax.broadcasted_iota(jnp.int32, (rank, width), 0)

    def pick(got, w, term):
        @pl.when(term >= 0)
        def _():
            kept = jnp.where(line < ranks_ref[0, term], got[w], 0.0)
            picked[pl.ds(pl.multiple_of(term * rank, rank), rank)] = kept

    for got, message in zip(gots, messages):
        for w, (slot, there) in enumerate(message.slots(me, False)):
            pick(got, w, jnp.where(there, term_of[slot], -1))
    both = side_by_side(picked[...])
    total = fold(dot(hi_ref[...], both) + dot(lo_ref[...], both)) + diag_ref[...]
    if groups == 1:
        outs[0][...] = total
        return
    stage[...] = total
    part = total.shape[0] // groups
    own = lax.axis_index("kern")
    for at in range(groups):
        dest = partner(own, at, groups)[0]
        outs[at][...] = stage[pl.ds(pl.multiple_of(dest * part, part), part)]


def rows(offsets, ranks, gots, left_hi, left_lo, diag_part, slots, groups):
    size, total = left_hi.shape
    width = diag_part.shape[1]
    messages = messages_of(lax.axis_size("tile"), slots)
    return call(
        functools.partial(row_kernel, messages, groups),
        [struct(size // groups, width)] * groups,
        [in_vmem] * groups,
        [in_smem, in_smem] + [in_vmem] * (len(messages) + 3),
        [
            pltpu.VMEM((size, width), f32),
            pltpu.VMEM((total, width), f32),
            pltpu.SMEM((slots,), jnp.int32),
        ],
        flops=8 * total * size * width,
        moved=4 * total * (size + width),
    )(offsets, ranks, *gots, left_hi, left_lo, diag_part)


def mix_kernel(groups, *refs):
    fields, weights_ref, outs = refs[:groups], refs[groups], refs[groups + 1 :]
    me = lax.axis_index("kern")
    for at in range(groups):
        base = partner(me, at, groups)[0] * groups
        total = None
        for b in range(groups):
            term = fields[b][...] * weights_ref[base + partner(me, b, groups)[1]]
            total = term if total is None else total + term
        outs[at][...] = total


def mix(fields, weights):
    groups = len(fields)
    part, width = fields[0].shape
    return call(
        functools.partial(mix_kernel, groups),
        [struct(part, width)] * groups,
        [in_vmem] * groups,
        [in_vmem] * (groups + 1),
        flops=2 * groups * groups * part * width,
        moved=8 * groups * part * width,
    )(*fields, weights)


def deliver(coeffs, slots):
    messages = messages_of(lax.axis_size("tile"), slots)
    return [lax.ppermute(sent, "tile", message.pairs) for sent, message in zip(coeffs, messages)]


def local(
    diag_tiles,
    left_factors,
    right_factors,
    tile_offsets,
    tile_ranks,
    mixing,
    block_index,
    rhs_field,
):
    diag_tile = diag_tiles[0, 0]
    right_tile = right_factors[0, 0]
    offsets = tile_offsets[0]
    ranks = tile_ranks[0]
    slots, rank, size = right_tile.shape
    groups = lax.axis_size("kern")
    left_rows = left_factors.reshape(-1, size)
    table = mixing.reshape(mixing.shape[0], groups * groups).T
    index = block_index.reshape(groups, size // groups)
    cols = rhs_field[0]

    coeffs, split_right = first_coefficients(cols, right_tile)
    gots = deliver(coeffs, slots)
    diag_part, left_hi, left_lo, weights = prepare(diag_tile, cols, left_rows, table, index)
    first = rows(offsets, ranks, gots, left_hi, left_lo, diag_part, slots, groups)
    mixed = exchange(mix(exchange(first, "kern"), weights), "kern")
    coeffs, cols = next_coefficients(mixed, split_right, slots, rank)
    gots = deliver(coeffs, slots)
    diag_part = diagonal(diag_tile, cols)
    return rows(offsets, ranks, gots, left_hi, left_lo, diag_part, slots, 1)[0][None]


def solution(mesh):
    in_specs = (
        P("kern", "tile", None, None),
        P("kern", "tile", None, None, None),
        P("kern", "tile", None, None, None),
        P("kern", "tile", None),
        P("kern", "tile", None),
        P(),
        P("tile"),
        P("kern", "tile", None),
    )
    out_specs = P("kern", "tile", None)
    return jax.shard_map(local, mesh=mesh, in_specs=in_specs, out_specs=out_specs, check_vma=False)
```

time: 118 us -> 58.2 us (0.49)
  waiting for transfers between devices: 61.8 us -> 22.7 us
  matrix products: 15.4 us -> 0 us
  Pallas kernels: 0 us -> 8.7 us
  blocking collectives: 8.26 us -> 0 us
  local copies, waits for them, and re-layouts: 5.6 us -> 1.33 us
    ppermute x24 -> x20, waiting for transfers between devices: 57.3 us -> 22.7 us  [the longest x14 15.3 us: deliver(): lax.ppermute(sent, 'tile', message.pairs)]
    dot_general x9 -> x0, matrix products: 14.6 us -> none  [the longest x2 4.37 us: apply_kernel(): jnp.einsum('kqp,kqc->pc', left_tile, chosen, precision=highest)]
    pallas_call x0 -> x7, Pallas kernels: none -> 8.7 us  [the longest x2 3.37 us: rows(): call(functools.partial(row_kernel, messages, groups), [struct(size // gro...]
    all_to_all x1 -> x0, blocking collectives: 8.26 us -> none  [local(): lax.all_to_all(blended, 'kern', split_axis=0, concat_axis=1, tiled=True)[0]]
    all_to_all x1 -> x0, waiting for transfers between devices: 4.45 us -> none  [local(): lax.all_to_all(first[None], 'kern', split_axis=1, concat_axis=0, tiled=True)]
    all_to_all x1 -> x0, starting transfers between devices: 3.72 us -> none  [local(): lax.all_to_all(first[None], 'kern', split_axis=1, concat_axis=0, tiled=True)]
    ppermute x24 -> x20, starting transfers between devices: 22.7 us -> 25.3 us  [the longest x14 18.1 us: deliver(): lax.ppermute(sent, 'tile', message.pairs)]
    dynamic_slice x1 -> x0, local copies, waits for them, and re-layouts: 1.34 us -> none  [local(): lax.dynamic_slice_in_dim(block_index, own_group * part_len, part_len)]
  transfers between devices with their start and end apart: 25 -> 20, of which waited for: 16 -> 13; matrix products, arithmetic and copies ran while one was open for 3% -> 0% of each run, Pallas kernels for 0% -> 2%
where the time goes in v4:
time: 58.2 us; the launch traced here: 58.1 us
  starting transfers between devices  25.3 us (43%)
  waiting for transfers between devices  22.7 us (39%)
  Pallas kernels  8.7 us (15%)
  local copies, waits for them, and re-layouts  1.33 us (2%)
    ppermute x14, starting transfers between devices, deliver(): lax.ppermute(sent, 'tile', message.pairs)  18.1 us
    ppermute x14, waiting for transfers between devices, deliver(): lax.ppermute(sent, 'tile', message.pairs)  15.3 us
    ppermute x6, waiting for transfers between devices, exchange(): arrived.append(lax.ppermute(values[step], axis, step_pairs(count, step)))  7.4 us
    ppermute x6, starting transfers between devices, exchange(): arrived.append(lax.ppermute(values[step], axis, step_pairs(count, step)))  7.11 us
    pallas_call x2, Pallas kernels, rows(): call(functools.partial(row_kernel, messages, groups), [struct(size // gro...  3.37 us
    pallas_call x1, Pallas kernels, first_coefficients(): call(functools.partial(first_coeff_kernel, messages), outs, [in_vmem] * l...  3.18 us
    unnamed x14, local copies, waits for them, and re-layouts  1.33 us
  transfers between devices with their start and end apart: 20, of which 13 were waited for; matrix products, arithmetic and copies ran while one was open for 0% of the time, Pallas kernels for 2%

profile of v4, /device:TPU:0, one launch (start us, length us, event | category | flops | bytes accessed | tf_op | source)
XLA Modules:
  0.0 58.1 jit_solution(9550707946916152113)
XLA Ops:
  0.0 3.2 %shard_map.82 = (f32[2,80,128]{2,1,0:T(8,128)S(1)}, f32[2,80,128]{2,1,0:T(8,128)S(1)}, f32[2,80,128]{2,1,0:T(8,128)S(1)}, f32[2,80,128]{2,1,0:T(8,128)S(1)}, f32...) custom-call(f32[512,128]{1,0:T(8,128)} %bitcast.14, ...), custom_call_target="tpu_custom_call" | custom-call | flops 545259520 | bytes 4792320 | tf_op jit(solution)/shard_map/pallas_call | solution.py:168
  3.2 4.6 %collective-permute-start = (f32[2,80,128]{2,1,0:T(8,128)S(1)}, f32[2,80,128]{2,1,0:T(8,128)S(1)}, u32[]{:S(2)}, u32[]{:S(2)}) collective-permute-start(f32[2,80,128]{2,1,0:T(8,128)S(1)} %get-tuple-element.33), channel_id=1, source_target_pairs={{0,7},{1,6},{2,5},{3,4},{4,3},{5,2},{6,1},{7,0},{8,15},{9,14},{10,... | collective-permute-start | bytes 245768 | tf_op jit(solution)/shard_map/ppermute | solution.py:364
  8.8 2.4 %collective-permute-start.3 = (f32[2,80,128]{2,1,0:T(8,128)S(1)}, f32[2,80,128]{2,1,0:T(8,128)S(1)}, u32[]{:S(2)}, u32[]{:S(2)}) collective-permute-start(f32[2,80,128]{2,1,0:T(8,128)S(1)} %get-tuple-element.36), channel_id=1, source_target_pairs={{0,4},{1,5},{2,6},{3,7},{4,0},{5,1},{6,2},{7,3},{8,12},{9,13},{10,... | collective-permute-start | bytes 245768 | tf_op jit(solution)/shard_map/ppermute | solution.py:364
  11.2 1.4 %collective-permute-start.4 = (f32[2,80,128]{2,1,0:T(8,128)S(1)}, f32[2,80,128]{2,1,0:T(8,128)S(1)}, u32[]{:S(2)}, u32[]{:S(2)}) collective-permute-start(f32[2,80,128]{2,1,0:T(8,128)S(1)} %get-tuple-element.37), channel_id=1, source_target_pairs={{0,3},{1,2},{2,1},{3,0},{4,7},{5,6},{6,5},{7,4},{8,11},{9,10},{10,... | collective-permute-start | bytes 245768 | tf_op jit(solution)/shard_map/ppermute | solution.py:364
  13.0 1.3 %copy-done.1 = f32[1,1,8,80,512]{4,3,2,1,0:T(8,128)S(1)} copy-done((f32[1,1,8,80,512]{4,3,2,1,0:T(8,128)S(1)}, f32[1,1,8,80,512]{4,3,2,1,0:T(8,128)}, u32[]{:S(2)}) %copy-start.1) | copy-done | bytes 1310744
  14.3 0.8 %shard_map.83 = (f32[512,128]{1,0:T(8,128)S(1)}, bf16[512,640]{1,0:T(8,128)(2,1)S(1)}, bf16[512,640]{1,0:T(8,128)(2,1)S(1)}, f32[16,128,128]{2,1,0:T(8,128)S(1)}) custom-call(f32[512,512]{1,0:T(8,128)S(1)} %bitcast.11, f32[512,128]{1,0:T(8,128)S(1)} %bitcast.15, f32[640,512]{1,0:T(8,128)S(1)} %bitcast.13, f32[16,64]{1,0:T(8,128)S(1)} %bitcast.16, ...), custom_call_target="tpu_custom_call" | custom-call | flops 268435456 | bytes 4194304 | tf_op jit(solution)/shard_map/pallas_call | solution.py:265
  15.7 5.2 %collective-permute-done.2.refs_2_ = f32[2,80,128]{2,1,0:T(8,128)S(1)} collective-permute-done((f32[2,80,128]{2,1,0:T(8,128)S(1)}, f32[2,80,128]{2,1,0:T(8,128)S(1)}, u32[]{:S(2)}, u32[]{:S(2)}) %collective-permute-start.2) | collective-permute-done | bytes 81952 | tf_op jit(solution)/shard_map/ppermute | solution.py:364
  20.9 1.9 %collective-permute-done.3.refs_3_ = f32[2,80,128]{2,1,0:T(8,128)S(1)} collective-permute-done((f32[2,80,128]{2,1,0:T(8,128)S(1)}, f32[2,80,128]{2,1,0:T(8,128)S(1)}, u32[]{:S(2)}, u32[]{:S(2)}) %collective-permute-start.3) | collective-permute-done | bytes 81952 | tf_op jit(solution)/shard_map/ppermute | solution.py:364
  22.8 1.3 %shard_map.84 = (f32[128,128]{1,0:T(8,128)S(1)}, f32[128,128]{1,0:T(8,128)S(1)}, f32[128,128]{1,0:T(8,128)S(1)}, f32[128,128]{1,0:T(8,128)S(1)}) custom-call(s32[1,8]{1,0:T(1,128)S(1)} %bitcast.18, s32[1,8]{1,0:T(1,128)S(1)} %bitcast.20, f32[2,80,128]{2,1,0:T(8,128)S(1)} %collective-permute-done.refs_0_, f32[2,80,128]{2,1,0:T(8,128)S(1)} %collective-permute-done.1.refs_1_, ...), custom_call_target="tpu_custom_call" | custom-call | flops 335544320 | bytes 1638400 | tf_op jit(solution)/shard_map/pallas_call | solution.py:322
  24.2 1.6 %collective-permute-start.7 = (f32[128,128]{1,0:T(8,128)S(1)}, f32[128,128]{1,0:T(8,128)S(1)}, u32[]{:S(2)}, u32[]{:S(2)}) collective-permute-start(f32[128,128]{1,0:T(8,128)S(1)} %get-tuple-element.44), channel_id=1, source_target_pairs={{0,8},{8,0},{16,24},{24,16},{1,9},{9,1},{17,25},{25,17},{2,10},{10... | collective-permute-start | bytes 196616 | tf_op jit(solution)/shard_map/ppermute | solution.py:72
  25.7 1.5 %collective-permute-start.8 = (f32[128,128]{1,0:T(8,128)S(1)}, f32[128,128]{1,0:T(8,128)S(1)}, u32[]{:S(2)}, u32[]{:S(2)}) collective-permute-start(f32[128,128]{1,0:T(8,128)S(1)} %get-tuple-element.45), channel_id=1, source_target_pairs={{0,16},{8,24},{16,0},{24,8},{1,17},{9,25},{17,1},{25,9},{2,18},{10... | collective-permute-start | bytes 196616 | tf_op jit(solution)/shard_map/ppermute | solution.py:72
  28.5 1.5 %collective-permute-done.8.refs_2_ = f32[128,128]{1,0:T(8,128)S(1)} collective-permute-done((f32[128,128]{1,0:T(8,128)S(1)}, f32[128,128]{1,0:T(8,128)S(1)}, u32[]{:S(2)}, u32[]{:S(2)}) %collective-permute-start.8) | collective-permute-done | bytes 65568 | tf_op jit(solution)/shard_map/ppermute | solution.py:72
  30.0 2.4 %collective-permute-done.9.refs_3_ = f32[128,128]{1,0:T(8,128)S(1)} collective-permute-done((f32[128,128]{1,0:T(8,128)S(1)}, f32[128,128]{1,0:T(8,128)S(1)}, u32[]{:S(2)}, u32[]{:S(2)}) %collective-permute-start.9) | collective-permute-done | bytes 65568 | tf_op jit(solution)/shard_map/ppermute | solution.py:72
  33.6 2.4 %collective-permute-start.12 = (f32[128,128]{1,0:T(8,128)S(1)}, f32[128,128]{1,0:T(8,128)S(1)}, u32[]{:S(2)}, u32[]{:S(2)}) collective-permute-start(f32[128,128]{1,0:T(8,128)S(1)} %get-tuple-element.51), channel_id=1, source_target_pairs={{0,24},{8,16},{16,8},{24,0},{1,25},{9,17},{17,9},{25,1},{2,26},{10... | collective-permute-start | bytes 196616 | tf_op jit(solution)/shard_map/ppermute | solution.py:72
  36.1 0.8 %collective-permute-done.10.refs_1_ = f32[128,128]{1,0:T(8,128)S(1)} collective-permute-done((f32[128,128]{1,0:T(8,128)S(1)}, f32[128,128]{1,0:T(8,128)S(1)}, u32[]{:S(2)}, u32[]{:S(2)}) %collective-permute-start.10) | collective-permute-done | bytes 65568 | tf_op jit(solution)/shard_map/ppermute | solution.py:72
  37.4 1.4 %collective-permute-done.12.refs_3_ = f32[128,128]{1,0:T(8,128)S(1)} collective-permute-done((f32[128,128]{1,0:T(8,128)S(1)}, f32[128,128]{1,0:T(8,128)S(1)}, u32[]{:S(2)}, u32[]{:S(2)}) %collective-permute-start.12) | collective-permute-done | bytes 65568 | tf_op jit(solution)/shard_map/ppermute | solution.py:72
  39.7 2.6 %collective-permute-start.19 = (f32[1,80,128]{2,1,0:T(8,128)S(1)}, f32[1,80,128]{2,1,0:T(8,128)S(1)}, u32[]{:S(2)}, u32[]{:S(2)}) collective-permute-start(f32[1,80,128]{2,1,0:T(8,128)S(1)} %get-tuple-element.59), channel_id=1, source_target_pairs={{0,1},{1,0},{2,3},{3,2},{4,5},{5,4},{6,7},{7,6},{8,9},{9,8},{10,11... | collective-permute-start | bytes 122888 | tf_op jit(solution)/shard_map/ppermute | solution.py:364
  42.2 1.3 %collective-permute-start.14 = (f32[2,80,128]{2,1,0:T(8,128)S(1)}, f32[2,80,128]{2,1,0:T(8,128)S(1)}, u32[]{:S(2)}, u32[]{:S(2)}) collective-permute-start(f32[2,80,128]{2,1,0:T(8,128)S(1)} %get-tuple-element.54), channel_id=1, source_target_pairs={{0,6},{1,7},{2,4},{3,5},{4,2},{5,3},{6,0},{7,1},{8,14},{9,15},{10,... | collective-permute-start | bytes 245768 | tf_op jit(solution)/shard_map/ppermute | solution.py:364
  43.6 2.2 %collective-permute-start.16 = (f32[2,80,128]{2,1,0:T(8,128)S(1)}, f32[2,80,128]{2,1,0:T(8,128)S(1)}, u32[]{:S(2)}, u32[]{:S(2)}) collective-permute-start(f32[2,80,128]{2,1,0:T(8,128)S(1)} %get-tuple-element.56), channel_id=1, source_target_pairs={{0,4},{1,5},{2,6},{3,7},{4,0},{5,1},{6,2},{7,3},{8,12},{9,13},{10,... | collective-permute-start | bytes 245768 | tf_op jit(solution)/shard_map/ppermute | solution.py:364
  46.4 1.6 %collective-permute-start.18 = (f32[2,80,128]{2,1,0:T(8,128)S(1)}, f32[2,80,128]{2,1,0:T(8,128)S(1)}, u32[]{:S(2)}, u32[]{:S(2)}) collective-permute-start(f32[2,80,128]{2,1,0:T(8,128)S(1)} %get-tuple-element.58), channel_id=1, source_target_pairs={{0,2},{1,3},{2,0},{3,1},{4,6},{5,7},{6,4},{7,5},{8,10},{9,11},{10,... | collective-permute-start | bytes 245768 | tf_op jit(solution)/shard_map/ppermute | solution.py:364
  48.4 1.0 %collective-permute-done.14.refs_1_ = f32[2,80,128]{2,1,0:T(8,128)S(1)} collective-permute-done((f32[2,80,128]{2,1,0:T(8,128)S(1)}, f32[2,80,128]{2,1,0:T(8,128)S(1)}, u32[]{:S(2)}, u32[]{:S(2)}) %collective-permute-start.14) | collective-permute-done | bytes 81952 | tf_op jit(solution)/shard_map/ppermute | solution.py:364
  49.5 4.3 %collective-permute-done.15.refs_2_ = f32[2,80,128]{2,1,0:T(8,128)S(1)} collective-permute-done((f32[2,80,128]{2,1,0:T(8,128)S(1)}, f32[2,80,128]{2,1,0:T(8,128)S(1)}, u32[]{:S(2)}, u32[]{:S(2)}) %collective-permute-start.15) | collective-permute-done | bytes 81952 | tf_op jit(solution)/shard_map/ppermute | solution.py:364
  53.7 1.7 %collective-permute-done.16.refs_3_ = f32[2,80,128]{2,1,0:T(8,128)S(1)} collective-permute-done((f32[2,80,128]{2,1,0:T(8,128)S(1)}, f32[2,80,128]{2,1,0:T(8,128)S(1)}, u32[]{:S(2)}, u32[]{:S(2)}) %collective-permute-start.16) | collective-permute-done | bytes 81952 | tf_op jit(solution)/shard_map/ppermute | solution.py:364
  56.1 2.0 %shard_map.88 = f32[512,128]{1,0:T(8,128)} custom-call(s32[1,8]{1,0:T(1,128)S(1)} %bitcast.19, s32[1,8]{1,0:T(1,128)S(1)} %bitcast.21, f32[2,80,128]{2,1,0:T(8,128)S(1)} %collective-permute-done.13.refs_0_, f32[2,80,128]{2,1,0:T(8,128)S(1)} %collective-permute-done.14.refs_1_, f32[2,80,128]{2,1,0:T(8,128)S(1)} %collective-permute-done.15.refs_2_, ...), custom_call_target="tpu_custom_call" | custom-call | flops 335544320 | bytes 1638400 | tf_op jit(solution)/shard_map/pallas_call | solution.py:322
  (37 shorter events, 7.4 us)
Async XLA Ops:
  0.0 13.0 %copy-start.3 = (f32[64,4,4]{0,2,1:T(4,128)S(1)}, f32[64,4,4]{0,2,1:T(4,128)}, u32[]{:S(2)}) copy-start(f32[64,4,4]{0,2,1:T(4,128)} %param.13) | copy-start | bytes 12292
  0.0 13.0 %copy-start = (f32[1,1,512,512]{3,2,1,0:T(8,128)S(1)}, f32[1,1,512,512]{3,2,1,0:T(8,128)}, u32[]{:S(2)}) copy-start(f32[1,1,512,512]{3,2,1,0:T(8,128)} %param.8) | copy-start | bytes 3145732
  0.0 22.8 %copy-start.5 = (s32[1,1,8]{2,1,0:T(1,128)S(1)}, s32[1,1,8]{2,1,0:T(1,128)}, u32[]{:S(2)}) copy-start(s32[1,1,8]{2,1,0:T(1,128)} %param.11) | copy-start | bytes 100
  0.0 22.8 %copy-start.6 = (s32[1,1,8]{2,1,0:T(1,128)S(1)}, s32[1,1,8]{2,1,0:T(1,128)}, u32[]{:S(2)}) copy-start(s32[1,1,8]{2,1,0:T(1,128)} %param.12) | copy-start | bytes 100
  3.2 9.4 %collective-permute-start = (f32[2,80,128]{2,1,0:T(8,128)S(1)}, f32[2,80,128]{2,1,0:T(8,128)S(1)}, u32[]{:S(2)}, u32[]{:S(2)}) collective-permute-start(f32[2,80,128]{2,1,0:T(8,128)S(1)} %get-tuple-element.33), channel_id=1, source_target_pairs={{0,7},{1,6},{2,5},{3,4},{4,3},{5,2},{6,1},{7,0},{8,15},{9,14},{10,... | collective-permute-start | bytes 245768 | tf_op jit(solution)/shard_map/ppermute | solution.py:364
  7.8 3.4 %collective-permute-start.6 = (f32[1,80,128]{2,1,0:T(8,128)S(1)}, f32[1,80,128]{2,1,0:T(8,128)S(1)}, u32[]{:S(2)}, u32[]{:S(2)}) collective-permute-start(f32[1,80,128]{2,1,0:T(8,128)S(1)} %get-tuple-element.39), channel_id=1, source_target_pairs={{0,1},{1,0},{2,3},{3,2},{4,5},{5,4},{6,7},{7,6},{8,9},{9,8},{10,11... | collective-permute-start | bytes 122888 | tf_op jit(solution)/shard_map/ppermute | solution.py:364
  8.5 7.2 %collective-permute-start.1 = (f32[2,80,128]{2,1,0:T(8,128)S(1)}, f32[2,80,128]{2,1,0:T(8,128)S(1)}, u32[]{:S(2)}, u32[]{:S(2)}) collective-permute-start(f32[2,80,128]{2,1,0:T(8,128)S(1)} %get-tuple-element.34), channel_id=1, source_target_pairs={{0,6},{1,7},{2,4},{3,5},{4,2},{5,3},{6,0},{7,1},{8,14},{9,15},{10,... | collective-permute-start | bytes 245768 | tf_op jit(solution)/shard_map/ppermute | solution.py:364
  8.5 12.4 %collective-permute-start.2 = (f32[2,80,128]{2,1,0:T(8,128)S(1)}, f32[2,80,128]{2,1,0:T(8,128)S(1)}, u32[]{:S(2)}, u32[]{:S(2)}) collective-permute-start(f32[2,80,128]{2,1,0:T(8,128)S(1)} %get-tuple-element.35), channel_id=1, source_target_pairs={{0,5},{1,4},{2,7},{3,6},{4,1},{5,0},{6,3},{7,2},{8,13},{9,12},{10,... | collective-permute-start | bytes 245768 | tf_op jit(solution)/shard_map/ppermute | solution.py:364
  8.8 14.0 %collective-permute-start.3 = (f32[2,80,128]{2,1,0:T(8,128)S(1)}, f32[2,80,128]{2,1,0:T(8,128)S(1)}, u32[]{:S(2)}, u32[]{:S(2)}) collective-permute-start(f32[2,80,128]{2,1,0:T(8,128)S(1)} %get-tuple-element.36), channel_id=1, source_target_pairs={{0,4},{1,5},{2,6},{3,7},{4,0},{5,1},{6,2},{7,3},{8,12},{9,13},{10,... | collective-permute-start | bytes 245768 | tf_op jit(solution)/shard_map/ppermute | solution.py:364
  11.2 11.6 %collective-permute-start.4 = (f32[2,80,128]{2,1,0:T(8,128)S(1)}, f32[2,80,128]{2,1,0:T(8,128)S(1)}, u32[]{:S(2)}, u32[]{:S(2)}) collective-permute-start(f32[2,80,128]{2,1,0:T(8,128)S(1)} %get-tuple-element.37), channel_id=1, source_target_pairs={{0,3},{1,2},{2,1},{3,0},{4,7},{5,6},{6,5},{7,4},{8,11},{9,10},{10,... | collective-permute-start | bytes 245768 | tf_op jit(solution)/shard_map/ppermute | solution.py:364
  12.6 10.2 %collective-permute-start.5 = (f32[2,80,128]{2,1,0:T(8,128)S(1)}, f32[2,80,128]{2,1,0:T(8,128)S(1)}, u32[]{:S(2)}, u32[]{:S(2)}) collective-permute-start(f32[2,80,128]{2,1,0:T(8,128)S(1)} %get-tuple-element.38), channel_id=1, source_target_pairs={{0,2},{1,3},{2,0},{3,1},{4,6},{5,7},{6,4},{7,5},{8,10},{9,11},{10,... | collective-permute-start | bytes 245768 | tf_op jit(solution)/shard_map/ppermute | solution.py:364
  24.2 4.3 %collective-permute-start.7 = (f32[128,128]{1,0:T(8,128)S(1)}, f32[128,128]{1,0:T(8,128)S(1)}, u32[]{:S(2)}, u32[]{:S(2)}) collective-permute-start(f32[128,128]{1,0:T(8,128)S(1)} %get-tuple-element.44), channel_id=1, source_target_pairs={{0,8},{8,0},{16,24},{24,16},{1,9},{9,1},{17,25},{25,17},{2,10},{10... | collective-permute-start | bytes 196616 | tf_op jit(solution)/shard_map/ppermute | solution.py:72
  25.7 4.3 %collective-permute-start.8 = (f32[128,128]{1,0:T(8,128)S(1)}, f32[128,128]{1,0:T(8,128)S(1)}, u32[]{:S(2)}, u32[]{:S(2)}) collective-permute-start(f32[128,128]{1,0:T(8,128)S(1)} %get-tuple-element.45), channel_id=1, source_target_pairs={{0,16},{8,24},{16,0},{24,8},{1,17},{9,25},{17,1},{25,9},{2,18},{10... | collective-permute-start | bytes 196616 | tf_op jit(solution)/shard_map/ppermute | solution.py:72
  27.2 5.2 %collective-permute-start.9 = (f32[128,128]{1,0:T(8,128)S(1)}, f32[128,128]{1,0:T(8,128)S(1)}, u32[]{:S(2)}, u32[]{:S(2)}) collective-permute-start(f32[128,128]{1,0:T(8,128)S(1)} %get-tuple-element.46), channel_id=1, source_target_pairs={{0,24},{8,16},{16,8},{24,0},{1,25},{9,17},{17,9},{25,1},{2,26},{10... | collective-permute-start | bytes 196616 | tf_op jit(solution)/shard_map/ppermute | solution.py:72
  32.5 4.3 %collective-permute-start.10 = (f32[128,128]{1,0:T(8,128)S(1)}, f32[128,128]{1,0:T(8,128)S(1)}, u32[]{:S(2)}, u32[]{:S(2)}) collective-permute-start(f32[128,128]{1,0:T(8,128)S(1)} %get-tuple-element.49), channel_id=1, source_target_pairs={{0,8},{8,0},{16,24},{24,16},{1,9},{9,1},{17,25},{25,17},{2,10},{10... | collective-permute-start | bytes 196616 | tf_op jit(solution)/shard_map/ppermute | solution.py:72
  33.1 4.3 %collective-permute-start.11 = (f32[128,128]{1,0:T(8,128)S(1)}, f32[128,128]{1,0:T(8,128)S(1)}, u32[]{:S(2)}, u32[]{:S(2)}) collective-permute-start(f32[128,128]{1,0:T(8,128)S(1)} %get-tuple-element.50), channel_id=1, source_target_pairs={{0,16},{8,24},{16,0},{24,8},{1,17},{9,25},{17,1},{25,9},{2,18},{10... | collective-permute-start | bytes 196616 | tf_op jit(solution)/shard_map/ppermute | solution.py:72
  33.6 5.2 %collective-permute-start.12 = (f32[128,128]{1,0:T(8,128)S(1)}, f32[128,128]{1,0:T(8,128)S(1)}, u32[]{:S(2)}, u32[]{:S(2)}) collective-permute-start(f32[128,128]{1,0:T(8,128)S(1)} %get-tuple-element.51), channel_id=1, source_target_pairs={{0,24},{8,16},{16,8},{24,0},{1,25},{9,17},{17,9},{25,1},{2,26},{10... | collective-permute-start | bytes 196616 | tf_op jit(solution)/shard_map/ppermute | solution.py:72
  39.6 6.8 %collective-permute-start.13 = (f32[2,80,128]{2,1,0:T(8,128)S(1)}, f32[2,80,128]{2,1,0:T(8,128)S(1)}, u32[]{:S(2)}, u32[]{:S(2)}) collective-permute-start(f32[2,80,128]{2,1,0:T(8,128)S(1)} %get-tuple-element.53), channel_id=1, source_target_pairs={{0,7},{1,6},{2,5},{3,4},{4,3},{5,2},{6,1},{7,0},{8,15},{9,14},{10,... | collective-permute-start | bytes 245768 | tf_op jit(solution)/shard_map/ppermute | solution.py:364
  39.7 6.2 %collective-permute-start.19 = (f32[1,80,128]{2,1,0:T(8,128)S(1)}, f32[1,80,128]{2,1,0:T(8,128)S(1)}, u32[]{:S(2)}, u32[]{:S(2)}) collective-permute-start(f32[1,80,128]{2,1,0:T(8,128)S(1)} %get-tuple-element.59), channel_id=1, source_target_pairs={{0,1},{1,0},{2,3},{3,2},{4,5},{5,4},{6,7},{7,6},{8,9},{9,8},{10,11... | collective-permute-start | bytes 122888 | tf_op jit(solution)/shard_map/ppermute | solution.py:364
  42.2 7.2 %collective-permute-start.14 = (f32[2,80,128]{2,1,0:T(8,128)S(1)}, f32[2,80,128]{2,1,0:T(8,128)S(1)}, u32[]{:S(2)}, u32[]{:S(2)}) collective-permute-start(f32[2,80,128]{2,1,0:T(8,128)S(1)} %get-tuple-element.54), channel_id=1, source_target_pairs={{0,6},{1,7},{2,4},{3,5},{4,2},{5,3},{6,0},{7,1},{8,14},{9,15},{10,... | collective-permute-start | bytes 245768 | tf_op jit(solution)/shard_map/ppermute | solution.py:364
  43.6 10.2 %collective-permute-start.15 = (f32[2,80,128]{2,1,0:T(8,128)S(1)}, f32[2,80,128]{2,1,0:T(8,128)S(1)}, u32[]{:S(2)}, u32[]{:S(2)}) collective-permute-start(f32[2,80,128]{2,1,0:T(8,128)S(1)} %get-tuple-element.55), channel_id=1, source_target_pairs={{0,5},{1,4},{2,7},{3,6},{4,1},{5,0},{6,3},{7,2},{8,13},{9,12},{10,... | collective-permute-start | bytes 245768 | tf_op jit(solution)/shard_map/ppermute | solution.py:364
  43.6 11.9 %collective-permute-start.16 = (f32[2,80,128]{2,1,0:T(8,128)S(1)}, f32[2,80,128]{2,1,0:T(8,128)S(1)}, u32[]{:S(2)}, u32[]{:S(2)}) collective-permute-start(f32[2,80,128]{2,1,0:T(8,128)S(1)} %get-tuple-element.56), channel_id=1, source_target_pairs={{0,4},{1,5},{2,6},{3,7},{4,0},{5,1},{6,2},{7,3},{8,12},{9,13},{10,... | collective-permute-start | bytes 245768 | tf_op jit(solution)/shard_map/ppermute | solution.py:364
  45.8 9.7 %collective-permute-start.17 = (f32[2,80,128]{2,1,0:T(8,128)S(1)}, f32[2,80,128]{2,1,0:T(8,128)S(1)}, u32[]{:S(2)}, u32[]{:S(2)}) collective-permute-start(f32[2,80,128]{2,1,0:T(8,128)S(1)} %get-tuple-element.57), channel_id=1, source_target_pairs={{0,3},{1,2},{2,1},{3,0},{4,7},{5,6},{6,5},{7,4},{8,11},{9,10},{10,... | collective-permute-start | bytes 245768 | tf_op jit(solution)/shard_map/ppermute | solution.py:364
  46.4 9.7 %collective-permute-start.18 = (f32[2,80,128]{2,1,0:T(8,128)S(1)}, f32[2,80,128]{2,1,0:T(8,128)S(1)}, u32[]{:S(2)}, u32[]{:S(2)}) collective-permute-start(f32[2,80,128]{2,1,0:T(8,128)S(1)} %get-tuple-element.58), channel_id=1, source_target_pairs={{0,2},{1,3},{2,0},{3,1},{4,6},{5,7},{6,4},{7,5},{8,10},{9,11},{10,... | collective-permute-start | bytes 245768 | tf_op jit(solution)/shard_map/ppermute | solution.py:364
  (3 other events, 27.3 us)

commit v5 on v4

--- a/solution.py
+++ b/solution.py
@@ -63,14 +63,6 @@
     if count & (count - 1) == 0:
         return me ^ step, me ^ step
     return lax.rem(me + step, count), lax.rem(me + count - step, count)
-
-
-def exchange(values, axis):
-    count = lax.axis_size(axis)
-    arrived = [values[0]]
-    for step in range(1, count):
-        arrived.append(lax.ppermute(values[step], axis, step_pairs(count, step)))
-    return arrived
 
 
 class Message:
@@ -181,37 +173,33 @@
     return got[:-1], got[-1]
 
 
-def next_coeff_kernel(messages, groups, *refs):
-    parts, split_ref = refs[:groups], refs[groups]
-    outs, cols_ref = refs[groups + 1 : -1], refs[-1]
-    part = parts[0].shape[0]
+def next_coeff_kernel(messages, fields_ref, weights_ref, split_ref, *refs):
+    outs, cols_ref = refs[:-1], refs[-1]
     rank = outs[0].shape[1]
-    me = lax.axis_index("kern")
-    for at in range(groups):
-        source = partner(me, at, groups)[1]
-        cols_ref[pl.ds(pl.multiple_of(source * part, part), part)] = parts[at][...]
-    both = side_by_side(cols_ref[...])
+    mixed = fields_ref[0] * weights_ref[0]
+    for b in range(1, fields_ref.shape[0]):
+        mixed = mixed + fields_ref[b] * weights_ref[b]
+    cols_ref[...] = mixed
+    both = side_by_side(mixed)
     base = 0
     for chunk in chunks_of(messages):
         base = chunk_coefficients(split_ref, base, chunk, messages, rank, both, outs)
 
 
-def next_coefficients(parts, split_right, slots, rank):
+def next_coefficients(fields, weights, split_right, slots, rank):
     messages = messages_of(lax.axis_size("tile"), slots)
-    groups = len(parts)
-    part, width = parts[0].shape
-    size = part * groups
+    _, size, width = fields.shape
     total = split_right.shape[0]
     outs = [struct(message.width, rank, width) for message in messages]
     outs.append(struct(size, width))
     got = call(
-        functools.partial(next_coeff_kernel, messages, groups),
+        functools.partial(next_coeff_kernel, messages),
         outs,
         [in_vmem] * len(outs),
-        [in_vmem] * (groups + 1),
+        [in_vmem] * 3,
         flops=4 * total * size * width,
         moved=2 * total * (size + width),
-    )(*parts, split_right)
+    )(fields, weights, split_right)
     return got[:-1], got[-1]
 
 
@@ -246,29 +234,26 @@
     for at in range(0, total, step):
         span = slice(at, at + step)
         left_hi[:, span], left_lo[:, span] = split(left_ref[span].T)
-    entries = table_ref.shape[1]
-    part = index_ref.shape[1]
-    index = index_ref[pl.ds(lax.axis_index("kern"), 1)]
-    hot = (lax.broadcasted_iota(jnp.int32, (entries, part), 0) == index).astype(f32)
-    weights = jnp.dot(
-        table_ref[...], hot, precision=lax.Precision.HIGHEST, preferred_element_type=f32
-    )
+    own = table_ref[lax.axis_index("kern")]
+    groups, entries = own.shape
+    size = index_ref.shape[1]
+    hot = (lax.broadcasted_iota(jnp.int32, (entries, size), 0) == index_ref[...]).astype(f32)
+    weights = jnp.dot(own, hot, precision=lax.Precision.HIGHEST, preferred_element_type=f32)
     width = weights_ref.shape[2]
-    for at in range(weights_ref.shape[0]):
-        weights_ref[at] = jnp.broadcast_to(weights[at : at + 1], (width, part)).T
+    for b in range(groups):
+        weights_ref[b] = jnp.broadcast_to(weights[b : b + 1], (width, size)).T
 
 
 def prepare(diag_tile, cols, left_rows, table, index):
     size, width = cols.shape
     total = left_rows.shape[0]
-    part = index.shape[1]
     return call(
         prepare_kernel,
         [
             struct(size, width),
             struct(size, total, dtype=bf16),
             struct(size, total, dtype=bf16),
-            struct(table.shape[0], part, width),
+            struct(table.shape[0], size, width),
         ],
         [in_vmem] * 4,
         [in_vmem] * 5,
@@ -277,10 +262,10 @@
     )(diag_tile, cols, left_rows, table, index)
 
 
-def row_kernel(messages, groups, offs_ref, ranks_ref, *refs):
+def row_kernel(messages, offs_ref, ranks_ref, *refs):
     gots = refs[: len(messages)]
     hi_ref, lo_ref, diag_ref = refs[len(messages) : len(messages) + 3]
-    outs, (stage, picked, term_of) = refs[len(messages) + 3 : -3], refs[-3:]
+    out_ref, picked, term_of = refs[-3:]
     terms = offs_ref.shape[1]
     rank, width = gots[0].shape[1:]
     slots = term_of.shape[0]
@@ -303,60 +288,25 @@
         for w, (slot, there) in enumerate(message.slots(me, False)):
             pick(got, w, jnp.where(there, term_of[slot], -1))
     both = side_by_side(picked[...])
-    total = fold(dot(hi_ref[...], both) + dot(lo_ref[...], both)) + diag_ref[...]
-    if groups == 1:
-        outs[0][...] = total
-        return
-    stage[...] = total
-    part = total.shape[0] // groups
-    own = lax.axis_index("kern")
-    for at in range(groups):
-        dest = partner(own, at, groups)[0]
-        outs[at][...] = stage[pl.ds(pl.multiple_of(dest * part, part), part)]
-
-
-def rows(offsets, ranks, gots, left_hi, left_lo, diag_part, slots, groups):
+    out_ref[...] = fold(dot(hi_ref[...], both) + dot(lo_ref[...], both)) + diag_ref[...]
+
+
+def rows(offsets, ranks, gots, left_hi, left_lo, diag_part, slots):
     size, total = left_hi.shape
     width = diag_part.shape[1]
     messages = messages_of(lax.axis_size("tile"), slots)
     return call(
-        functools.partial(row_kernel, messages, groups),
-        [struct(size // groups, width)] * groups,
-        [in_vmem] * groups,
+        functools.partial(row_kernel, messages),
+        struct(size, width),
+        in_vmem,
         [in_smem, in_smem] + [in_vmem] * (len(messages) + 3),
         [
-            pltpu.VMEM((size, width), f32),
             pltpu.VMEM((total, width), f32),
             pltpu.SMEM((slots,), jnp.int32),
         ],
         flops=8 * total * size * width,
         moved=4 * total * (size + width),
     )(offsets, ranks, *gots, left_hi, left_lo, diag_part)
-
-
-def mix_kernel(groups, *refs):
-    fields, weights_ref, outs = refs[:groups], refs[groups], refs[groups + 1 :]
-    me = lax.axis_index("kern")
-    for at in range(groups):
-        base = partner(me, at, groups)[0] * groups
-        total = None
-        for b in range(groups):
-            term = fields[b][...] * weights_ref[base + partner(me, b, groups)[1]]
-            total = term if total is None else total + term
-        outs[at][...] = total
-
-
-def mix(fields, weights):
-    groups = len(fields)
-    part, width = fields[0].shape
-    return call(
-        functools.partial(mix_kernel, groups),
-        [struct(part, width)] * groups,
-        [in_vmem] * groups,
-        [in_vmem] * (groups + 1),
-        flops=2 * groups * groups * part * width,
-        moved=8 * groups * part * width,
-    )(*fields, weights)
 
 
 def deliver(coeffs, slots):
@@ -379,21 +329,20 @@
     offsets = tile_offsets[0]
     ranks = tile_ranks[0]
     slots, rank, size = right_tile.shape
-    groups = lax.axis_size("kern")
     left_rows = left_factors.reshape(-1, size)
-    table = mixing.reshape(mixing.shape[0], groups * groups).T
-    index = block_index.reshape(groups, size // groups)
+    table = mixing.transpose(1, 2, 0)
+    index = block_index[None]
     cols = rhs_field[0]
 
     coeffs, split_right = first_coefficients(cols, right_tile)
     gots = deliver(coeffs, slots)
     diag_part, left_hi, left_lo, weights = prepare(diag_tile, cols, left_rows, table, index)
-    first = rows(offsets, ranks, gots, left_hi, left_lo, diag_part, slots, groups)
-    mixed = exchange(mix(exchange(first, "kern"), weights), "kern")
-    coeffs, cols = next_coefficients(mixed, split_right, slots, rank)
+    first = rows(offsets, ranks, gots, left_hi, left_lo, diag_part, slots)
+    fields = lax.all_gather(first, "kern")
+    coeffs, cols = next_coefficients(fields, weights, split_right, slots, rank)
     gots = deliver(coeffs, slots)
     diag_part = diagonal(diag_tile, cols)
-    return rows(offsets, ranks, gots, left_hi, left_lo, diag_part, slots, 1)[0][None]
+    return rows(offsets, ranks, gots, left_hi, left_lo, diag_part, slots)[None]
 
 
 def solution(mesh):

time: 58.2 us -> 90.3 us (1.55)
  waiting for transfers between devices: 22.7 us -> 42.8 us
  between operations: 0.1 us -> 13.5 us
  starting transfers between devices: 25.3 us -> 18.1 us
  local copies, waits for them, and re-layouts: 1.33 us -> 6.48 us
    all_gather x0 -> x1, waiting for transfers between devices: none -> 26.9 us  [local(): fields = lax.all_gather(first, 'kern')]
    ppermute x6 -> x0, waiting for transfers between devices: 7.4 us -> none  [exchange(): arrived.append(lax.ppermute(values[step], axis, step_pairs(count, step)))]
    ppermute x6 -> x0, starting transfers between devices: 7.11 us -> none  [exchange(): arrived.append(lax.ppermute(values[step], axis, step_pairs(count, step)))]
    unnamed x14 -> x24, local copies, waits for them, and re-layouts: 1.33 us -> 6.48 us
    pallas_call x4 -> x3, Pallas kernels: 4.25 us -> 4.81 us  [the longest x2 4.04 us: rows(): call(functools.partial(row_kernel, messages), struct(size, width), in_vme...]
  transfers between devices with their start and end apart: 20 -> 15, of which waited for: 13 -> 6; matrix products, arithmetic and copies ran while one was open for 0% -> 0% of each run, Pallas kernels for 2% -> 1%
where the time goes in v5:
time: 90.3 us; the launch traced here: 90.1 us
  waiting for transfers between devices  42.8 us (47%)
  starting transfers between devices  18.1 us (20%)
  between operations  13.5 us (15%)
  Pallas kernels  9.24 us (10%)
  local copies, waits for them, and re-layouts  6.48 us (7%)
    all_gather x1, waiting for transfers between devices, local(): fields = lax.all_gather(first, 'kern')  26.9 us
    ppermute x14, starting transfers between devices, deliver(): lax.ppermute(sent, 'tile', message.pairs)  18.1 us
    ppermute x14, waiting for transfers between devices, deliver(): lax.ppermute(sent, 'tile', message.pairs)  15.9 us
    unnamed x24, local copies, waits for them, and re-layouts  6.48 us
    pallas_call x2, Pallas kernels, rows(): call(functools.partial(row_kernel, messages), struct(size, width), in_vme...  4.04 us
    pallas_call x1, Pallas kernels, first_coefficients(): call(functools.partial(first_coeff_kernel, messages), outs, [in_vmem] * l...  3.16 us
  transfers between devices with their start and end apart: 15, of which 6 were waited for; matrix products, arithmetic and copies ran while one was open for 0% of the time, Pallas kernels for 1%

profile of v5, /device:TPU:0, one launch (start us, length us, event | category | flops | bytes accessed | tf_op | source)
XLA Modules:
  0.0 90.1 jit_solution(10703794020003483881)
XLA Ops:
  6.6 3.2 %shard_map.82 = (f32[2,80,128]{2,1,0:T(8,128)S(1)}, f32[2,80,128]{2,1,0:T(8,128)S(1)}, f32[2,80,128]{2,1,0:T(8,128)S(1)}, f32[2,80,128]{2,1,0:T(8,128)S(1)}, f32...) custom-call(f32[512,128]{1,0:T(8,128)} %bitcast.13, ...), custom_call_target="tpu_custom_call" | custom-call | flops 545259520 | bytes 4792320 | tf_op jit(solution)/shard_map/pallas_call | solution.py:160
  9.8 1.4 %copy-done.1 = bf16[2080,512]{1,0:T(8,128)(2,1)} copy-done((bf16[2080,512]{1,0:T(8,128)(2,1)}, bf16[2080,512]{1,0:T(8,128)(2,1)S(1)}, u32[]{:S(2)}) %copy-start.1) | copy-done | bytes 2129944
  11.1 4.6 %collective-permute-start = (f32[2,80,128]{2,1,0:T(8,128)S(1)}, f32[2,80,128]{2,1,0:T(8,128)S(1)}, u32[]{:S(2)}, u32[]{:S(2)}) collective-permute-start(f32[2,80,128]{2,1,0:T(8,128)S(1)} %get-tuple-element.25), channel_id=1, source_target_pairs={{0,7},{1,6},{2,5},{3,4},{4,3},{5,2},{6,1},{7,0},{8,15},{9,14},{10,... | collective-permute-start | bytes 245768 | tf_op jit(solution)/shard_map/ppermute | solution.py:314
  16.7 2.3 %collective-permute-start.3 = (f32[2,80,128]{2,1,0:T(8,128)S(1)}, f32[2,80,128]{2,1,0:T(8,128)S(1)}, u32[]{:S(2)}, u32[]{:S(2)}) collective-permute-start(f32[2,80,128]{2,1,0:T(8,128)S(1)} %get-tuple-element.28), channel_id=1, source_target_pairs={{0,4},{1,5},{2,6},{3,7},{4,0},{5,1},{6,2},{7,3},{8,12},{9,13},{10,... | collective-permute-start | bytes 245768 | tf_op jit(solution)/shard_map/ppermute | solution.py:314
  19.0 1.5 %collective-permute-start.4 = (f32[2,80,128]{2,1,0:T(8,128)S(1)}, f32[2,80,128]{2,1,0:T(8,128)S(1)}, u32[]{:S(2)}, u32[]{:S(2)}) collective-permute-start(f32[2,80,128]{2,1,0:T(8,128)S(1)} %get-tuple-element.29), channel_id=1, source_target_pairs={{0,3},{1,2},{2,1},{3,0},{4,7},{5,6},{6,5},{7,4},{8,11},{9,10},{10,... | collective-permute-start | bytes 245768 | tf_op jit(solution)/shard_map/ppermute | solution.py:314
  20.8 1.3 %copy-done.3 = f32[1,1,8,80,512]{4,3,2,1,0:T(8,128)S(1)} copy-done((f32[1,1,8,80,512]{4,3,2,1,0:T(8,128)S(1)}, f32[1,1,8,80,512]{4,3,2,1,0:T(8,128)}, u32[]{:S(2)}) %copy-start.3) | copy-done | bytes 1310744
  22.1 0.8 shard_map.83
  23.0 1.0 %copy-done.5 = f32[4,512,128]{2,1,0:T(8,128)} copy-done((f32[4,512,128]{2,1,0:T(8,128)}, f32[4,512,128]{2,1,0:T(8,128)S(1)}, u32[]{:S(2)}) %copy-start.5) | copy-done | bytes 1048600
  23.9 4.8 %collective-permute-done.2.refs_2_ = f32[2,80,128]{2,1,0:T(8,128)S(1)} collective-permute-done((f32[2,80,128]{2,1,0:T(8,128)S(1)}, f32[2,80,128]{2,1,0:T(8,128)S(1)}, u32[]{:S(2)}, u32[]{:S(2)}) %collective-permute-start.2) | collective-permute-done | bytes 81952 | tf_op jit(solution)/shard_map/ppermute | solution.py:314
  28.8 1.9 %collective-permute-done.3.refs_3_ = f32[2,80,128]{2,1,0:T(8,128)S(1)} collective-permute-done((f32[2,80,128]{2,1,0:T(8,128)S(1)}, f32[2,80,128]{2,1,0:T(8,128)S(1)}, u32[]{:S(2)}, u32[]{:S(2)}) %collective-permute-start.3) | collective-permute-done | bytes 81952 | tf_op jit(solution)/shard_map/ppermute | solution.py:314
  30.7 2.0 %shard_map.84 = f32[512,128]{1,0:T(8,128)} custom-call(s32[1,8]{1,0:T(1,128)S(1)} %bitcast.17, s32[1,8]{1,0:T(1,128)S(1)} %bitcast.19, f32[2,80,128]{2,1,0:T(8,128)S(1)} %collective-permute-done.refs_0_, f32[2,80,128]{2,1,0:T(8,128)S(1)} %collective-permute-done.1.refs_1_, f32[2,80,128]{2,1,0:T(8,128)S(1)} %collective-permute-done.2.refs_2_, ...), custom_call_target="tpu_custom_call" | custom-call | flops 335544320 | bytes 1638400 | tf_op jit(solution)/shard_map/pallas_call | solution.py:298
  32.7 26.9 %all-gather.3.cloned.1.call-done = f32[2048,128]{1,0:T(8,128)} async-done(((f32[512,128]{1,0:T(8,128)}), f32[2048,128]{1,0:T(8,128)}) %all-gather.3.cloned.1.call-update) | async-done | bytes 1048592 | tf_op jit(solution)/shard_map/all_gather | solution.py:341
  59.6 1.6 %copy-done.2 = bf16[2080,512]{1,0:T(8,128)(2,1)S(1)} copy-done((bf16[2080,512]{1,0:T(8,128)(2,1)S(1)}, bf16[2080,512]{1,0:T(8,128)(2,1)}, u32[]{:S(2)}) %copy-start.2) | copy-done | bytes 2129944
  61.2 1.2 %copy-done.7 = f32[2048,128]{1,0:T(8,128)S(1)} copy-done((f32[2048,128]{1,0:T(8,128)S(1)}, f32[2048,128]{1,0:T(8,128)}, u32[]{:S(2)}) %copy-start.7) | copy-done | bytes 1048600
  62.4 0.8 shard_map.85
  63.2 2.8 %collective-permute-start.7 = (f32[2,80,128]{2,1,0:T(8,128)S(1)}, f32[2,80,128]{2,1,0:T(8,128)S(1)}, u32[]{:S(2)}, u32[]{:S(2)}) collective-permute-start(f32[2,80,128]{2,1,0:T(8,128)S(1)} %get-tuple-element.37), channel_id=1, source_target_pairs={{0,7},{1,6},{2,5},{3,4},{4,3},{5,2},{6,1},{7,0},{8,15},{9,14},{10,... | collective-permute-start | bytes 245768 | tf_op jit(solution)/shard_map/ppermute | solution.py:314
  66.0 0.7 collective-permute-start.13
  67.2 2.2 %collective-permute-start.10 = (f32[2,80,128]{2,1,0:T(8,128)S(1)}, f32[2,80,128]{2,1,0:T(8,128)S(1)}, u32[]{:S(2)}, u32[]{:S(2)}) collective-permute-start(f32[2,80,128]{2,1,0:T(8,128)S(1)} %get-tuple-element.40), channel_id=1, source_target_pairs={{0,4},{1,5},{2,6},{3,7},{4,0},{5,1},{6,2},{7,3},{8,12},{9,13},{10,... | collective-permute-start | bytes 245768 | tf_op jit(solution)/shard_map/ppermute | solution.py:314
  69.5 1.4 %collective-permute-start.11 = (f32[2,80,128]{2,1,0:T(8,128)S(1)}, f32[2,80,128]{2,1,0:T(8,128)S(1)}, u32[]{:S(2)}, u32[]{:S(2)}) collective-permute-start(f32[2,80,128]{2,1,0:T(8,128)S(1)} %get-tuple-element.41), channel_id=1, source_target_pairs={{0,3},{1,2},{2,1},{3,0},{4,7},{5,6},{6,5},{7,4},{8,11},{9,10},{10,... | collective-permute-start | bytes 245768 | tf_op jit(solution)/shard_map/ppermute | solution.py:314
  70.8 0.8 collective-permute-start.12
  72.1 1.9 %collective-permute-done.8.refs_1_ = f32[2,80,128]{2,1,0:T(8,128)S(1)} collective-permute-done((f32[2,80,128]{2,1,0:T(8,128)S(1)}, f32[2,80,128]{2,1,0:T(8,128)S(1)}, u32[]{:S(2)}, u32[]{:S(2)}) %collective-permute-start.8) | collective-permute-done | bytes 81952 | tf_op jit(solution)/shard_map/ppermute | solution.py:314
  74.0 5.5 %collective-permute-done.9.refs_2_ = f32[2,80,128]{2,1,0:T(8,128)S(1)} collective-permute-done((f32[2,80,128]{2,1,0:T(8,128)S(1)}, f32[2,80,128]{2,1,0:T(8,128)S(1)}, u32[]{:S(2)}, u32[]{:S(2)}) %collective-permute-start.9) | collective-permute-done | bytes 81952 | tf_op jit(solution)/shard_map/ppermute | solution.py:314
  79.4 1.8 %collective-permute-done.10.refs_3_ = f32[2,80,128]{2,1,0:T(8,128)S(1)} collective-permute-done((f32[2,80,128]{2,1,0:T(8,128)S(1)}, f32[2,80,128]{2,1,0:T(8,128)S(1)}, u32[]{:S(2)}, u32[]{:S(2)}) %collective-permute-start.10) | collective-permute-done | bytes 81952 | tf_op jit(solution)/shard_map/ppermute | solution.py:314
  81.2 2.0 %shard_map.87 = f32[512,128]{1,0:T(8,128)} custom-call(s32[1,8]{1,0:T(1,128)S(1)} %bitcast.18, s32[1,8]{1,0:T(1,128)S(1)} %bitcast.20, f32[2,80,128]{2,1,0:T(8,128)S(1)} %collective-permute-done.7.refs_0_, f32[2,80,128]{2,1,0:T(8,128)S(1)} %collective-permute-done.8.refs_1_, f32[2,80,128]{2,1,0:T(8,128)S(1)} %collective-permute-done.9.refs_2_, ...), custom_call_target="tpu_custom_call" | custom-call | flops 335544320 | bytes 1638400 | tf_op jit(solution)/shard_map/pallas_call | solution.py:298
  (37 shorter events, 2.4 us)
Async XLA Ops:
  6.5 14.3 %copy-start.4 = (f32[1,512,128]{2,1,0:T(8,128)S(1)}, f32[1,512,128]{2,1,0:T(8,128)}, u32[]{:S(2)}) copy-start(f32[1,512,128]{2,1,0:T(8,128)} %param.15) | copy-start | bytes 786436
  6.5 14.3 %copy-start.11 = (s32[512]{0:T(512)S(1)}, s32[512]{0:T(512)}, u32[]{:S(2)}) copy-start(s32[512]{0:T(512)} %param.14) | copy-start | bytes 6148
  6.5 14.3 %copy-start.8 = (f32[64,4,4]{0,2,1:T(4,128)S(1)}, f32[64,4,4]{0,2,1:T(4,128)}, u32[]{:S(2)}) copy-start(f32[64,4,4]{0,2,1:T(4,128)} %param.13) | copy-start | bytes 12292
  6.5 14.3 %copy-start = (f32[1,1,512,512]{3,2,1,0:T(8,128)S(1)}, f32[1,1,512,512]{3,2,1,0:T(8,128)}, u32[]{:S(2)}) copy-start(f32[1,1,512,512]{3,2,1,0:T(8,128)} %param.8) | copy-start | bytes 3145732
  6.5 53.1 %all-gather.3.cloned.1.call-start = ((), (), s32[]{:S(2)}) async-start(), calls=%async_computation | async-start | bytes 1310720 | tf_op jit(solution)/shard_map/all_gather | solution.py:341
  6.6 24.1 %copy-start.9 = (s32[1,1,8]{2,1,0:T(1,128)S(1)}, s32[1,1,8]{2,1,0:T(1,128)}, u32[]{:S(2)}) copy-start(s32[1,1,8]{2,1,0:T(1,128)} %param.11) | copy-start | bytes 100
  6.6 24.1 %copy-start.10 = (s32[1,1,8]{2,1,0:T(1,128)S(1)}, s32[1,1,8]{2,1,0:T(1,128)}, u32[]{:S(2)}) copy-start(s32[1,1,8]{2,1,0:T(1,128)} %param.12) | copy-start | bytes 100
  9.8 1.4 %copy-start.1 = (bf16[2080,512]{1,0:T(8,128)(2,1)}, bf16[2080,512]{1,0:T(8,128)(2,1)S(1)}, u32[]{:S(2)}) copy-start(bf16[2080,512]{1,0:T(8,128)(2,1)S(1)} %get-tuple-element.36.split_ref) | copy-start | bytes 6389764
  11.1 9.3 %collective-permute-start = (f32[2,80,128]{2,1,0:T(8,128)S(1)}, f32[2,80,128]{2,1,0:T(8,128)S(1)}, u32[]{:S(2)}, u32[]{:S(2)}) collective-permute-start(f32[2,80,128]{2,1,0:T(8,128)S(1)} %get-tuple-element.25), channel_id=1, source_target_pairs={{0,7},{1,6},{2,5},{3,4},{4,3},{5,2},{6,1},{7,0},{8,15},{9,14},{10,... | collective-permute-start | bytes 245768 | tf_op jit(solution)/shard_map/ppermute | solution.py:314
  15.7 3.2 %collective-permute-start.6 = (f32[1,80,128]{2,1,0:T(8,128)S(1)}, f32[1,80,128]{2,1,0:T(8,128)S(1)}, u32[]{:S(2)}, u32[]{:S(2)}) collective-permute-start(f32[1,80,128]{2,1,0:T(8,128)S(1)} %get-tuple-element.31), channel_id=1, source_target_pairs={{0,1},{1,0},{2,3},{3,2},{4,5},{5,4},{6,7},{7,6},{8,9},{9,8},{10,11... | collective-permute-start | bytes 122888 | tf_op jit(solution)/shard_map/ppermute | solution.py:314
  16.3 7.6 %collective-permute-start.1 = (f32[2,80,128]{2,1,0:T(8,128)S(1)}, f32[2,80,128]{2,1,0:T(8,128)S(1)}, u32[]{:S(2)}, u32[]{:S(2)}) collective-permute-start(f32[2,80,128]{2,1,0:T(8,128)S(1)} %get-tuple-element.26), channel_id=1, source_target_pairs={{0,6},{1,7},{2,4},{3,5},{4,2},{5,3},{6,0},{7,1},{8,14},{9,15},{10,... | collective-permute-start | bytes 245768 | tf_op jit(solution)/shard_map/ppermute | solution.py:314
  16.3 12.4 %collective-permute-start.2 = (f32[2,80,128]{2,1,0:T(8,128)S(1)}, f32[2,80,128]{2,1,0:T(8,128)S(1)}, u32[]{:S(2)}, u32[]{:S(2)}) collective-permute-start(f32[2,80,128]{2,1,0:T(8,128)S(1)} %get-tuple-element.27), channel_id=1, source_target_pairs={{0,5},{1,4},{2,7},{3,6},{4,1},{5,0},{6,3},{7,2},{8,13},{9,12},{10,... | collective-permute-start | bytes 245768 | tf_op jit(solution)/shard_map/ppermute | solution.py:314
  16.7 14.0 %collective-permute-start.3 = (f32[2,80,128]{2,1,0:T(8,128)S(1)}, f32[2,80,128]{2,1,0:T(8,128)S(1)}, u32[]{:S(2)}, u32[]{:S(2)}) collective-permute-start(f32[2,80,128]{2,1,0:T(8,128)S(1)} %get-tuple-element.28), channel_id=1, source_target_pairs={{0,4},{1,5},{2,6},{3,7},{4,0},{5,1},{6,2},{7,3},{8,12},{9,13},{10,... | collective-permute-start | bytes 245768 | tf_op jit(solution)/shard_map/ppermute | solution.py:314
  19.0 11.7 %collective-permute-start.4 = (f32[2,80,128]{2,1,0:T(8,128)S(1)}, f32[2,80,128]{2,1,0:T(8,128)S(1)}, u32[]{:S(2)}, u32[]{:S(2)}) collective-permute-start(f32[2,80,128]{2,1,0:T(8,128)S(1)} %get-tuple-element.29), channel_id=1, source_target_pairs={{0,3},{1,2},{2,1},{3,0},{4,7},{5,6},{6,5},{7,4},{8,11},{9,10},{10,... | collective-permute-start | bytes 245768 | tf_op jit(solution)/shard_map/ppermute | solution.py:314
  20.4 10.2 %collective-permute-start.5 = (f32[2,80,128]{2,1,0:T(8,128)S(1)}, f32[2,80,128]{2,1,0:T(8,128)S(1)}, u32[]{:S(2)}, u32[]{:S(2)}) collective-permute-start(f32[2,80,128]{2,1,0:T(8,128)S(1)} %get-tuple-element.30), channel_id=1, source_target_pairs={{0,2},{1,3},{2,0},{3,1},{4,6},{5,7},{6,4},{7,5},{8,10},{9,11},{10,... | collective-permute-start | bytes 245768 | tf_op jit(solution)/shard_map/ppermute | solution.py:314
  23.9 35.7 %copy-start.6 = (f32[4,512,128]{2,1,0:T(8,128)S(1)}, f32[4,512,128]{2,1,0:T(8,128)}, u32[]{:S(2)}) copy-start(f32[4,512,128]{2,1,0:T(8,128)} %copy-done.5) | copy-start | bytes 3145732
  59.6 1.6 %copy-start.2 = (bf16[2080,512]{1,0:T(8,128)(2,1)S(1)}, bf16[2080,512]{1,0:T(8,128)(2,1)}, u32[]{:S(2)}) copy-start(bf16[2080,512]{1,0:T(8,128)(2,1)} %copy-done.1) | copy-start | bytes 6389764
  63.2 7.6 %collective-permute-start.7 = (f32[2,80,128]{2,1,0:T(8,128)S(1)}, f32[2,80,128]{2,1,0:T(8,128)S(1)}, u32[]{:S(2)}, u32[]{:S(2)}) collective-permute-start(f32[2,80,128]{2,1,0:T(8,128)S(1)} %get-tuple-element.37), channel_id=1, source_target_pairs={{0,7},{1,6},{2,5},{3,4},{4,3},{5,2},{6,1},{7,0},{8,15},{9,14},{10,... | collective-permute-start | bytes 245768 | tf_op jit(solution)/shard_map/ppermute | solution.py:314
  66.0 3.4 %collective-permute-start.13 = (f32[1,80,128]{2,1,0:T(8,128)S(1)}, f32[1,80,128]{2,1,0:T(8,128)S(1)}, u32[]{:S(2)}, u32[]{:S(2)}) collective-permute-start(f32[1,80,128]{2,1,0:T(8,128)S(1)} %get-tuple-element.43), channel_id=1, source_target_pairs={{0,1},{1,0},{2,3},{3,2},{4,5},{5,4},{6,7},{7,6},{8,9},{9,8},{10,11... | collective-permute-start | bytes 122888 | tf_op jit(solution)/shard_map/ppermute | solution.py:314
  66.7 7.2 %collective-permute-start.8 = (f32[2,80,128]{2,1,0:T(8,128)S(1)}, f32[2,80,128]{2,1,0:T(8,128)S(1)}, u32[]{:S(2)}, u32[]{:S(2)}) collective-permute-start(f32[2,80,128]{2,1,0:T(8,128)S(1)} %get-tuple-element.38), channel_id=1, source_target_pairs={{0,6},{1,7},{2,4},{3,5},{4,2},{5,3},{6,0},{7,1},{8,14},{9,15},{10,... | collective-permute-start | bytes 245768 | tf_op jit(solution)/shard_map/ppermute | solution.py:314
  67.2 12.2 %collective-permute-start.9 = (f32[2,80,128]{2,1,0:T(8,128)S(1)}, f32[2,80,128]{2,1,0:T(8,128)S(1)}, u32[]{:S(2)}, u32[]{:S(2)}) collective-permute-start(f32[2,80,128]{2,1,0:T(8,128)S(1)} %get-tuple-element.39), channel_id=1, source_target_pairs={{0,5},{1,4},{2,7},{3,6},{4,1},{5,0},{6,3},{7,2},{8,13},{9,12},{10,... | collective-permute-start | bytes 245768 | tf_op jit(solution)/shard_map/ppermute | solution.py:314
  67.2 14.0 %collective-permute-start.10 = (f32[2,80,128]{2,1,0:T(8,128)S(1)}, f32[2,80,128]{2,1,0:T(8,128)S(1)}, u32[]{:S(2)}, u32[]{:S(2)}) collective-permute-start(f32[2,80,128]{2,1,0:T(8,128)S(1)} %get-tuple-element.40), channel_id=1, source_target_pairs={{0,4},{1,5},{2,6},{3,7},{4,0},{5,1},{6,2},{7,3},{8,12},{9,13},{10,... | collective-permute-start | bytes 245768 | tf_op jit(solution)/shard_map/ppermute | solution.py:314
  69.5 11.8 %collective-permute-start.11 = (f32[2,80,128]{2,1,0:T(8,128)S(1)}, f32[2,80,128]{2,1,0:T(8,128)S(1)}, u32[]{:S(2)}, u32[]{:S(2)}) collective-permute-start(f32[2,80,128]{2,1,0:T(8,128)S(1)} %get-tuple-element.41), channel_id=1, source_target_pairs={{0,3},{1,2},{2,1},{3,0},{4,7},{5,6},{6,5},{7,4},{8,11},{9,10},{10,... | collective-permute-start | bytes 245768 | tf_op jit(solution)/shard_map/ppermute | solution.py:314
  70.8 10.4 %collective-permute-start.12 = (f32[2,80,128]{2,1,0:T(8,128)S(1)}, f32[2,80,128]{2,1,0:T(8,128)S(1)}, u32[]{:S(2)}, u32[]{:S(2)}) collective-permute-start(f32[2,80,128]{2,1,0:T(8,128)S(1)} %get-tuple-element.42), channel_id=1, source_target_pairs={{0,2},{1,3},{2,0},{3,1},{4,6},{5,7},{6,4},{7,5},{8,10},{9,11},{10,... | collective-permute-start | bytes 245768 | tf_op jit(solution)/shard_map/ppermute | solution.py:314
  (3 other events, 3.5 us)
Sparse Core Ops, SparseCore 0:
  32.8 26.7 all-gather.2

commit v6 on v5

--- a/solution.py
+++ b/solution.py
@@ -63,6 +63,24 @@
     if count & (count - 1) == 0:
         return me ^ step, me ^ step
     return lax.rem(me + step, count), lax.rem(me + count - step, count)
+
+
+def gather_fields(halves):
+    count = lax.axis_size("kern")
+    if count == 4 and len(halves) == 2:
+        near, across = step_pairs(count, 1), step_pairs(count, 2)
+        low, high = halves
+        near_low = lax.ppermute(low, "kern", near)
+        across_high = lax.ppermute(high, "kern", across)
+        near_high = lax.ppermute(high, "kern", near)
+        across_low = lax.ppermute(low, "kern", across)
+        last_low = lax.ppermute(near_low, "kern", across)
+        last_high = lax.ppermute(across_high, "kern", near)
+        return [halves, [near_low, near_high], [across_low, across_high], [last_low, last_high]]
+    fields = [halves]
+    for step in range(1, count):
+        fields.append([lax.ppermute(half, "kern", step_pairs(count, step)) for half in halves])
+    return fields
 
 
 class Message:
@@ -124,20 +142,28 @@
     return base + 2 * size
 
 
-def first_coeff_kernel(messages, cols_ref, right_ref, *refs):
-    outs, (split_ref, cols, right, sems) = refs[: len(messages)], refs[len(messages) :]
+def first_coeff_kernel(messages, fresh, cols_ref, right_ref, *refs):
+    outs, refs = refs[: len(messages)], refs[len(messages) :]
+    split_ref = refs[0]
     rank = right_ref.shape[1]
     me = lax.axis_index("tile")
-    cols_copy = pltpu.make_async_copy(cols_ref, cols, sems.at[right.shape[0]])
-    cols_copy.start()
+    if fresh:
+        both_ref, right, sems, cols = refs[1:]
+        cols_copy = pltpu.make_async_copy(cols_ref, cols, sems.at[right.shape[0]])
+        cols_copy.start()
+    else:
+        both_ref = cols_ref
+        right, sems = refs[1:]
     copies = []
     for message in messages:
         for slot, _ in message.slots(me, True):
             at = len(copies)
             copies.append(pltpu.make_async_copy(right_ref.at[slot], right.at[at], sems.at[at]))
             copies[-1].start()
-    cols_copy.wait()
-    both = side_by_side(cols[...])
+    if fresh:
+        cols_copy.wait()
+        both_ref[...] = side_by_side(cols[...])
+    both = both_ref[...]
     base, block = 0, 0
     for chunk in chunks_of(messages):
         blocks = sum(messages[at].width for at in chunk)
@@ -150,56 +176,71 @@
         base = chunk_coefficients(split_ref, base, chunk, messages, rank, both, outs)
 
 
-def first_coefficients(cols, right_tile):
+def first_coefficients(cols, right_tile, messages, fresh):
     slots, rank, size = right_tile.shape
-    messages = messages_of(lax.axis_size("tile"), slots)
     blocks = sum(message.width for message in messages)
-    width = cols.shape[1]
+    width = cols.shape[1] if fresh else cols.shape[1] // 2
     outs = [struct(message.width, rank, width) for message in messages]
     outs.append(struct(2 * blocks * rank, size, dtype=bf16))
+    scratch = [pltpu.VMEM((blocks, rank, size), f32), pltpu.SemaphoreType.DMA((blocks + 1,))]
+    if fresh:
+        outs.append(struct(size, 2 * width, dtype=bf16))
+        scratch.append(pltpu.VMEM(cols.shape, f32))
     got = call(
-        functools.partial(first_coeff_kernel, messages),
+        functools.partial(first_coeff_kernel, messages, fresh),
         outs,
         [in_vmem] * len(outs),
-        [in_hbm, in_hbm],
-        [
-            pltpu.VMEM(cols.shape, f32),
-            pltpu.VMEM((blocks, rank, size), f32),
-            pltpu.SemaphoreType.DMA((blocks + 1,)),
-        ],
+        [in_hbm if fresh else in_vmem, in_hbm],
+        scratch,
         flops=8 * blocks * rank * size * width,
         moved=4 * blocks * rank * (2 * size + width),
-    )(to_hbm(cols), to_hbm(right_tile))
-    return got[:-1], got[-1]
-
-
-def next_coeff_kernel(messages, fields_ref, weights_ref, split_ref, *refs):
-    outs, cols_ref = refs[:-1], refs[-1]
+    )(to_hbm(cols) if fresh else cols, to_hbm(right_tile))
+    return got[: len(messages)], got[len(messages)], got[-1] if fresh else cols
+
+
+def next_coeff_kernel(message_sets, halves, *refs):
+    count = lax.axis_size("kern")
+    fields = refs[: count * halves]
+    weights_ref = refs[count * halves]
+    splits = refs[count * halves + 1 : count * halves + 1 + len(message_sets)]
+    outs, cols_ref = refs[count * halves + 1 + len(message_sets) : -1], refs[-1]
+    me = lax.axis_index("kern")
+    part = fields[0].shape[0]
+    for half in range(halves):
+        rows_of = pl.ds(half * part, part)
+        total = None
+        for step in range(count):
+            source = partner(me, step, count)[1]
+            term = fields[step * halves + half][...] * weights_ref[source, rows_of]
+            total = term if total is None else total + term
+        cols_ref[rows_of] = total
+    both = side_by_side(cols_ref[...])
     rank = outs[0].shape[1]
-    mixed = fields_ref[0] * weights_ref[0]
-    for b in range(1, fields_ref.shape[0]):
-        mixed = mixed + fields_ref[b] * weights_ref[b]
-    cols_ref[...] = mixed
-    both = side_by_side(mixed)
-    base = 0
-    for chunk in chunks_of(messages):
-        base = chunk_coefficients(split_ref, base, chunk, messages, rank, both, outs)
-
-
-def next_coefficients(fields, weights, split_right, slots, rank):
-    messages = messages_of(lax.axis_size("tile"), slots)
-    _, size, width = fields.shape
-    total = split_right.shape[0]
-    outs = [struct(message.width, rank, width) for message in messages]
+    done = 0
+    for messages, split_ref in zip(message_sets, splits):
+        here = outs[done : done + len(messages)]
+        done += len(messages)
+        base = 0
+        for chunk in chunks_of(messages):
+            base = chunk_coefficients(split_ref, base, chunk, messages, rank, both, here)
+
+
+def next_coefficients(fields, weights, splits, message_sets, rank):
+    halves = len(fields[0])
+    part, width = fields[0][0].shape
+    size = part * halves
+    outs = [struct(message.width, rank, width) for group in message_sets for message in group]
     outs.append(struct(size, width))
+    total = sum(split_right.shape[0] for split_right in splits)
+    flat = [half for field in fields for half in field]
     got = call(
-        functools.partial(next_coeff_kernel, messages),
+        functools.partial(next_coeff_kernel, message_sets, halves),
         outs,
         [in_vmem] * len(outs),
-        [in_vmem] * 3,
+        [in_vmem] * (len(flat) + 1 + len(splits)),
         flops=4 * total * size * width,
         moved=2 * total * (size + width),
-    )(fields, weights, split_right)
+    )(*flat, weights, *splits)
     return got[:-1], got[-1]
 
 
@@ -226,14 +267,15 @@
 
 
 def prepare_kernel(
-    diag_ref, cols_ref, left_ref, table_ref, index_ref, diag_out, left_hi, left_lo, weights_ref
+    halves, diag_hbm, cols_hbm, left_hbm, table_ref, index_ref,
+    diag_out, left_out, weights_ref, diag_ref, cols_ref, left_ref, sems,
 ):
-    diag_out[...] = times_diag(diag_ref, cols_ref)
-    total = left_ref.shape[0]
-    step = 128 if total % 128 == 0 else total
-    for at in range(0, total, step):
-        span = slice(at, at + step)
-        left_hi[:, span], left_lo[:, span] = split(left_ref[span].T)
+    copies = []
+    for at, (source, target) in enumerate(
+        ((diag_hbm, diag_ref), (cols_hbm, cols_ref), (left_hbm, left_ref))
+    ):
+        copies.append(pltpu.make_async_copy(source, target, sems.at[at]))
+        copies[-1].start()
     own = table_ref[lax.axis_index("kern")]
     groups, entries = own.shape
     size = index_ref.shape[1]
@@ -242,30 +284,55 @@
     width = weights_ref.shape[2]
     for b in range(groups):
         weights_ref[b] = jnp.broadcast_to(weights[b : b + 1], (width, size)).T
-
-
-def prepare(diag_tile, cols, left_rows, table, index):
+    copies[0].wait()
+    copies[1].wait()
+    diag_out[...] = times_diag(diag_ref, cols_ref)
+    copies[2].wait()
+    total = left_ref.shape[0]
+    step = 128 if total % 128 == 0 else total
+    part = size // halves
+    for at in range(0, total, step):
+        span = slice(at, at + step)
+        hi, lo = split(left_ref[span].T)
+        for half in range(halves):
+            base = 2 * half * part
+            rows_of = slice(half * part, (half + 1) * part)
+            left_out[base : base + part, span] = hi[rows_of]
+            left_out[base + part : base + 2 * part, span] = lo[rows_of]
+
+
+def prepare(diag_tile, cols, left_rows, table, index, halves):
     size, width = cols.shape
     total = left_rows.shape[0]
+    groups = table.shape[0]
     return call(
-        prepare_kernel,
+        functools.partial(prepare_kernel, halves),
         [
             struct(size, width),
-            struct(size, total, dtype=bf16),
-            struct(size, total, dtype=bf16),
-            struct(table.shape[0], size, width),
+            struct(2 * size, total, dtype=bf16),
+            struct(groups, size, width),
         ],
-        [in_vmem] * 4,
-        [in_vmem] * 5,
+        [in_vmem] * 3,
+        [in_hbm] * 3 + [in_vmem] * 2,
+        [
+            pltpu.VMEM(diag_tile.shape, f32),
+            pltpu.VMEM(cols.shape, f32),
+            pltpu.VMEM(left_rows.shape, f32),
+            pltpu.SemaphoreType.DMA((3,)),
+        ],
         flops=8 * size * size * width,
         moved=8 * total * size + 4 * size * (size + 2 * width),
-    )(diag_tile, cols, left_rows, table, index)
-
-
-def row_kernel(messages, offs_ref, ranks_ref, *refs):
+    )(to_hbm(diag_tile), to_hbm(cols), to_hbm(left_rows), table, index)
+
+
+def row_kernel(messages, halves, final, offs_ref, ranks_ref, *refs):
     gots = refs[: len(messages)]
-    hi_ref, lo_ref, diag_ref = refs[len(messages) : len(messages) + 3]
-    out_ref, picked, term_of = refs[-3:]
+    left_ref, diag_ref = refs[len(messages) : len(messages) + 2]
+    outs = refs[len(messages) + 2 :]
+    if final:
+        outs, (picked, term_of, stage, sems) = outs[:-4], outs[-4:]
+    else:
+        outs, (picked, term_of) = outs[:-2], outs[-2:]
     terms = offs_ref.shape[1]
     rank, width = gots[0].shape[1:]
     slots = term_of.shape[0]
@@ -288,29 +355,42 @@
         for w, (slot, there) in enumerate(message.slots(me, False)):
             pick(got, w, jnp.where(there, term_of[slot], -1))
     both = side_by_side(picked[...])
-    out_ref[...] = fold(dot(hi_ref[...], both) + dot(lo_ref[...], both)) + diag_ref[...]
-
-
-def rows(offsets, ranks, gots, left_hi, left_lo, diag_part, slots):
-    size, total = left_hi.shape
-    width = diag_part.shape[1]
-    messages = messages_of(lax.axis_size("tile"), slots)
+    part = diag_ref.shape[0] // halves
+    sent = []
+    for half in range(halves):
+        rows_of = pl.ds(half * part, part)
+        got = fold(dot(left_ref[pl.ds(2 * half * part, 2 * part)], both))
+        total = got[:part] + got[part:] + diag_ref[rows_of]
+        if final:
+            stage[rows_of] = total
+            sent.append(
+                pltpu.make_async_copy(stage.at[rows_of], outs[0].at[rows_of], sems.at[half])
+            )
+            sent[-1].start()
+        else:
+            outs[half][...] = total
+    for copy in sent:
+        copy.wait()
+
+
+def rows(offsets, ranks, gots, messages, left_split, diag_part, slots, halves, final):
+    size, width = diag_part.shape
+    total = left_split.shape[1]
+    scratch = [pltpu.VMEM((total, width), f32), pltpu.SMEM((slots,), jnp.int32)]
+    if final:
+        scratch += [pltpu.VMEM((size, width), f32), pltpu.SemaphoreType.DMA((halves,))]
     return call(
-        functools.partial(row_kernel, messages),
-        struct(size, width),
-        in_vmem,
-        [in_smem, in_smem] + [in_vmem] * (len(messages) + 3),
-        [
-            pltpu.VMEM((total, width), f32),
-            pltpu.SMEM((slots,), jnp.int32),
-        ],
+        functools.partial(row_kernel, messages, halves, final),
+        pltpu.HBM((size, width), f32) if final else [struct(size // halves, width)] * halves,
+        in_hbm if final else [in_vmem] * halves,
+        [in_smem, in_smem] + [in_vmem] * (len(messages) + 2),
+        scratch,
         flops=8 * total * size * width,
         moved=4 * total * (size + width),
-    )(offsets, ranks, *gots, left_hi, left_lo, diag_part)
-
-
-def deliver(coeffs, slots):
-    messages = messages_of(lax.axis_size("tile"), slots)
+    )(offsets, ranks, *gots, left_split, diag_part)
+
+
+def deliver(coeffs, messages):
     return [lax.ppermute(sent, "tile", message.pairs) for sent, message in zip(coeffs, messages)]
 
 
@@ -329,20 +409,27 @@
     offsets = tile_offsets[0]
     ranks = tile_ranks[0]
     slots, rank, size = right_tile.shape
+    halves = 2 if size % 32 == 0 else 1
     left_rows = left_factors.reshape(-1, size)
     table = mixing.transpose(1, 2, 0)
     index = block_index[None]
     cols = rhs_field[0]
 
-    coeffs, split_right = first_coefficients(cols, right_tile)
-    gots = deliver(coeffs, slots)
-    diag_part, left_hi, left_lo, weights = prepare(diag_tile, cols, left_rows, table, index)
-    first = rows(offsets, ranks, gots, left_hi, left_lo, diag_part, slots)
-    fields = lax.all_gather(first, "kern")
-    coeffs, cols = next_coefficients(fields, weights, split_right, slots, rank)
-    gots = deliver(coeffs, slots)
+    messages = messages_of(lax.axis_size("tile"), slots)
+    far = (len(messages) + 1) // 2
+    message_sets = [messages[:far], messages[far:]]
+    gots, splits, given = [], [], cols
+    for group in message_sets:
+        coeffs, split_right, given = first_coefficients(given, right_tile, group, not splits)
+        gots += deliver(coeffs, group)
+        splits.append(split_right)
+    diag_part, left_split, weights = prepare(diag_tile, cols, left_rows, table, index, halves)
+    first = rows(offsets, ranks, gots, messages, left_split, diag_part, slots, halves, False)
+    fields = gather_fields(first)
+    coeffs, cols = next_coefficients(fields, weights, splits, message_sets, rank)
+    gots = deliver(coeffs, messages)
     diag_part = diagonal(diag_tile, cols)
-    return rows(offsets, ranks, gots, left_hi, left_lo, diag_part, slots)[None]
+    return rows(offsets, ranks, gots, messages, left_split, diag_part, slots, halves, True)[None]
 
 
 def solution(mesh):

time: 90.3 us -> 56.6 us (0.63)
  waiting for transfers between devices: 42.8 us -> 20.1 us
  between operations: 13.5 us -> 0.1 us
  starting transfers between devices: 18.1 us -> 25.3 us
  local copies, waits for them, and re-layouts: 6.48 us -> 0.02 us
  Pallas kernels: 9.24 us -> 10.9 us
    all_gather x1 -> x0, waiting for transfers between devices: 26.9 us -> none  [local(): fields = lax.all_gather(first, 'kern')]
    ppermute x0 -> x6, starting transfers between devices: none -> 7.14 us  [the longest x1 1.78 us: gather_fields(): near_low = lax.ppermute(low, 'kern', near)]
    unnamed x24 -> x10, local copies, waits for them, and re-layouts: 6.48 us -> 0.02 us
    ppermute x0 -> x6, waiting for transfers between devices: none -> 6.02 us  [the longest x1 1.55 us: gather_fields(): near_low = lax.ppermute(low, 'kern', near)]
    ppermute x14, waiting for transfers between devices: 15.9 us -> 14.1 us  [deliver(): lax.ppermute(sent, 'tile', message.pairs)]
    pallas_call x5 -> x6, Pallas kernels: 8.79 us -> 10.5 us  [the longest x2 4.16 us: first_coefficients(): call(functools.partial(first_coeff_kernel, messages, fresh), outs, [in_vm...]
  transfers between devices with their start and end apart: 15 -> 20, of which waited for: 6 -> 12; matrix products, arithmetic and copies ran while one was open for 0% -> 0% of each run, Pallas kernels for 1% -> 8%
where the time goes in v6:
time: 56.6 us; the launch traced here: 56.5 us
  starting transfers between devices  25.3 us (45%)
  waiting for transfers between devices  20.1 us (36%)
  Pallas kernels  10.9 us (19%)
    ppermute x14, starting transfers between devices, deliver(): lax.ppermute(sent, 'tile', message.pairs)  18.2 us
    ppermute x14, waiting for transfers between devices, deliver(): lax.ppermute(sent, 'tile', message.pairs)  14.1 us
    pallas_call x2, Pallas kernels, first_coefficients(): call(functools.partial(first_coeff_kernel, messages, fresh), outs, [in_vm...  4.16 us
    pallas_call x2, Pallas kernels, rows(): call(functools.partial(row_kernel, messages, halves, final), pltpu.HBM((s...  3.37 us
    pallas_call x1, Pallas kernels, prepare(): call(functools.partial(prepare_kernel, halves), [struct(size, width), str...  2.18 us
    ppermute x1, starting transfers between devices, gather_fields(): near_low = lax.ppermute(low, 'kern', near)  1.78 us
    ppermute x1, waiting for transfers between devices, gather_fields(): near_low = lax.ppermute(low, 'kern', near)  1.55 us
    ppermute x1, starting transfers between devices, gather_fields(): last_low = lax.ppermute(near_low, 'kern', across)  1.54 us
  transfers between devices with their start and end apart: 20, of which 12 were waited for; matrix products, arithmetic and copies ran while one was open for 0% of the time, Pallas kernels for 8%

profile of v6, /device:TPU:0, one launch (start us, length us, event | category | flops | bytes accessed | tf_op | source)
XLA Modules:
  0.0 56.5 jit_solution(13207026409777936330)
XLA Ops:
  0.0 2.3 %shard_map.82 = (f32[2,80,128]{2,1,0:T(8,128)S(1)}, f32[2,80,128]{2,1,0:T(8,128)S(1)}, f32[2,80,128]{2,1,0:T(8,128)S(1)}, f32[2,80,128]{2,1,0:T(8,128)S(1)}, bf1...) custom-call(f32[512,128]{1,0:T(8,128)} %bitcast.20, f32[12,80,512]{2,1,0:T(8,128)} %bitcast.17), custom_call_target="tpu_custom_call" | custom-call | flops 335544320 | bytes 2949120 | tf_op jit(solution)/shard_map/pallas_call | solution.py:189
  2.4 4.6 %collective-permute-start = (f32[2,80,128]{2,1,0:T(8,128)S(1)}, f32[2,80,128]{2,1,0:T(8,128)S(1)}, u32[]{:S(2)}, u32[]{:S(2)}) collective-permute-start(f32[2,80,128]{2,1,0:T(8,128)S(1)} %get-tuple-element.28), channel_id=1, source_target_pairs={{0,7},{1,6},{2,5},{3,4},{4,3},{5,2},{6,1},{7,0},{8,15},{9,14},{10,... | collective-permute-start | bytes 245768 | tf_op jit(solution)/shard_map/ppermute | solution.py:394
  6.9 1.8 %shard_map.83 = (f32[2,80,128]{2,1,0:T(8,128)S(1)}, f32[2,80,128]{2,1,0:T(8,128)S(1)}, f32[1,80,128]{2,1,0:T(8,128)S(1)}, bf16[800,512]{1,0:T(8,128)(2,1)S(1)}) custom-call(bf16[512,256]{1,0:T(8,128)(2,1)S(1)} %get-tuple-element.32.cols_ref, f32[12,80,512]{2,1,0:T(8,128)} %bitcast.18), custom_call_target="tpu_custom_call" | custom-call | flops 209715200 | bytes 1843200 | tf_op jit(solution)/shard_map/pallas_call | solution.py:189
  9.9 2.3 %collective-permute-start.3 = (f32[2,80,128]{2,1,0:T(8,128)S(1)}, f32[2,80,128]{2,1,0:T(8,128)S(1)}, u32[]{:S(2)}, u32[]{:S(2)}) collective-permute-start(f32[2,80,128]{2,1,0:T(8,128)S(1)} %get-tuple-element.31), channel_id=1, source_target_pairs={{0,4},{1,5},{2,6},{3,7},{4,0},{5,1},{6,2},{7,3},{8,12},{9,13},{10,... | collective-permute-start | bytes 245768 | tf_op jit(solution)/shard_map/ppermute | solution.py:394
  12.2 1.4 %collective-permute-start.4 = (f32[2,80,128]{2,1,0:T(8,128)S(1)}, f32[2,80,128]{2,1,0:T(8,128)S(1)}, u32[]{:S(2)}, u32[]{:S(2)}) collective-permute-start(f32[2,80,128]{2,1,0:T(8,128)S(1)} %get-tuple-element.33), channel_id=1, source_target_pairs={{0,3},{1,2},{2,1},{3,0},{4,7},{5,6},{6,5},{7,4},{8,11},{9,10},{10,... | collective-permute-start | bytes 245768 | tf_op jit(solution)/shard_map/ppermute | solution.py:394
  14.0 2.2 %shard_map.84 = (f32[512,128]{1,0:T(8,128)S(1)}, bf16[1024,640]{1,0:T(8,128)(2,1)S(1)}, f32[4,512,128]{2,1,0:T(8,128)S(1)}) custom-call(f32[512,512]{1,0:T(8,128)} %bitcast.9, f32[512,128]{1,0:T(8,128)} %bitcast.21, f32[640,512]{1,0:T(8,128)} %bitcast.19, f32[4,4,64]{2,1,0:T(4,128)S(1)} %bitcast.11, s32[1,512]{1,0:T(1,128)S(1)} %bitcast.12), custom_call_target="tpu_custom_call" | custom-call | flops 268435456 | bytes 4194304 | tf_op jit(solution)/shard_map/pallas_call | solution.py:308
  16.7 3.5 %collective-permute-done.2.refs_2_ = f32[2,80,128]{2,1,0:T(8,128)S(1)} collective-permute-done((f32[2,80,128]{2,1,0:T(8,128)S(1)}, f32[2,80,128]{2,1,0:T(8,128)S(1)}, u32[]{:S(2)}, u32[]{:S(2)}) %collective-permute-start.2) | collective-permute-done | bytes 81952 | tf_op jit(solution)/shard_map/ppermute | solution.py:394
  20.2 2.1 %collective-permute-done.3.refs_3_ = f32[2,80,128]{2,1,0:T(8,128)S(1)} collective-permute-done((f32[2,80,128]{2,1,0:T(8,128)S(1)}, f32[2,80,128]{2,1,0:T(8,128)S(1)}, u32[]{:S(2)}, u32[]{:S(2)}) %collective-permute-start.3) | collective-permute-done | bytes 81952 | tf_op jit(solution)/shard_map/ppermute | solution.py:394
  22.3 1.3 %shard_map.85 = (f32[256,128]{1,0:T(8,128)S(1)}, f32[256,128]{1,0:T(8,128)S(1)}) custom-call(s32[1,8]{1,0:T(1,128)S(1)} %bitcast.13, s32[1,8]{1,0:T(1,128)S(1)} %bitcast.15, f32[2,80,128]{2,1,0:T(8,128)S(1)} %collective-permute-done.refs_0_, f32[2,80,128]{2,1,0:T(8,128)S(1)} %collective-permute-done.1.refs_1_, ...), custom_call_target="tpu_custom_call" | custom-call | flops 335544320 | bytes 1638400 | tf_op jit(solution)/shard_map/pallas_call | solution.py:382
  23.6 1.8 %collective-permute-start.7 = (f32[256,128]{1,0:T(8,128)S(1)}, f32[256,128]{1,0:T(8,128)S(1)}, u32[]{:S(2)}, u32[]{:S(2)}) collective-permute-start(f32[256,128]{1,0:T(8,128)S(1)} %get-tuple-element.38.refs_0_), channel_id=1, source_target_pairs={{0,8},{8,0},{16,24},{24,16},{1,9},{9,1},{17,25},{25,17},{2,10},{10... | collective-permute-start | bytes 393224 | tf_op jit(solution)/shard_map/ppermute | solution.py:73
  25.4 1.5 %collective-permute-start.10 = (f32[256,128]{1,0:T(8,128)S(1)}, f32[256,128]{1,0:T(8,128)S(1)}, u32[]{:S(2)}, u32[]{:S(2)}) collective-permute-start(f32[256,128]{1,0:T(8,128)S(1)} %get-tuple-element.39.refs_1_), channel_id=1, source_target_pairs={{0,16},{8,24},{16,0},{24,8},{1,17},{9,25},{17,1},{25,9},{2,18},{10... | collective-permute-start | bytes 393224 | tf_op jit(solution)/shard_map/ppermute | solution.py:74
  27.7 1.5 %collective-permute-done.7.refs_2_ = f32[256,128]{1,0:T(8,128)S(1)} collective-permute-done((f32[256,128]{1,0:T(8,128)S(1)}, f32[256,128]{1,0:T(8,128)S(1)}, u32[]{:S(2)}, u32[]{:S(2)}) %collective-permute-start.7) | collective-permute-done | bytes 131104 | tf_op jit(solution)/shard_map/ppermute | solution.py:73
  29.3 1.5 %collective-permute-start.11 = (f32[256,128]{1,0:T(8,128)S(1)}, f32[256,128]{1,0:T(8,128)S(1)}, u32[]{:S(2)}, u32[]{:S(2)}) collective-permute-start(f32[256,128]{1,0:T(8,128)S(1)} %collective-permute-done.7.refs_2_), channel_id=1, source_target_pairs={{0,16},{8,24},{16,0},{24,8},{1,17},{9,25},{17,1},{25,9},{2,18},{10... | collective-permute-start | bytes 393224 | tf_op jit(solution)/shard_map/ppermute | solution.py:77
  30.8 1.0 %collective-permute-done.10.refs_5_ = f32[256,128]{1,0:T(8,128)S(1)} collective-permute-done((f32[256,128]{1,0:T(8,128)S(1)}, f32[256,128]{1,0:T(8,128)S(1)}, u32[]{:S(2)}, u32[]{:S(2)}) %collective-permute-start.10) | collective-permute-done | bytes 131104 | tf_op jit(solution)/shard_map/ppermute | solution.py:74
  31.8 1.5 %collective-permute-start.12 = (f32[256,128]{1,0:T(8,128)S(1)}, f32[256,128]{1,0:T(8,128)S(1)}, u32[]{:S(2)}, u32[]{:S(2)}) collective-permute-start(f32[256,128]{1,0:T(8,128)S(1)} %collective-permute-done.10.refs_5_), channel_id=1, source_target_pairs={{0,8},{8,0},{16,24},{24,16},{1,9},{9,1},{17,25},{25,17},{2,10},{10... | collective-permute-start | bytes 393224 | tf_op jit(solution)/shard_map/ppermute | solution.py:78
  33.3 1.3 %collective-permute-done.9.refs_4_ = f32[256,128]{1,0:T(8,128)S(1)} collective-permute-done((f32[256,128]{1,0:T(8,128)S(1)}, f32[256,128]{1,0:T(8,128)S(1)}, u32[]{:S(2)}, u32[]{:S(2)}) %collective-permute-start.9) | collective-permute-done | bytes 131104 | tf_op jit(solution)/shard_map/ppermute | solution.py:76
  34.6 1.5 %collective-permute-done.11.refs_6_ = f32[256,128]{1,0:T(8,128)S(1)} collective-permute-done((f32[256,128]{1,0:T(8,128)S(1)}, f32[256,128]{1,0:T(8,128)S(1)}, u32[]{:S(2)}, u32[]{:S(2)}) %collective-permute-start.11) | collective-permute-done | bytes 131104 | tf_op jit(solution)/shard_map/ppermute | solution.py:77
  37.7 3.3 %collective-permute-start.19 = (f32[1,80,128]{2,1,0:T(8,128)S(1)}, f32[1,80,128]{2,1,0:T(8,128)S(1)}, u32[]{:S(2)}, u32[]{:S(2)}) collective-permute-start(f32[1,80,128]{2,1,0:T(8,128)S(1)} %get-tuple-element.49), channel_id=1, source_target_pairs={{0,1},{1,0},{2,3},{3,2},{4,5},{5,4},{6,7},{7,6},{8,9},{9,8},{10,11... | collective-permute-start | bytes 122888 | tf_op jit(solution)/shard_map/ppermute | solution.py:394
  41.6 2.2 %collective-permute-start.16 = (f32[2,80,128]{2,1,0:T(8,128)S(1)}, f32[2,80,128]{2,1,0:T(8,128)S(1)}, u32[]{:S(2)}, u32[]{:S(2)}) collective-permute-start(f32[2,80,128]{2,1,0:T(8,128)S(1)} %get-tuple-element.46), channel_id=1, source_target_pairs={{0,4},{1,5},{2,6},{3,7},{4,0},{5,1},{6,2},{7,3},{8,12},{9,13},{10,... | collective-permute-start | bytes 245768 | tf_op jit(solution)/shard_map/ppermute | solution.py:394
  43.8 1.2 %collective-permute-start.17 = (f32[2,80,128]{2,1,0:T(8,128)S(1)}, f32[2,80,128]{2,1,0:T(8,128)S(1)}, u32[]{:S(2)}, u32[]{:S(2)}) collective-permute-start(f32[2,80,128]{2,1,0:T(8,128)S(1)} %get-tuple-element.47), channel_id=1, source_target_pairs={{0,3},{1,2},{2,1},{3,0},{4,7},{5,6},{6,5},{7,4},{8,11},{9,10},{10,... | collective-permute-start | bytes 245768 | tf_op jit(solution)/shard_map/ppermute | solution.py:394
  46.4 1.7 %collective-permute-done.14.refs_1_ = f32[2,80,128]{2,1,0:T(8,128)S(1)} collective-permute-done((f32[2,80,128]{2,1,0:T(8,128)S(1)}, f32[2,80,128]{2,1,0:T(8,128)S(1)}, u32[]{:S(2)}, u32[]{:S(2)}) %collective-permute-start.14) | collective-permute-done | bytes 81952 | tf_op jit(solution)/shard_map/ppermute | solution.py:394
  48.2 4.3 %collective-permute-done.15.refs_2_ = f32[2,80,128]{2,1,0:T(8,128)S(1)} collective-permute-done((f32[2,80,128]{2,1,0:T(8,128)S(1)}, f32[2,80,128]{2,1,0:T(8,128)S(1)}, u32[]{:S(2)}, u32[]{:S(2)}) %collective-permute-start.15) | collective-permute-done | bytes 81952 | tf_op jit(solution)/shard_map/ppermute | solution.py:394
  52.4 1.7 %collective-permute-done.16.refs_3_ = f32[2,80,128]{2,1,0:T(8,128)S(1)} collective-permute-done((f32[2,80,128]{2,1,0:T(8,128)S(1)}, f32[2,80,128]{2,1,0:T(8,128)S(1)}, u32[]{:S(2)}, u32[]{:S(2)}) %collective-permute-start.16) | collective-permute-done | bytes 81952 | tf_op jit(solution)/shard_map/ppermute | solution.py:394
  54.4 2.0 %shard_map.88 = f32[512,128]{1,0:T(8,128)} custom-call(s32[1,8]{1,0:T(1,128)S(1)} %bitcast.14, s32[1,8]{1,0:T(1,128)S(1)} %bitcast.16, f32[2,80,128]{2,1,0:T(8,128)S(1)} %collective-permute-done.13.refs_0_, f32[2,80,128]{2,1,0:T(8,128)S(1)} %collective-permute-done.14.refs_1_, f32[2,80,128]{2,1,0:T(8,128)S(1)} %collective-permute-done.15.refs_2_, ...), custom_call_target="tpu_custom_call" | custom-call | flops 335544320 | bytes 1638400 | tf_op jit(solution)/shard_map/pallas_call | solution.py:382
  (33 shorter events, 6.7 us)
Async XLA Ops:
  2.3 11.7 %copy-start.1 = (f32[64,4,4]{0,2,1:T(4,128)S(1)}, f32[64,4,4]{0,2,1:T(4,128)}, u32[]{:S(2)}) copy-start(f32[64,4,4]{0,2,1:T(4,128)} %param.13) | copy-start | bytes 12292
  2.4 11.6 %copy-start.2 = (s32[512]{0:T(512)S(1)}, s32[512]{0:T(512)}, u32[]{:S(2)}) copy-start(s32[512]{0:T(512)} %param.14) | copy-start | bytes 6148
  2.4 11.3 %collective-permute-start = (f32[2,80,128]{2,1,0:T(8,128)S(1)}, f32[2,80,128]{2,1,0:T(8,128)S(1)}, u32[]{:S(2)}, u32[]{:S(2)}) collective-permute-start(f32[2,80,128]{2,1,0:T(8,128)S(1)} %get-tuple-element.28), channel_id=1, source_target_pairs={{0,7},{1,6},{2,5},{3,4},{4,3},{5,2},{6,1},{7,0},{8,15},{9,14},{10,... | collective-permute-start | bytes 245768 | tf_op jit(solution)/shard_map/ppermute | solution.py:394
  8.8 3.4 %collective-permute-start.6 = (f32[1,80,128]{2,1,0:T(8,128)S(1)}, f32[1,80,128]{2,1,0:T(8,128)S(1)}, u32[]{:S(2)}, u32[]{:S(2)}) collective-permute-start(f32[1,80,128]{2,1,0:T(8,128)S(1)} %get-tuple-element.35), channel_id=1, source_target_pairs={{0,1},{1,0},{2,3},{3,2},{4,5},{5,4},{6,7},{7,6},{8,9},{9,8},{10,11... | collective-permute-start | bytes 122888 | tf_op jit(solution)/shard_map/ppermute | solution.py:394
  9.5 7.2 %collective-permute-start.1 = (f32[2,80,128]{2,1,0:T(8,128)S(1)}, f32[2,80,128]{2,1,0:T(8,128)S(1)}, u32[]{:S(2)}, u32[]{:S(2)}) collective-permute-start(f32[2,80,128]{2,1,0:T(8,128)S(1)} %get-tuple-element.29), channel_id=1, source_target_pairs={{0,6},{1,7},{2,4},{3,5},{4,2},{5,3},{6,0},{7,1},{8,14},{9,15},{10,... | collective-permute-start | bytes 245768 | tf_op jit(solution)/shard_map/ppermute | solution.py:394
  9.5 10.7 %collective-permute-start.2 = (f32[2,80,128]{2,1,0:T(8,128)S(1)}, f32[2,80,128]{2,1,0:T(8,128)S(1)}, u32[]{:S(2)}, u32[]{:S(2)}) collective-permute-start(f32[2,80,128]{2,1,0:T(8,128)S(1)} %get-tuple-element.30), channel_id=1, source_target_pairs={{0,5},{1,4},{2,7},{3,6},{4,1},{5,0},{6,3},{7,2},{8,13},{9,12},{10,... | collective-permute-start | bytes 245768 | tf_op jit(solution)/shard_map/ppermute | solution.py:394
  9.9 12.4 %collective-permute-start.3 = (f32[2,80,128]{2,1,0:T(8,128)S(1)}, f32[2,80,128]{2,1,0:T(8,128)S(1)}, u32[]{:S(2)}, u32[]{:S(2)}) collective-permute-start(f32[2,80,128]{2,1,0:T(8,128)S(1)} %get-tuple-element.31), channel_id=1, source_target_pairs={{0,4},{1,5},{2,6},{3,7},{4,0},{5,1},{6,2},{7,3},{8,12},{9,13},{10,... | collective-permute-start | bytes 245768 | tf_op jit(solution)/shard_map/ppermute | solution.py:394
  12.2 10.1 %collective-permute-start.4 = (f32[2,80,128]{2,1,0:T(8,128)S(1)}, f32[2,80,128]{2,1,0:T(8,128)S(1)}, u32[]{:S(2)}, u32[]{:S(2)}) collective-permute-start(f32[2,80,128]{2,1,0:T(8,128)S(1)} %get-tuple-element.33), channel_id=1, source_target_pairs={{0,3},{1,2},{2,1},{3,0},{4,7},{5,6},{6,5},{7,4},{8,11},{9,10},{10,... | collective-permute-start | bytes 245768 | tf_op jit(solution)/shard_map/ppermute | solution.py:394
  13.6 8.7 %collective-permute-start.5 = (f32[2,80,128]{2,1,0:T(8,128)S(1)}, f32[2,80,128]{2,1,0:T(8,128)S(1)}, u32[]{:S(2)}, u32[]{:S(2)}) collective-permute-start(f32[2,80,128]{2,1,0:T(8,128)S(1)} %get-tuple-element.34), channel_id=1, source_target_pairs={{0,2},{1,3},{2,0},{3,1},{4,6},{5,7},{6,4},{7,5},{8,10},{9,11},{10,... | collective-permute-start | bytes 245768 | tf_op jit(solution)/shard_map/ppermute | solution.py:394
  14.0 8.3 %copy-start.4 = (s32[1,1,8]{2,1,0:T(1,128)S(1)}, s32[1,1,8]{2,1,0:T(1,128)}, u32[]{:S(2)}) copy-start(s32[1,1,8]{2,1,0:T(1,128)} %param.12) | copy-start | bytes 100
  23.6 5.7 %collective-permute-start.7 = (f32[256,128]{1,0:T(8,128)S(1)}, f32[256,128]{1,0:T(8,128)S(1)}, u32[]{:S(2)}, u32[]{:S(2)}) collective-permute-start(f32[256,128]{1,0:T(8,128)S(1)} %get-tuple-element.38.refs_0_), channel_id=1, source_target_pairs={{0,8},{8,0},{16,24},{24,16},{1,9},{9,1},{17,25},{25,17},{2,10},{10... | collective-permute-start | bytes 393224 | tf_op jit(solution)/shard_map/ppermute | solution.py:73
  25.4 6.4 %collective-permute-start.10 = (f32[256,128]{1,0:T(8,128)S(1)}, f32[256,128]{1,0:T(8,128)S(1)}, u32[]{:S(2)}, u32[]{:S(2)}) collective-permute-start(f32[256,128]{1,0:T(8,128)S(1)} %get-tuple-element.39.refs_1_), channel_id=1, source_target_pairs={{0,16},{8,24},{16,0},{24,8},{1,17},{9,25},{17,1},{25,9},{2,18},{10... | collective-permute-start | bytes 393224 | tf_op jit(solution)/shard_map/ppermute | solution.py:74
  26.9 7.7 %collective-permute-start.9 = (f32[256,128]{1,0:T(8,128)S(1)}, f32[256,128]{1,0:T(8,128)S(1)}, u32[]{:S(2)}, u32[]{:S(2)}) collective-permute-start(f32[256,128]{1,0:T(8,128)S(1)} %get-tuple-element.38.refs_0_), channel_id=1, source_target_pairs={{0,16},{8,24},{16,0},{24,8},{1,17},{9,25},{17,1},{25,9},{2,18},{10... | collective-permute-start | bytes 393224 | tf_op jit(solution)/shard_map/ppermute | solution.py:76
  27.4 7.2 %collective-permute-start.8 = (f32[256,128]{1,0:T(8,128)S(1)}, f32[256,128]{1,0:T(8,128)S(1)}, u32[]{:S(2)}, u32[]{:S(2)}) collective-permute-start(f32[256,128]{1,0:T(8,128)S(1)} %get-tuple-element.39.refs_1_), channel_id=1, source_target_pairs={{0,8},{8,0},{16,24},{24,16},{1,9},{9,1},{17,25},{25,17},{2,10},{10... | collective-permute-start | bytes 393224 | tf_op jit(solution)/shard_map/ppermute | solution.py:75
  29.3 6.8 %collective-permute-start.11 = (f32[256,128]{1,0:T(8,128)S(1)}, f32[256,128]{1,0:T(8,128)S(1)}, u32[]{:S(2)}, u32[]{:S(2)}) collective-permute-start(f32[256,128]{1,0:T(8,128)S(1)} %collective-permute-done.7.refs_2_), channel_id=1, source_target_pairs={{0,16},{8,24},{16,0},{24,8},{1,17},{9,25},{17,1},{25,9},{2,18},{10... | collective-permute-start | bytes 393224 | tf_op jit(solution)/shard_map/ppermute | solution.py:77
  31.8 5.0 %collective-permute-start.12 = (f32[256,128]{1,0:T(8,128)S(1)}, f32[256,128]{1,0:T(8,128)S(1)}, u32[]{:S(2)}, u32[]{:S(2)}) collective-permute-start(f32[256,128]{1,0:T(8,128)S(1)} %collective-permute-done.10.refs_5_), channel_id=1, source_target_pairs={{0,8},{8,0},{16,24},{24,16},{1,9},{9,1},{17,25},{25,17},{2,10},{10... | collective-permute-start | bytes 393224 | tf_op jit(solution)/shard_map/ppermute | solution.py:78
  36.8 9.2 %copy-start = (f32[1,1,512,512]{3,2,1,0:T(8,128)S(1)}, f32[1,1,512,512]{3,2,1,0:T(8,128)}, u32[]{:S(2)}) copy-start(f32[1,1,512,512]{3,2,1,0:T(8,128)} %param.8) | copy-start | bytes 3145732
  37.6 7.5 %collective-permute-start.13 = (f32[2,80,128]{2,1,0:T(8,128)S(1)}, f32[2,80,128]{2,1,0:T(8,128)S(1)}, u32[]{:S(2)}, u32[]{:S(2)}) collective-permute-start(f32[2,80,128]{2,1,0:T(8,128)S(1)} %get-tuple-element.43), channel_id=1, source_target_pairs={{0,7},{1,6},{2,5},{3,4},{4,3},{5,2},{6,1},{7,0},{8,15},{9,14},{10,... | collective-permute-start | bytes 245768 | tf_op jit(solution)/shard_map/ppermute | solution.py:394
  37.7 6.2 %collective-permute-start.19 = (f32[1,80,128]{2,1,0:T(8,128)S(1)}, f32[1,80,128]{2,1,0:T(8,128)S(1)}, u32[]{:S(2)}, u32[]{:S(2)}) collective-permute-start(f32[1,80,128]{2,1,0:T(8,128)S(1)} %get-tuple-element.49), channel_id=1, source_target_pairs={{0,1},{1,0},{2,3},{3,2},{4,5},{5,4},{6,7},{7,6},{8,9},{9,8},{10,11... | collective-permute-start | bytes 122888 | tf_op jit(solution)/shard_map/ppermute | solution.py:394
  40.9 7.2 %collective-permute-start.14 = (f32[2,80,128]{2,1,0:T(8,128)S(1)}, f32[2,80,128]{2,1,0:T(8,128)S(1)}, u32[]{:S(2)}, u32[]{:S(2)}) collective-permute-start(f32[2,80,128]{2,1,0:T(8,128)S(1)} %get-tuple-element.44), channel_id=1, source_target_pairs={{0,6},{1,7},{2,4},{3,5},{4,2},{5,3},{6,0},{7,1},{8,14},{9,15},{10,... | collective-permute-start | bytes 245768 | tf_op jit(solution)/shard_map/ppermute | solution.py:394
  41.6 10.9 %collective-permute-start.15 = (f32[2,80,128]{2,1,0:T(8,128)S(1)}, f32[2,80,128]{2,1,0:T(8,128)S(1)}, u32[]{:S(2)}, u32[]{:S(2)}) collective-permute-start(f32[2,80,128]{2,1,0:T(8,128)S(1)} %get-tuple-element.45), channel_id=1, source_target_pairs={{0,5},{1,4},{2,7},{3,6},{4,1},{5,0},{6,3},{7,2},{8,13},{9,12},{10,... | collective-permute-start | bytes 245768 | tf_op jit(solution)/shard_map/ppermute | solution.py:394
  41.6 12.6 %collective-permute-start.16 = (f32[2,80,128]{2,1,0:T(8,128)S(1)}, f32[2,80,128]{2,1,0:T(8,128)S(1)}, u32[]{:S(2)}, u32[]{:S(2)}) collective-permute-start(f32[2,80,128]{2,1,0:T(8,128)S(1)} %get-tuple-element.46), channel_id=1, source_target_pairs={{0,4},{1,5},{2,6},{3,7},{4,0},{5,1},{6,2},{7,3},{8,12},{9,13},{10,... | collective-permute-start | bytes 245768 | tf_op jit(solution)/shard_map/ppermute | solution.py:394
  43.8 10.4 %collective-permute-start.17 = (f32[2,80,128]{2,1,0:T(8,128)S(1)}, f32[2,80,128]{2,1,0:T(8,128)S(1)}, u32[]{:S(2)}, u32[]{:S(2)}) collective-permute-start(f32[2,80,128]{2,1,0:T(8,128)S(1)} %get-tuple-element.47), channel_id=1, source_target_pairs={{0,3},{1,2},{2,1},{3,0},{4,7},{5,6},{6,5},{7,4},{8,11},{9,10},{10,... | collective-permute-start | bytes 245768 | tf_op jit(solution)/shard_map/ppermute | solution.py:394
  45.0 9.4 %collective-permute-start.18 = (f32[2,80,128]{2,1,0:T(8,128)S(1)}, f32[2,80,128]{2,1,0:T(8,128)S(1)}, u32[]{:S(2)}, u32[]{:S(2)}) collective-permute-start(f32[2,80,128]{2,1,0:T(8,128)S(1)} %get-tuple-element.48), channel_id=1, source_target_pairs={{0,2},{1,3},{2,0},{3,1},{4,6},{5,7},{6,4},{7,5},{8,10},{9,11},{10,... | collective-permute-start | bytes 245768 | tf_op jit(solution)/shard_map/ppermute | solution.py:394
  (1 other events, 8.3 us)

commit v7 on v6

--- a/solution.py
+++ b/solution.py
@@ -65,38 +65,19 @@
     return lax.rem(me + step, count), lax.rem(me + count - step, count)
 
 
-def gather_fields(halves):
-    count = lax.axis_size("kern")
-    if count == 4 and len(halves) == 2:
-        near, across = step_pairs(count, 1), step_pairs(count, 2)
-        low, high = halves
-        near_low = lax.ppermute(low, "kern", near)
-        across_high = lax.ppermute(high, "kern", across)
-        near_high = lax.ppermute(high, "kern", near)
-        across_low = lax.ppermute(low, "kern", across)
-        last_low = lax.ppermute(near_low, "kern", across)
-        last_high = lax.ppermute(across_high, "kern", near)
-        return [halves, [near_low, near_high], [across_low, across_high], [last_low, last_high]]
-    fields = [halves]
-    for step in range(1, count):
-        fields.append([lax.ppermute(half, "kern", step_pairs(count, step)) for half in halves])
-    return fields
+def exchange(values, axis):
+    count = lax.axis_size(axis)
+    arrived = [values[0]] * count
+    for step in range(count - 1, 0, -1):
+        arrived[step] = lax.ppermute(values[step], axis, step_pairs(count, step))
+    return arrived
 
 
 class Message:
-    def __init__(self, count, reach, step=None, slot=None):
-        self.count, self.reach, self.step, self.slot = count, reach, step, slot
-        if slot is not None:
-            offset = slot - reach if slot < reach else slot - reach + 1
-            self.width = 1
-            self.pairs = [(source, (source - offset) % count) for source in range(count)]
-        else:
-            self.pairs = step_pairs(count, step)
-            self.width = 1
-            for source, dest in self.pairs:
-                ahead = (source - dest) % count
-                if ahead <= reach and count - ahead <= reach:
-                    self.width = 2
+    def __init__(self, count, reach, pairs, step=None, places=(0,), slot=None):
+        self.count, self.reach, self.pairs = count, reach, pairs
+        self.step, self.places, self.slot = step, places, slot
+        self.width = len(places)
 
     def slots(self, me, sending):
         if self.slot is not None:
@@ -106,17 +87,38 @@
         column, row = (me, dest) if sending else (source, me)
         ahead = lax.rem(column - row + count, count)
         first = jnp.where(ahead <= reach, ahead + reach - 1, ahead - count + reach)
-        if self.width == 1:
-            return [(first, True)]
         both = jnp.logical_and(ahead <= reach, count - ahead <= reach)
-        return [(first, True), (jnp.where(both, ahead - count + reach, first), both)]
-
-
-def messages_of(count, slots):
+        second = jnp.where(both, ahead - count + reach, first)
+        return [((first, True), (second, both))[place] for place in self.places]
+
+
+def step_messages(count, reach, step):
+    pairs = step_pairs(count, step)
+    doubles = []
+    for source, dest in pairs:
+        ahead = (source - dest) % count
+        if ahead <= reach and count - ahead <= reach:
+            doubles.append((source, dest))
+    if not doubles:
+        return [Message(count, reach, pairs, step)]
+    if len(doubles) < len(pairs) and step >= count // 2:
+        return [Message(count, reach, pairs, step), Message(count, reach, doubles, step, (1,))]
+    return [Message(count, reach, pairs, step, (0, 1))]
+
+
+def message_sets_of(count, slots):
     reach = slots // 2
     if reach < count <= 2 * reach:
-        return [Message(count, reach, step=step) for step in range(count - 1, 0, -1)]
-    return [Message(count, reach, slot=slot) for slot in range(slots)]
+        sets = [[], []]
+        for step in range(count - 1, 0, -1):
+            sets[step < count // 2] += step_messages(count, reach, step)
+        return sets
+    messages = []
+    for slot in range(slots):
+        offset = slot - reach if slot < reach else slot - reach + 1
+        pairs = [(source, (source - offset) % count) for source in range(count)]
+        messages.append(Message(count, reach, pairs, slot=slot))
+    return [messages]
 
 
 def chunks_of(messages, most=4):
@@ -198,22 +200,14 @@
     return got[: len(messages)], got[len(messages)], got[-1] if fresh else cols
 
 
-def next_coeff_kernel(message_sets, halves, *refs):
-    count = lax.axis_size("kern")
-    fields = refs[: count * halves]
-    weights_ref = refs[count * halves]
-    splits = refs[count * halves + 1 : count * halves + 1 + len(message_sets)]
-    outs, cols_ref = refs[count * halves + 1 + len(message_sets) : -1], refs[-1]
+def next_coeff_kernel(message_sets, groups, *refs):
+    parts, refs = refs[:groups], refs[groups:]
+    splits, outs, cols_ref = refs[: len(message_sets)], refs[len(message_sets) : -1], refs[-1]
+    part = parts[0].shape[0]
     me = lax.axis_index("kern")
-    part = fields[0].shape[0]
-    for half in range(halves):
-        rows_of = pl.ds(half * part, part)
-        total = None
-        for step in range(count):
-            source = partner(me, step, count)[1]
-            term = fields[step * halves + half][...] * weights_ref[source, rows_of]
-            total = term if total is None else total + term
-        cols_ref[rows_of] = total
+    for at in range(groups):
+        source = partner(me, at, groups)[1]
+        cols_ref[pl.ds(pl.multiple_of(source * part, part), part)] = parts[at][...]
     both = side_by_side(cols_ref[...])
     rank = outs[0].shape[1]
     done = 0
@@ -225,22 +219,21 @@
             base = chunk_coefficients(split_ref, base, chunk, messages, rank, both, here)
 
 
-def next_coefficients(fields, weights, splits, message_sets, rank):
-    halves = len(fields[0])
-    part, width = fields[0][0].shape
-    size = part * halves
+def next_coefficients(parts, splits, message_sets, rank):
+    groups = len(parts)
+    part, width = parts[0].shape
+    size = part * groups
     outs = [struct(message.width, rank, width) for group in message_sets for message in group]
     outs.append(struct(size, width))
     total = sum(split_right.shape[0] for split_right in splits)
-    flat = [half for field in fields for half in field]
     got = call(
-        functools.partial(next_coeff_kernel, message_sets, halves),
+        functools.partial(next_coeff_kernel, message_sets, groups),
         outs,
         [in_vmem] * len(outs),
-        [in_vmem] * (len(flat) + 1 + len(splits)),
+        [in_vmem] * (groups + len(splits)),
         flops=4 * total * size * width,
         moved=2 * total * (size + width),
-    )(*flat, weights, *splits)
+    )(*parts, *splits)
     return got[:-1], got[-1]
 
 
@@ -276,19 +269,21 @@
     ):
         copies.append(pltpu.make_async_copy(source, target, sems.at[at]))
         copies[-1].start()
-    own = table_ref[lax.axis_index("kern")]
-    groups, entries = own.shape
-    size = index_ref.shape[1]
-    hot = (lax.broadcasted_iota(jnp.int32, (entries, size), 0) == index_ref[...]).astype(f32)
-    weights = jnp.dot(own, hot, precision=lax.Precision.HIGHEST, preferred_element_type=f32)
+    entries = table_ref.shape[1]
+    part = index_ref.shape[1]
+    index = index_ref[pl.ds(lax.axis_index("kern"), 1)]
+    hot = (lax.broadcasted_iota(jnp.int32, (entries, part), 0) == index).astype(f32)
+    weights = jnp.dot(
+        table_ref[...], hot, precision=lax.Precision.HIGHEST, preferred_element_type=f32
+    )
     width = weights_ref.shape[2]
-    for b in range(groups):
-        weights_ref[b] = jnp.broadcast_to(weights[b : b + 1], (width, size)).T
+    for at in range(weights_ref.shape[0]):
+        weights_ref[at] = jnp.broadcast_to(weights[at : at + 1], (width, part)).T
     copies[0].wait()
     copies[1].wait()
     diag_out[...] = times_diag(diag_ref, cols_ref)
     copies[2].wait()
-    total = left_ref.shape[0]
+    total, size = left_ref.shape
     step = 128 if total % 128 == 0 else total
     part = size // halves
     for at in range(0, total, step):
@@ -304,13 +299,13 @@
 def prepare(diag_tile, cols, left_rows, table, index, halves):
     size, width = cols.shape
     total = left_rows.shape[0]
-    groups = table.shape[0]
+    part = index.shape[1]
     return call(
         functools.partial(prepare_kernel, halves),
         [
             struct(size, width),
             struct(2 * size, total, dtype=bf16),
-            struct(groups, size, width),
+            struct(table.shape[0], part, width),
         ],
         [in_vmem] * 3,
         [in_hbm] * 3 + [in_vmem] * 2,
@@ -325,14 +320,11 @@
     )(to_hbm(diag_tile), to_hbm(cols), to_hbm(left_rows), table, index)
 
 
-def row_kernel(messages, halves, final, offs_ref, ranks_ref, *refs):
+def row_kernel(messages, halves, groups, offs_ref, ranks_ref, *refs):
     gots = refs[: len(messages)]
     left_ref, diag_ref = refs[len(messages) : len(messages) + 2]
-    outs = refs[len(messages) + 2 :]
-    if final:
-        outs, (picked, term_of, stage, sems) = outs[:-4], outs[-4:]
-    else:
-        outs, (picked, term_of) = outs[:-2], outs[-2:]
+    refs = refs[len(messages) + 2 :]
+    outs, (picked, term_of, stage, sems) = refs[:groups], refs[groups:]
     terms = offs_ref.shape[1]
     rank, width = gots[0].shape[1:]
     slots = term_of.shape[0]
@@ -361,30 +353,62 @@
         rows_of = pl.ds(half * part, part)
         got = fold(dot(left_ref[pl.ds(2 * half * part, 2 * part)], both))
         total = got[:part] + got[part:] + diag_ref[rows_of]
-        if final:
-            stage[rows_of] = total
+        stage[rows_of] = total
+        if groups == 1:
             sent.append(
                 pltpu.make_async_copy(stage.at[rows_of], outs[0].at[rows_of], sems.at[half])
             )
             sent[-1].start()
-        else:
-            outs[half][...] = total
     for copy in sent:
         copy.wait()
-
-
-def rows(offsets, ranks, gots, messages, left_split, diag_part, slots, halves, final):
+    if groups > 1:
+        part = stage.shape[0] // groups
+        own = lax.axis_index("kern")
+        for at in range(groups):
+            dest = partner(own, at, groups)[0]
+            outs[at][...] = stage[pl.ds(pl.multiple_of(dest * part, part), part)]
+
+
+def mix_kernel(groups, *refs):
+    fields, weights_ref, outs = refs[:groups], refs[groups], refs[groups + 1 :]
+    me = lax.axis_index("kern")
+    for at in range(groups):
+        base = partner(me, at, groups)[0] * groups
+        total = None
+        for b in range(groups):
+            term = fields[b][...] * weights_ref[base + partner(me, b, groups)[1]]
+            total = term if total is None else total + term
+        outs[at][...] = total
+
+
+def mix(fields, weights):
+    groups = len(fields)
+    part, width = fields[0].shape
+    return call(
+        functools.partial(mix_kernel, groups),
+        [struct(part, width)] * groups,
+        [in_vmem] * groups,
+        [in_vmem] * (groups + 1),
+        flops=2 * groups * groups * part * width,
+        moved=8 * groups * part * width,
+    )(*fields, weights)
+
+
+def rows(offsets, ranks, gots, messages, left_split, diag_part, slots, halves, groups):
     size, width = diag_part.shape
     total = left_split.shape[1]
-    scratch = [pltpu.VMEM((total, width), f32), pltpu.SMEM((slots,), jnp.int32)]
-    if final:
-        scratch += [pltpu.VMEM((size, width), f32), pltpu.SemaphoreType.DMA((halves,))]
+    last = groups == 1
     return call(
-        functools.partial(row_kernel, messages, halves, final),
-        pltpu.HBM((size, width), f32) if final else [struct(size // halves, width)] * halves,
-        in_hbm if final else [in_vmem] * halves,
+        functools.partial(row_kernel, messages, halves, groups),
+        pltpu.HBM((size, width), f32) if last else [struct(size // groups, width)] * groups,
+        in_hbm if last else [in_vmem] * groups,
         [in_smem, in_smem] + [in_vmem] * (len(messages) + 2),
-        scratch,
+        [
+            pltpu.VMEM((total, width), f32),
+            pltpu.SMEM((slots,), jnp.int32),
+            pltpu.VMEM((size, width), f32),
+            pltpu.SemaphoreType.DMA((halves,)),
+        ],
         flops=8 * total * size * width,
         moved=4 * total * (size + width),
     )(offsets, ranks, *gots, left_split, diag_part)
@@ -411,25 +435,25 @@
     slots, rank, size = right_tile.shape
     halves = 2 if size % 32 == 0 else 1
     left_rows = left_factors.reshape(-1, size)
-    table = mixing.transpose(1, 2, 0)
-    index = block_index[None]
+    groups = lax.axis_size("kern")
+    table = mixing.reshape(mixing.shape[0], groups * groups).T
+    index = block_index.reshape(groups, size // groups)
     cols = rhs_field[0]
 
-    messages = messages_of(lax.axis_size("tile"), slots)
-    far = (len(messages) + 1) // 2
-    message_sets = [messages[:far], messages[far:]]
+    message_sets = message_sets_of(lax.axis_size("tile"), slots)
+    messages = [message for group in message_sets for message in group]
     gots, splits, given = [], [], cols
     for group in message_sets:
         coeffs, split_right, given = first_coefficients(given, right_tile, group, not splits)
         gots += deliver(coeffs, group)
         splits.append(split_right)
     diag_part, left_split, weights = prepare(diag_tile, cols, left_rows, table, index, halves)
-    first = rows(offsets, ranks, gots, messages, left_split, diag_part, slots, halves, False)
-    fields = gather_fields(first)
-    coeffs, cols = next_coefficients(fields, weights, splits, message_sets, rank)
+    first = rows(offsets, ranks, gots, messages, left_split, diag_part, slots, halves, groups)
+    mixed = exchange(mix(exchange(first, "kern"), weights), "kern")
+    coeffs, cols = next_coefficients(mixed, splits, message_sets, rank)
     gots = deliver(coeffs, messages)
     diag_part = diagonal(diag_tile, cols)
-    return rows(offsets, ranks, gots, messages, left_split, diag_part, slots, halves, True)[None]
+    return rows(offsets, ranks, gots, messages, left_split, diag_part, slots, halves, 1)[None]
 
 
 def solution(mesh):

time: 56.6 us -> 65.4 us (1.16)
  starting transfers between devices: 25.3 us -> 32.6 us
  waiting for transfers between devices: 20.1 us -> 21.2 us
    ppermute x14 -> x16, starting transfers between devices: 18.2 us -> 25.5 us  [deliver(): lax.ppermute(sent, 'tile', message.pairs)]
    ppermute x6, waiting for transfers between devices: 6.02 us -> 7.4 us  [exchange(): arrived[step] = lax.ppermute(values[step], axis, step_pairs(count, step))]
    ppermute x14 -> x16, waiting for transfers between devices: 14.1 us -> 13.8 us  [deliver(): lax.ppermute(sent, 'tile', message.pairs)]
    pallas_call x3 -> x4, Pallas kernels: 4.15 us -> 4.31 us  [the longest x2 3.43 us: rows(): call(functools.partial(row_kernel, messages, halves, groups), pltpu.HBM((...]
  transfers between devices with their start and end apart: 20 -> 22, of which waited for: 12 -> 13; matrix products, arithmetic and copies ran while one was open for 0% -> 0% of each run, Pallas kernels for 8% -> 7%
where the time goes in v7:
time: 65.4 us; the launch traced here: 65.2 us
  starting transfers between devices  32.6 us (50%)
  waiting for transfers between devices  21.2 us (32%)
  Pallas kernels  11.1 us (17%)
    ppermute x16, starting transfers between devices, deliver(): lax.ppermute(sent, 'tile', message.pairs)  25.5 us
    ppermute x16, waiting for transfers between devices, deliver(): lax.ppermute(sent, 'tile', message.pairs)  13.8 us
    ppermute x6, waiting for transfers between devices, exchange(): arrived[step] = lax.ppermute(values[step], axis, step_pairs(count, step))  7.4 us
    ppermute x6, starting transfers between devices, exchange(): arrived[step] = lax.ppermute(values[step], axis, step_pairs(count, step))  7.11 us
    pallas_call x2, Pallas kernels, first_coefficients(): call(functools.partial(first_coeff_kernel, messages, fresh), outs, [in_vm...  4.16 us
    pallas_call x2, Pallas kernels, rows(): call(functools.partial(row_kernel, messages, halves, groups), pltpu.HBM((...  3.43 us
    pallas_call x1, Pallas kernels, prepare(): call(functools.partial(prepare_kernel, halves), [struct(size, width), str...  2.2 us
  transfers between devices with their start and end apart: 22, of which 13 were waited for; matrix products, arithmetic and copies ran while one was open for 0% of the time, Pallas kernels for 7%

profile of v7, /device:TPU:0, one launch (start us, length us, event | category | flops | bytes accessed | tf_op | source)
XLA Modules:
  0.0 65.2 jit_solution(17384539502052557549)
XLA Ops:
  0.0 2.3 %shard_map.82 = (f32[1,80,128]{2,1,0:T(8,128)S(1)}, f32[1,80,128]{2,1,0:T(8,128)S(1)}, f32[2,80,128]{2,1,0:T(8,128)S(1)}, f32[2,80,128]{2,1,0:T(8,128)S(1)}, f32...) custom-call(f32[512,128]{1,0:T(8,128)} %bitcast.22, f32[12,80,512]{2,1,0:T(8,128)} %bitcast.19), custom_call_target="tpu_custom_call" | custom-call | flops 335544320 | bytes 2949120 | tf_op jit(solution)/shard_map/pallas_call | solution.py:191
  2.4 4.6 %collective-permute-start = (f32[1,80,128]{2,1,0:T(8,128)S(1)}, f32[1,80,128]{2,1,0:T(8,128)S(1)}, u32[]{:S(2)}, u32[]{:S(2)}) collective-permute-start(f32[1,80,128]{2,1,0:T(8,128)S(1)} %get-tuple-element.36), channel_id=1, source_target_pairs={{0,7},{1,6},{2,5},{3,4},{4,3},{5,2},{6,1},{7,0},{8,15},{9,14},{10,... | collective-permute-start | bytes 122888 | tf_op jit(solution)/shard_map/ppermute | solution.py:418
  7.6 1.8 %shard_map.83 = (f32[2,80,128]{2,1,0:T(8,128)S(1)}, f32[2,80,128]{2,1,0:T(8,128)S(1)}, f32[1,80,128]{2,1,0:T(8,128)S(1)}, bf16[800,512]{1,0:T(8,128)(2,1)S(1)}) custom-call(bf16[512,256]{1,0:T(8,128)(2,1)S(1)} %get-tuple-element.41.cols_ref, f32[12,80,512]{2,1,0:T(8,128)} %bitcast.20), custom_call_target="tpu_custom_call" | custom-call | flops 209715200 | bytes 1843200 | tf_op jit(solution)/shard_map/pallas_call | solution.py:191
  9.4 2.0 %collective-permute-start.7 = (f32[1,80,128]{2,1,0:T(8,128)S(1)}, f32[1,80,128]{2,1,0:T(8,128)S(1)}, u32[]{:S(2)}, u32[]{:S(2)}) collective-permute-start(f32[1,80,128]{2,1,0:T(8,128)S(1)} %get-tuple-element.44), channel_id=1, source_target_pairs={{0,1},{1,0},{2,3},{3,2},{4,5},{5,4},{6,7},{7,6},{8,9},{9,8},{10,11... | collective-permute-start | bytes 122888 | tf_op jit(solution)/shard_map/ppermute | solution.py:418
  11.4 3.5 %collective-permute-start.2 = (f32[2,80,128]{2,1,0:T(8,128)S(1)}, f32[2,80,128]{2,1,0:T(8,128)S(1)}, u32[]{:S(2)}, u32[]{:S(2)}) collective-permute-start(f32[2,80,128]{2,1,0:T(8,128)S(1)} %get-tuple-element.38), channel_id=1, source_target_pairs={{0,6},{1,7},{2,4},{3,5},{4,2},{5,3},{6,0},{7,1},{8,14},{9,15},{10,... | collective-permute-start | bytes 245768 | tf_op jit(solution)/shard_map/ppermute | solution.py:418
  14.9 2.7 %collective-permute-start.4 = (f32[2,80,128]{2,1,0:T(8,128)S(1)}, f32[2,80,128]{2,1,0:T(8,128)S(1)}, u32[]{:S(2)}, u32[]{:S(2)}) collective-permute-start(f32[2,80,128]{2,1,0:T(8,128)S(1)} %get-tuple-element.40), channel_id=1, source_target_pairs={{0,4},{1,5},{2,6},{3,7},{4,0},{5,1},{6,2},{7,3},{8,12},{9,13},{10,... | collective-permute-start | bytes 245768 | tf_op jit(solution)/shard_map/ppermute | solution.py:418
  17.6 1.7 %collective-permute-start.6 = (f32[2,80,128]{2,1,0:T(8,128)S(1)}, f32[2,80,128]{2,1,0:T(8,128)S(1)}, u32[]{:S(2)}, u32[]{:S(2)}) collective-permute-start(f32[2,80,128]{2,1,0:T(8,128)S(1)} %get-tuple-element.43), channel_id=1, source_target_pairs={{0,2},{1,3},{2,0},{3,1},{4,6},{5,7},{6,4},{7,5},{8,10},{9,11},{10,... | collective-permute-start | bytes 245768 | tf_op jit(solution)/shard_map/ppermute | solution.py:418
  19.3 2.2 %shard_map.84 = (f32[512,128]{1,0:T(8,128)S(1)}, bf16[1024,640]{1,0:T(8,128)(2,1)S(1)}, f32[16,128,128]{2,1,0:T(8,128)S(1)}) custom-call(f32[512,512]{1,0:T(8,128)} %bitcast.11, f32[512,128]{1,0:T(8,128)} %bitcast.23, f32[640,512]{1,0:T(8,128)} %bitcast.21, f32[16,64]{1,0:T(8,128)S(1)} %bitcast.13, s32[4,128]{1,0:T(4,128)S(1)} %bitcast.14), custom_call_target="tpu_custom_call" | custom-call | flops 268435456 | bytes 4194304 | tf_op jit(solution)/shard_map/pallas_call | solution.py:303
  21.5 1.7 %collective-permute-done.3.refs_3_ = f32[2,80,128]{2,1,0:T(8,128)S(1)} collective-permute-done((f32[2,80,128]{2,1,0:T(8,128)S(1)}, f32[2,80,128]{2,1,0:T(8,128)S(1)}, u32[]{:S(2)}, u32[]{:S(2)}) %collective-permute-start.3) | collective-permute-done | bytes 81952 | tf_op jit(solution)/shard_map/ppermute | solution.py:418
  23.3 1.8 %collective-permute-done.4.refs_4_ = f32[2,80,128]{2,1,0:T(8,128)S(1)} collective-permute-done((f32[2,80,128]{2,1,0:T(8,128)S(1)}, f32[2,80,128]{2,1,0:T(8,128)S(1)}, u32[]{:S(2)}, u32[]{:S(2)}) %collective-permute-start.4) | collective-permute-done | bytes 81952 | tf_op jit(solution)/shard_map/ppermute | solution.py:418
  25.5 2.0 %collective-permute-done.6.refs_6_ = f32[2,80,128]{2,1,0:T(8,128)S(1)} collective-permute-done((f32[2,80,128]{2,1,0:T(8,128)S(1)}, f32[2,80,128]{2,1,0:T(8,128)S(1)}, u32[]{:S(2)}, u32[]{:S(2)}) %collective-permute-start.6) | collective-permute-done | bytes 81952 | tf_op jit(solution)/shard_map/ppermute | solution.py:418
  28.9 1.6 %collective-permute-start.8 = (f32[128,128]{1,0:T(8,128)S(1)}, f32[128,128]{1,0:T(8,128)S(1)}, u32[]{:S(2)}, u32[]{:S(2)}) collective-permute-start(f32[128,128]{1,0:T(8,128)S(1)} %get-tuple-element.48), channel_id=1, source_target_pairs={{0,8},{8,0},{16,24},{24,16},{1,9},{9,1},{17,25},{25,17},{2,10},{10... | collective-permute-start | bytes 196616 | tf_op jit(solution)/shard_map/ppermute | solution.py:72
  30.5 1.5 %collective-permute-start.9 = (f32[128,128]{1,0:T(8,128)S(1)}, f32[128,128]{1,0:T(8,128)S(1)}, u32[]{:S(2)}, u32[]{:S(2)}) collective-permute-start(f32[128,128]{1,0:T(8,128)S(1)} %get-tuple-element.49), channel_id=1, source_target_pairs={{0,16},{8,24},{16,0},{24,8},{1,17},{9,25},{17,1},{25,9},{2,18},{10... | collective-permute-start | bytes 196616 | tf_op jit(solution)/shard_map/ppermute | solution.py:72
  33.3 1.5 %collective-permute-done.9.refs_2_ = f32[128,128]{1,0:T(8,128)S(1)} collective-permute-done((f32[128,128]{1,0:T(8,128)S(1)}, f32[128,128]{1,0:T(8,128)S(1)}, u32[]{:S(2)}, u32[]{:S(2)}) %collective-permute-start.9) | collective-permute-done | bytes 65568 | tf_op jit(solution)/shard_map/ppermute | solution.py:72
  34.8 2.4 %collective-permute-done.10.refs_3_ = f32[128,128]{1,0:T(8,128)S(1)} collective-permute-done((f32[128,128]{1,0:T(8,128)S(1)}, f32[128,128]{1,0:T(8,128)S(1)}, u32[]{:S(2)}, u32[]{:S(2)}) %collective-permute-start.10) | collective-permute-done | bytes 65568 | tf_op jit(solution)/shard_map/ppermute | solution.py:72
  38.4 2.5 %collective-permute-start.13 = (f32[128,128]{1,0:T(8,128)S(1)}, f32[128,128]{1,0:T(8,128)S(1)}, u32[]{:S(2)}, u32[]{:S(2)}) collective-permute-start(f32[128,128]{1,0:T(8,128)S(1)} %get-tuple-element.55), channel_id=1, source_target_pairs={{0,24},{8,16},{16,8},{24,0},{1,25},{9,17},{17,9},{25,1},{2,26},{10... | collective-permute-start | bytes 196616 | tf_op jit(solution)/shard_map/ppermute | solution.py:72
  45.1 1.8 %collective-permute-start.21 = (f32[1,80,128]{2,1,0:T(8,128)S(1)}, f32[1,80,128]{2,1,0:T(8,128)S(1)}, u32[]{:S(2)}, u32[]{:S(2)}) collective-permute-start(f32[1,80,128]{2,1,0:T(8,128)S(1)} %get-tuple-element.65), channel_id=1, source_target_pairs={{0,1},{1,0},{2,3},{3,2},{4,5},{5,4},{6,7},{7,6},{8,9},{9,8},{10,11... | collective-permute-start | bytes 122888 | tf_op jit(solution)/shard_map/ppermute | solution.py:418
  46.9 3.5 %collective-permute-start.16 = (f32[2,80,128]{2,1,0:T(8,128)S(1)}, f32[2,80,128]{2,1,0:T(8,128)S(1)}, u32[]{:S(2)}, u32[]{:S(2)}) collective-permute-start(f32[2,80,128]{2,1,0:T(8,128)S(1)} %get-tuple-element.60), channel_id=1, source_target_pairs={{0,6},{1,7},{2,4},{3,5},{4,2},{5,3},{6,0},{7,1},{8,14},{9,15},{10,... | collective-permute-start | bytes 245768 | tf_op jit(solution)/shard_map/ppermute | solution.py:418
  50.4 2.7 %collective-permute-start.18 = (f32[2,80,128]{2,1,0:T(8,128)S(1)}, f32[2,80,128]{2,1,0:T(8,128)S(1)}, u32[]{:S(2)}, u32[]{:S(2)}) collective-permute-start(f32[2,80,128]{2,1,0:T(8,128)S(1)} %get-tuple-element.62), channel_id=1, source_target_pairs={{0,4},{1,5},{2,6},{3,7},{4,0},{5,1},{6,2},{7,3},{8,12},{9,13},{10,... | collective-permute-start | bytes 245768 | tf_op jit(solution)/shard_map/ppermute | solution.py:418
  53.1 1.7 %collective-permute-start.20 = (f32[2,80,128]{2,1,0:T(8,128)S(1)}, f32[2,80,128]{2,1,0:T(8,128)S(1)}, u32[]{:S(2)}, u32[]{:S(2)}) collective-permute-start(f32[2,80,128]{2,1,0:T(8,128)S(1)} %get-tuple-element.64), channel_id=1, source_target_pairs={{0,2},{1,3},{2,0},{3,1},{4,6},{5,7},{6,4},{7,5},{8,10},{9,11},{10,... | collective-permute-start | bytes 245768 | tf_op jit(solution)/shard_map/ppermute | solution.py:418
  55.3 4.1 %collective-permute-done.17.refs_3_ = f32[2,80,128]{2,1,0:T(8,128)S(1)} collective-permute-done((f32[2,80,128]{2,1,0:T(8,128)S(1)}, f32[2,80,128]{2,1,0:T(8,128)S(1)}, u32[]{:S(2)}, u32[]{:S(2)}) %collective-permute-start.17) | collective-permute-done | bytes 81952 | tf_op jit(solution)/shard_map/ppermute | solution.py:418
  59.4 1.9 %collective-permute-done.18.refs_4_ = f32[2,80,128]{2,1,0:T(8,128)S(1)} collective-permute-done((f32[2,80,128]{2,1,0:T(8,128)S(1)}, f32[2,80,128]{2,1,0:T(8,128)S(1)}, u32[]{:S(2)}, u32[]{:S(2)}) %collective-permute-start.18) | collective-permute-done | bytes 81952 | tf_op jit(solution)/shard_map/ppermute | solution.py:418
  61.3 1.8 %collective-permute-done.20.refs_6_ = f32[2,80,128]{2,1,0:T(8,128)S(1)} collective-permute-done((f32[2,80,128]{2,1,0:T(8,128)S(1)}, f32[2,80,128]{2,1,0:T(8,128)S(1)}, u32[]{:S(2)}, u32[]{:S(2)}) %collective-permute-start.20) | collective-permute-done | bytes 81952 | tf_op jit(solution)/shard_map/ppermute | solution.py:418
  63.1 2.0 %shard_map.89 = f32[512,128]{1,0:T(8,128)} custom-call(s32[1,8]{1,0:T(1,128)S(1)} %bitcast.16, s32[1,8]{1,0:T(1,128)S(1)} %bitcast.18, f32[1,80,128]{2,1,0:T(8,128)S(1)} %collective-permute-done.14.refs_0_, f32[1,80,128]{2,1,0:T(8,128)S(1)} %collective-permute-done.15.refs_1_, f32[2,80,128]{2,1,0:T(8,128)S(1)} %collective-permute-done.16.refs_2_, ...), custom_call_target="tpu_custom_call" | custom-call | flops 335544320 | bytes 1638400 | tf_op jit(solution)/shard_map/pallas_call | solution.py:401
  (38 shorter events, 9.6 us)
Async XLA Ops:
  2.3 17.0 %copy-start.1 = (f32[64,4,4]{0,2,1:T(4,128)S(1)}, f32[64,4,4]{0,2,1:T(4,128)}, u32[]{:S(2)}) copy-start(f32[64,4,4]{0,2,1:T(4,128)} %param.13) | copy-start | bytes 12292
  2.4 12.6 %collective-permute-start = (f32[1,80,128]{2,1,0:T(8,128)S(1)}, f32[1,80,128]{2,1,0:T(8,128)S(1)}, u32[]{:S(2)}, u32[]{:S(2)}) collective-permute-start(f32[1,80,128]{2,1,0:T(8,128)S(1)} %get-tuple-element.36), channel_id=1, source_target_pairs={{0,7},{1,6},{2,5},{3,4},{4,3},{5,2},{6,1},{7,0},{8,15},{9,14},{10,... | collective-permute-start | bytes 122888 | tf_op jit(solution)/shard_map/ppermute | solution.py:418
  6.9 10.7 %collective-permute-start.1 = (f32[1,80,128]{2,1,0:T(8,128)S(1)}, f32[1,80,128]{2,1,0:T(8,128)S(1)}, u32[]{:S(2)}, u32[]{:S(2)}) collective-permute-start(f32[1,80,128]{2,1,0:T(8,128)S(1)} %get-tuple-element.37), channel_id=1, source_target_pairs={{1,6},{2,5},{5,2},{6,1},{9,14},{10,13},{13,10},{14,9},{17,22},{18,... | collective-permute-start | bytes 122888 | tf_op jit(solution)/shard_map/ppermute | solution.py:418
  9.4 8.2 %collective-permute-start.7 = (f32[1,80,128]{2,1,0:T(8,128)S(1)}, f32[1,80,128]{2,1,0:T(8,128)S(1)}, u32[]{:S(2)}, u32[]{:S(2)}) collective-permute-start(f32[1,80,128]{2,1,0:T(8,128)S(1)} %get-tuple-element.44), channel_id=1, source_target_pairs={{0,1},{1,0},{2,3},{3,2},{4,5},{5,4},{6,7},{7,6},{8,9},{9,8},{10,11... | collective-permute-start | bytes 122888 | tf_op jit(solution)/shard_map/ppermute | solution.py:418
  11.4 10.1 %collective-permute-start.2 = (f32[2,80,128]{2,1,0:T(8,128)S(1)}, f32[2,80,128]{2,1,0:T(8,128)S(1)}, u32[]{:S(2)}, u32[]{:S(2)}) collective-permute-start(f32[2,80,128]{2,1,0:T(8,128)S(1)} %get-tuple-element.38), channel_id=1, source_target_pairs={{0,6},{1,7},{2,4},{3,5},{4,2},{5,3},{6,0},{7,1},{8,14},{9,15},{10,... | collective-permute-start | bytes 245768 | tf_op jit(solution)/shard_map/ppermute | solution.py:418
  14.9 8.4 %collective-permute-start.3 = (f32[2,80,128]{2,1,0:T(8,128)S(1)}, f32[2,80,128]{2,1,0:T(8,128)S(1)}, u32[]{:S(2)}, u32[]{:S(2)}) collective-permute-start(f32[2,80,128]{2,1,0:T(8,128)S(1)} %get-tuple-element.39), channel_id=1, source_target_pairs={{0,5},{1,4},{2,7},{3,6},{4,1},{5,0},{6,3},{7,2},{8,13},{9,12},{10,... | collective-permute-start | bytes 245768 | tf_op jit(solution)/shard_map/ppermute | solution.py:418
  14.9 10.2 %collective-permute-start.4 = (f32[2,80,128]{2,1,0:T(8,128)S(1)}, f32[2,80,128]{2,1,0:T(8,128)S(1)}, u32[]{:S(2)}, u32[]{:S(2)}) collective-permute-start(f32[2,80,128]{2,1,0:T(8,128)S(1)} %get-tuple-element.40), channel_id=1, source_target_pairs={{0,4},{1,5},{2,6},{3,7},{4,0},{5,1},{6,2},{7,3},{8,12},{9,13},{10,... | collective-permute-start | bytes 245768 | tf_op jit(solution)/shard_map/ppermute | solution.py:418
  17.6 7.9 %collective-permute-start.5 = (f32[2,80,128]{2,1,0:T(8,128)S(1)}, f32[2,80,128]{2,1,0:T(8,128)S(1)}, u32[]{:S(2)}, u32[]{:S(2)}) collective-permute-start(f32[2,80,128]{2,1,0:T(8,128)S(1)} %get-tuple-element.42), channel_id=1, source_target_pairs={{0,3},{1,2},{2,1},{3,0},{4,7},{5,6},{6,5},{7,4},{8,11},{9,10},{10,... | collective-permute-start | bytes 245768 | tf_op jit(solution)/shard_map/ppermute | solution.py:418
  17.6 9.9 %collective-permute-start.6 = (f32[2,80,128]{2,1,0:T(8,128)S(1)}, f32[2,80,128]{2,1,0:T(8,128)S(1)}, u32[]{:S(2)}, u32[]{:S(2)}) collective-permute-start(f32[2,80,128]{2,1,0:T(8,128)S(1)} %get-tuple-element.43), channel_id=1, source_target_pairs={{0,2},{1,3},{2,0},{3,1},{4,6},{5,7},{6,4},{7,5},{8,10},{9,11},{10,... | collective-permute-start | bytes 245768 | tf_op jit(solution)/shard_map/ppermute | solution.py:418
  28.9 4.3 %collective-permute-start.8 = (f32[128,128]{1,0:T(8,128)S(1)}, f32[128,128]{1,0:T(8,128)S(1)}, u32[]{:S(2)}, u32[]{:S(2)}) collective-permute-start(f32[128,128]{1,0:T(8,128)S(1)} %get-tuple-element.48), channel_id=1, source_target_pairs={{0,8},{8,0},{16,24},{24,16},{1,9},{9,1},{17,25},{25,17},{2,10},{10... | collective-permute-start | bytes 196616 | tf_op jit(solution)/shard_map/ppermute | solution.py:72
  30.5 4.3 %collective-permute-start.9 = (f32[128,128]{1,0:T(8,128)S(1)}, f32[128,128]{1,0:T(8,128)S(1)}, u32[]{:S(2)}, u32[]{:S(2)}) collective-permute-start(f32[128,128]{1,0:T(8,128)S(1)} %get-tuple-element.49), channel_id=1, source_target_pairs={{0,16},{8,24},{16,0},{24,8},{1,17},{9,25},{17,1},{25,9},{2,18},{10... | collective-permute-start | bytes 196616 | tf_op jit(solution)/shard_map/ppermute | solution.py:72
  32.0 5.2 %collective-permute-start.10 = (f32[128,128]{1,0:T(8,128)S(1)}, f32[128,128]{1,0:T(8,128)S(1)}, u32[]{:S(2)}, u32[]{:S(2)}) collective-permute-start(f32[128,128]{1,0:T(8,128)S(1)} %get-tuple-element.50), channel_id=1, source_target_pairs={{0,24},{8,16},{16,8},{24,0},{1,25},{9,17},{17,9},{25,1},{2,26},{10... | collective-permute-start | bytes 196616 | tf_op jit(solution)/shard_map/ppermute | solution.py:72
  37.3 17.5 %copy-start = (f32[1,1,512,512]{3,2,1,0:T(8,128)S(1)}, f32[1,1,512,512]{3,2,1,0:T(8,128)}, u32[]{:S(2)}) copy-start(f32[1,1,512,512]{3,2,1,0:T(8,128)} %param.8) | copy-start | bytes 3145732
  37.3 4.3 %collective-permute-start.11 = (f32[128,128]{1,0:T(8,128)S(1)}, f32[128,128]{1,0:T(8,128)S(1)}, u32[]{:S(2)}, u32[]{:S(2)}) collective-permute-start(f32[128,128]{1,0:T(8,128)S(1)} %get-tuple-element.53), channel_id=1, source_target_pairs={{0,8},{8,0},{16,24},{24,16},{1,9},{9,1},{17,25},{25,17},{2,10},{10... | collective-permute-start | bytes 196616 | tf_op jit(solution)/shard_map/ppermute | solution.py:72
  37.9 4.3 %collective-permute-start.12 = (f32[128,128]{1,0:T(8,128)S(1)}, f32[128,128]{1,0:T(8,128)S(1)}, u32[]{:S(2)}, u32[]{:S(2)}) collective-permute-start(f32[128,128]{1,0:T(8,128)S(1)} %get-tuple-element.54), channel_id=1, source_target_pairs={{0,16},{8,24},{16,0},{24,8},{1,17},{9,25},{17,1},{25,9},{2,18},{10... | collective-permute-start | bytes 196616 | tf_op jit(solution)/shard_map/ppermute | solution.py:72
  38.4 5.2 %collective-permute-start.13 = (f32[128,128]{1,0:T(8,128)S(1)}, f32[128,128]{1,0:T(8,128)S(1)}, u32[]{:S(2)}, u32[]{:S(2)}) collective-permute-start(f32[128,128]{1,0:T(8,128)S(1)} %get-tuple-element.55), channel_id=1, source_target_pairs={{0,24},{8,16},{16,8},{24,0},{1,25},{9,17},{17,9},{25,1},{2,26},{10... | collective-permute-start | bytes 196616 | tf_op jit(solution)/shard_map/ppermute | solution.py:72
  44.3 6.1 %collective-permute-start.14 = (f32[1,80,128]{2,1,0:T(8,128)S(1)}, f32[1,80,128]{2,1,0:T(8,128)S(1)}, u32[]{:S(2)}, u32[]{:S(2)}) collective-permute-start(f32[1,80,128]{2,1,0:T(8,128)S(1)} %get-tuple-element.58), channel_id=1, source_target_pairs={{0,7},{1,6},{2,5},{3,4},{4,3},{5,2},{6,1},{7,0},{8,15},{9,14},{10,... | collective-permute-start | bytes 122888 | tf_op jit(solution)/shard_map/ppermute | solution.py:418
  44.4 8.7 %collective-permute-start.15 = (f32[1,80,128]{2,1,0:T(8,128)S(1)}, f32[1,80,128]{2,1,0:T(8,128)S(1)}, u32[]{:S(2)}, u32[]{:S(2)}) collective-permute-start(f32[1,80,128]{2,1,0:T(8,128)S(1)} %get-tuple-element.59), channel_id=1, source_target_pairs={{1,6},{2,5},{5,2},{6,1},{9,14},{10,13},{13,10},{14,9},{17,22},{18,... | collective-permute-start | bytes 122888 | tf_op jit(solution)/shard_map/ppermute | solution.py:418
  45.1 8.0 %collective-permute-start.21 = (f32[1,80,128]{2,1,0:T(8,128)S(1)}, f32[1,80,128]{2,1,0:T(8,128)S(1)}, u32[]{:S(2)}, u32[]{:S(2)}) collective-permute-start(f32[1,80,128]{2,1,0:T(8,128)S(1)} %get-tuple-element.65), channel_id=1, source_target_pairs={{0,1},{1,0},{2,3},{3,2},{4,5},{5,4},{6,7},{7,6},{8,9},{9,8},{10,11... | collective-permute-start | bytes 122888 | tf_op jit(solution)/shard_map/ppermute | solution.py:418
  46.9 8.3 %collective-permute-start.16 = (f32[2,80,128]{2,1,0:T(8,128)S(1)}, f32[2,80,128]{2,1,0:T(8,128)S(1)}, u32[]{:S(2)}, u32[]{:S(2)}) collective-permute-start(f32[2,80,128]{2,1,0:T(8,128)S(1)} %get-tuple-element.60), channel_id=1, source_target_pairs={{0,6},{1,7},{2,4},{3,5},{4,2},{5,3},{6,0},{7,1},{8,14},{9,15},{10,... | collective-permute-start | bytes 245768 | tf_op jit(solution)/shard_map/ppermute | solution.py:418
  50.4 9.0 %collective-permute-start.17 = (f32[2,80,128]{2,1,0:T(8,128)S(1)}, f32[2,80,128]{2,1,0:T(8,128)S(1)}, u32[]{:S(2)}, u32[]{:S(2)}) collective-permute-start(f32[2,80,128]{2,1,0:T(8,128)S(1)} %get-tuple-element.61), channel_id=1, source_target_pairs={{0,5},{1,4},{2,7},{3,6},{4,1},{5,0},{6,3},{7,2},{8,13},{9,12},{10,... | collective-permute-start | bytes 245768 | tf_op jit(solution)/shard_map/ppermute | solution.py:418
  50.4 10.9 %collective-permute-start.18 = (f32[2,80,128]{2,1,0:T(8,128)S(1)}, f32[2,80,128]{2,1,0:T(8,128)S(1)}, u32[]{:S(2)}, u32[]{:S(2)}) collective-permute-start(f32[2,80,128]{2,1,0:T(8,128)S(1)} %get-tuple-element.62), channel_id=1, source_target_pairs={{0,4},{1,5},{2,6},{3,7},{4,0},{5,1},{6,2},{7,3},{8,12},{9,13},{10,... | collective-permute-start | bytes 245768 | tf_op jit(solution)/shard_map/ppermute | solution.py:418
  53.1 8.2 %collective-permute-start.19 = (f32[2,80,128]{2,1,0:T(8,128)S(1)}, f32[2,80,128]{2,1,0:T(8,128)S(1)}, u32[]{:S(2)}, u32[]{:S(2)}) collective-permute-start(f32[2,80,128]{2,1,0:T(8,128)S(1)} %get-tuple-element.63), channel_id=1, source_target_pairs={{0,3},{1,2},{2,1},{3,0},{4,7},{5,6},{6,5},{7,4},{8,11},{9,10},{10,... | collective-permute-start | bytes 245768 | tf_op jit(solution)/shard_map/ppermute | solution.py:418
  53.1 10.0 %collective-permute-start.20 = (f32[2,80,128]{2,1,0:T(8,128)S(1)}, f32[2,80,128]{2,1,0:T(8,128)S(1)}, u32[]{:S(2)}, u32[]{:S(2)}) collective-permute-start(f32[2,80,128]{2,1,0:T(8,128)S(1)} %get-tuple-element.64), channel_id=1, source_target_pairs={{0,2},{1,3},{2,0},{3,1},{4,6},{5,7},{6,4},{7,5},{8,10},{9,11},{10,... | collective-permute-start | bytes 245768 | tf_op jit(solution)/shard_map/ppermute | solution.py:418
  (3 other events, 33.4 us)

commit v8 on v7

--- a/solution.py
+++ b/solution.py
@@ -1,4 +1,5 @@
 import functools
+import math
 
 import jax
 import jax.numpy as jnp
@@ -53,72 +54,89 @@
     )
 
 
-def step_pairs(count, step):
-    if count & (count - 1) == 0:
-        return [(source, source ^ step) for source in range(count)]
-    return [(source, (source + step) % count) for source in range(count)]
+def kern_step(tile, step, groups):
+    if groups != 4 or step not in (1, 2):
+        return step
+    return step + (tile & 1) * (3 - 2 * step)
 
 
 def partner(me, step, count):
     if count & (count - 1) == 0:
         return me ^ step, me ^ step
-    return lax.rem(me + step, count), lax.rem(me + count - step, count)
-
-
-def exchange(values, axis):
-    count = lax.axis_size(axis)
-    arrived = [values[0]] * count
-    for step in range(count - 1, 0, -1):
-        arrived[step] = lax.ppermute(values[step], axis, step_pairs(count, step))
+    return (me + step) % count, (me + count - step) % count
+
+
+def kern_partner(step, groups):
+    return partner(
+        lax.axis_index("kern"), kern_step(lax.axis_index("tile"), step, groups), groups
+    )
+
+
+def exchange(values):
+    groups, count = lax.axis_size("kern"), lax.axis_size("tile")
+    arrived = [values[0]]
+    for step in range(1, groups):
+        pairs = []
+        for group in range(groups):
+            for tile in range(count):
+                dest = partner(group, kern_step(tile, step, groups), groups)[0]
+                pairs.append((group * count + tile, dest * count + tile))
+        arrived.append(lax.ppermute(values[step], ("kern", "tile"), pairs))
     return arrived
 
 
 class Message:
-    def __init__(self, count, reach, pairs, step=None, places=(0,), slot=None):
-        self.count, self.reach, self.pairs = count, reach, pairs
-        self.step, self.places, self.slot = step, places, slot
-        self.width = len(places)
+    def __init__(self, count, reach, ahead=None, turn=0, slot=None):
+        self.count, self.reach, self.slot = count, reach, slot
+        self.ahead, self.turn = ahead, turn
+        self.width = 1
+        if slot is None and ahead <= reach and count - ahead <= reach:
+            self.width = 2
+        offset = ahead if slot is None else offset_of(slot, reach)
+        self.pairs = [(source, (source - offset) % count) for source in range(count)]
+        if slot is None and turn is not None:
+            self.pairs = [(source, self.mate(source)) for source in range(count)]
+
+    def mate(self, me):
+        upward = 1 - 2 * ((me // math.gcd(self.ahead, self.count) + self.turn) % 2)
+        return (me + upward * self.ahead + self.count) % self.count
+
+    def across(self):
+        half = self.count // 2
+        return self.width * sum((a < half) != (b < half) for a, b in self.pairs)
 
     def slots(self, me, sending):
         if self.slot is not None:
-            return [(self.slot, True)]
+            return [self.slot]
         count, reach = self.count, self.reach
-        dest, source = partner(me, self.step, count)
-        column, row = (me, dest) if sending else (source, me)
-        ahead = lax.rem(column - row + count, count)
-        first = jnp.where(ahead <= reach, ahead + reach - 1, ahead - count + reach)
-        both = jnp.logical_and(ahead <= reach, count - ahead <= reach)
-        second = jnp.where(both, ahead - count + reach, first)
-        return [((first, True), (second, both))[place] for place in self.places]
-
-
-def step_messages(count, reach, step):
-    pairs = step_pairs(count, step)
-    doubles = []
-    for source, dest in pairs:
-        ahead = (source - dest) % count
-        if ahead <= reach and count - ahead <= reach:
-            doubles.append((source, dest))
-    if not doubles:
-        return [Message(count, reach, pairs, step)]
-    if len(doubles) < len(pairs) and step >= count // 2:
-        return [Message(count, reach, pairs, step), Message(count, reach, doubles, step, (1,))]
-    return [Message(count, reach, pairs, step, (0, 1))]
+        if self.turn is None:
+            ahead = self.ahead
+        else:
+            mate = self.mate(me)
+            ahead = lax.rem((me - mate if sending else mate - me) + count, count)
+        below = ahead - count + reach
+        if self.width == 1:
+            return [jnp.where(ahead <= reach, ahead + reach - 1, below)]
+        return [ahead + reach - 1, below]
+
+
+def offset_of(slot, reach):
+    return slot - reach if slot < reach else slot - reach + 1
 
 
 def message_sets_of(count, slots):
     reach = slots // 2
-    if reach < count <= 2 * reach:
-        sets = [[], []]
-        for step in range(count - 1, 0, -1):
-            sets[step < count // 2] += step_messages(count, reach, step)
-        return sets
+    if not reach < count <= 2 * reach:
+        return [[Message(count, reach, slot=slot) for slot in range(slots)]]
     messages = []
-    for slot in range(slots):
-        offset = slot - reach if slot < reach else slot - reach + 1
-        pairs = [(source, (source - offset) % count) for source in range(count)]
-        messages.append(Message(count, reach, pairs, slot=slot))
-    return [messages]
+    if count & (count - 1) == 0:
+        for ahead in range(1, count // 2 + 1):
+            for turn in range(1 if 2 * ahead == count else 2):
+                messages.append(Message(count, reach, ahead, turn))
+    else:
+        messages = [Message(count, reach, ahead, None) for ahead in range(1, count)]
+    messages.sort(key=lambda message: -message.across())
+    return [messages[: count // 2 - 1], messages[count // 2 - 1 :]]
 
 
 def chunks_of(messages, most=4):
@@ -158,7 +176,7 @@
         right, sems = refs[1:]
     copies = []
     for message in messages:
-        for slot, _ in message.slots(me, True):
+        for slot in message.slots(me, True):
             at = len(copies)
             copies.append(pltpu.make_async_copy(right_ref.at[slot], right.at[at], sems.at[at]))
             copies[-1].start()
@@ -204,9 +222,8 @@
     parts, refs = refs[:groups], refs[groups:]
     splits, outs, cols_ref = refs[: len(message_sets)], refs[len(message_sets) : -1], refs[-1]
     part = parts[0].shape[0]
-    me = lax.axis_index("kern")
     for at in range(groups):
-        source = partner(me, at, groups)[1]
+        source = kern_partner(at, groups)[1]
         cols_ref[pl.ds(pl.multiple_of(source * part, part), part)] = parts[at][...]
     both = side_by_side(cols_ref[...])
     rank = outs[0].shape[1]
@@ -344,8 +361,8 @@
             picked[pl.ds(pl.multiple_of(term * rank, rank), rank)] = kept
 
     for got, message in zip(gots, messages):
-        for w, (slot, there) in enumerate(message.slots(me, False)):
-            pick(got, w, jnp.where(there, term_of[slot], -1))
+        for w, slot in enumerate(message.slots(me, False)):
+            pick(got, w, term_of[slot])
     both = side_by_side(picked[...])
     part = diag_ref.shape[0] // halves
     sent = []
@@ -363,20 +380,18 @@
         copy.wait()
     if groups > 1:
         part = stage.shape[0] // groups
-        own = lax.axis_index("kern")
         for at in range(groups):
-            dest = partner(own, at, groups)[0]
+            dest = kern_partner(at, groups)[0]
             outs[at][...] = stage[pl.ds(pl.multiple_of(dest * part, part), part)]
 
 
 def mix_kernel(groups, *refs):
     fields, weights_ref, outs = refs[:groups], refs[groups], refs[groups + 1 :]
-    me = lax.axis_index("kern")
     for at in range(groups):
-        base = partner(me, at, groups)[0] * groups
+        base = kern_partner(at, groups)[0] * groups
         total = None
         for b in range(groups):
-            term = fields[b][...] * weights_ref[base + partner(me, b, groups)[1]]
+            term = fields[b][...] * weights_ref[base + kern_partner(b, groups)[1]]
             total = term if total is None else total + term
         outs[at][...] = total
 
@@ -449,7 +464,7 @@
         splits.append(split_right)
     diag_part, left_split, weights = prepare(diag_tile, cols, left_rows, table, index, halves)
     first = rows(offsets, ranks, gots, messages, left_split, diag_part, slots, halves, groups)
-    mixed = exchange(mix(exchange(first, "kern"), weights), "kern")
+    mixed = exchange(mix(exchange(first), weights))
     coeffs, cols = next_coefficients(mixed, splits, message_sets, rank)
     gots = deliver(coeffs, messages)
     diag_part = diagonal(diag_tile, cols)

time: 65.4 us -> 58.4 us (0.89)
  starting transfers between devices: 32.6 us -> 23.5 us
  waiting for transfers between devices: 21.2 us -> 23.6 us
    ppermute x16 -> x14, starting transfers between devices: 25.5 us -> 16.4 us  [deliver(): lax.ppermute(sent, 'tile', message.pairs)]
    ppermute x16 -> x14, waiting for transfers between devices: 13.8 us -> 16.1 us  [deliver(): lax.ppermute(sent, 'tile', message.pairs)]
  transfers between devices with their start and end apart: 22 -> 20, of which waited for: 13 -> 12; matrix products, arithmetic and copies ran while one was open for 0% -> 0% of each run, Pallas kernels for 7% -> 5%
where the time goes in v8:
time: 58.4 us; the launch traced here: 58.2 us
  waiting for transfers between devices  23.6 us (40%)
  starting transfers between devices  23.5 us (40%)
  Pallas kernels  11 us (19%)
    ppermute x14, starting transfers between devices, deliver(): lax.ppermute(sent, 'tile', message.pairs)  16.4 us
    ppermute x14, waiting for transfers between devices, deliver(): lax.ppermute(sent, 'tile', message.pairs)  16.1 us
    ppermute x6, waiting for transfers between devices, exchange(): arrived.append(lax.ppermute(values[step], ('kern', 'tile'), pairs))  7.51 us
    ppermute x6, starting transfers between devices, exchange(): arrived.append(lax.ppermute(values[step], ('kern', 'tile'), pairs))  7.11 us
    pallas_call x2, Pallas kernels, first_coefficients(): call(functools.partial(first_coeff_kernel, messages, fresh), outs, [in_vm...  4.01 us
    pallas_call x2, Pallas kernels, rows(): call(functools.partial(row_kernel, messages, halves, groups), pltpu.HBM((...  3.55 us
    pallas_call x1, Pallas kernels, prepare(): call(functools.partial(prepare_kernel, halves), [struct(size, width), str...  2.2 us
  transfers between devices with their start and end apart: 20, of which 12 were waited for; matrix products, arithmetic and copies ran while one was open for 0% of the time, Pallas kernels for 5%

profile of v8, /device:TPU:0, one launch (start us, length us, event | category | flops | bytes accessed | tf_op | source)
XLA Modules:
  0.0 58.2 jit_solution(5611679004803729144)
XLA Ops:
  0.0 2.0 %shard_map.82 = (f32[2,80,128]{2,1,0:T(8,128)S(1)}, f32[2,80,128]{2,1,0:T(8,128)S(1)}, f32[2,80,128]{2,1,0:T(8,128)S(1)}, bf16[960,512]{1,0:T(8,128)(2,1)S(1)}, bf16[512,256]{1,0:T(8,128)(2,1)S(1)}) custom-call(f32[512,128]{1,0:T(8,128)} %bitcast.22, f32[12,80,512]{2,1,0:T(8,128)} %bitcast.19), custom_call_target="tpu_custom_call" | custom-call | flops 251658240 | bytes 2211840 | tf_op jit(solution)/shard_map/pallas_call | solution.py:209
  2.0 2.0 %shard_map.83 = (f32[2,80,128]{2,1,0:T(8,128)S(1)}, f32[1,80,128]{2,1,0:T(8,128)S(1)}, f32[1,80,128]{2,1,0:T(8,128)S(1)}, f32[2,80,128]{2,1,0:T(8,128)S(1)}, bf16[960,512]{1,0:T(8,128)(2,1)S(1)}) custom-call(bf16[512,256]{1,0:T(8,128)(2,1)S(1)} %get-tuple-element.37.cols_ref, f32[12,80,512]{2,1,0:T(8,128)} %bitcast.20), custom_call_target="tpu_custom_call" | custom-call | flops 251658240 | bytes 2211840 | tf_op jit(solution)/shard_map/pallas_call | solution.py:209
  4.1 4.6 %collective-permute-start.4 = (f32[1,80,128]{2,1,0:T(8,128)S(1)}, f32[1,80,128]{2,1,0:T(8,128)S(1)}, u32[]{:S(2)}, u32[]{:S(2)}) collective-permute-start(f32[1,80,128]{2,1,0:T(8,128)S(1)} %get-tuple-element.39), channel_id=1, source_target_pairs={{0,7},{1,2},{2,1},{3,4},{4,3},{5,6},{6,5},{7,0},{8,15},{9,10},{10,... | collective-permute-start | bytes 122888 | tf_op jit(solution)/shard_map/ppermute | solution.py:433
  9.6 2.4 %collective-permute-start.2 = (f32[2,80,128]{2,1,0:T(8,128)S(1)}, f32[2,80,128]{2,1,0:T(8,128)S(1)}, u32[]{:S(2)}, u32[]{:S(2)}) collective-permute-start(f32[2,80,128]{2,1,0:T(8,128)S(1)} %get-tuple-element.36), channel_id=1, source_target_pairs={{0,4},{1,5},{2,6},{3,7},{4,0},{5,1},{6,2},{7,3},{8,12},{9,13},{10,... | collective-permute-start | bytes 245768 | tf_op jit(solution)/shard_map/ppermute | solution.py:433
  13.3 2.2 %shard_map.84 = (f32[512,128]{1,0:T(8,128)S(1)}, bf16[1024,640]{1,0:T(8,128)(2,1)S(1)}, f32[16,128,128]{2,1,0:T(8,128)S(1)}) custom-call(f32[512,512]{1,0:T(8,128)} %bitcast.11, f32[512,128]{1,0:T(8,128)} %bitcast.23, f32[640,512]{1,0:T(8,128)} %bitcast.21, f32[16,64]{1,0:T(8,128)S(1)} %bitcast.13, s32[4,128]{1,0:T(4,128)S(1)} %bitcast.14), custom_call_target="tpu_custom_call" | custom-call | flops 268435456 | bytes 4194304 | tf_op jit(solution)/shard_map/pallas_call | solution.py:320
  15.8 4.8 %collective-permute-done.1.refs_1_ = f32[2,80,128]{2,1,0:T(8,128)S(1)} collective-permute-done((f32[2,80,128]{2,1,0:T(8,128)S(1)}, f32[2,80,128]{2,1,0:T(8,128)S(1)}, u32[]{:S(2)}, u32[]{:S(2)}) %collective-permute-start.1) | collective-permute-done | bytes 81952 | tf_op jit(solution)/shard_map/ppermute | solution.py:433
  20.6 2.6 %collective-permute-done.2.refs_2_ = f32[2,80,128]{2,1,0:T(8,128)S(1)} collective-permute-done((f32[2,80,128]{2,1,0:T(8,128)S(1)}, f32[2,80,128]{2,1,0:T(8,128)S(1)}, u32[]{:S(2)}, u32[]{:S(2)}) %collective-permute-start.2) | collective-permute-done | bytes 81952 | tf_op jit(solution)/shard_map/ppermute | solution.py:433
  23.2 1.4 %shard_map.85 = (f32[128,128]{1,0:T(8,128)S(1)}, f32[128,128]{1,0:T(8,128)S(1)}, f32[128,128]{1,0:T(8,128)S(1)}, f32[128,128]{1,0:T(8,128)S(1)}) custom-call(s32[1,8]{1,0:T(1,128)S(1)} %bitcast.15, s32[1,8]{1,0:T(1,128)S(1)} %bitcast.17, f32[2,80,128]{2,1,0:T(8,128)S(1)} %collective-permute-done.refs_0_, f32[2,80,128]{2,1,0:T(8,128)S(1)} %collective-permute-done.1.refs_1_, ...), custom_call_target="tpu_custom_call" | custom-call | flops 335544320 | bytes 1638400 | tf_op jit(solution)/shard_map/pallas_call | solution.py:416
  24.7 1.6 %collective-permute-start.7 = (f32[128,128]{1,0:T(8,128)S(1)}, f32[128,128]{1,0:T(8,128)S(1)}, u32[]{:S(2)}, u32[]{:S(2)}) collective-permute-start(f32[128,128]{1,0:T(8,128)S(1)} %get-tuple-element.45), channel_id=1, source_target_pairs={{0,8},{1,17},{2,10},{3,19},{4,12},{5,21},{6,14},{7,23},{8,0},{9,25... | collective-permute-start | bytes 196616 | tf_op jit(solution)/shard_map/ppermute | solution.py:84
  26.2 1.5 %collective-permute-start.8 = (f32[128,128]{1,0:T(8,128)S(1)}, f32[128,128]{1,0:T(8,128)S(1)}, u32[]{:S(2)}, u32[]{:S(2)}) collective-permute-start(f32[128,128]{1,0:T(8,128)S(1)} %get-tuple-element.46), channel_id=1, source_target_pairs={{0,16},{1,9},{2,18},{3,11},{4,20},{5,13},{6,22},{7,15},{8,24},{9,1... | collective-permute-start | bytes 196616 | tf_op jit(solution)/shard_map/ppermute | solution.py:84
  28.2 1.4 %collective-permute-done.7.refs_1_ = f32[128,128]{1,0:T(8,128)S(1)} collective-permute-done((f32[128,128]{1,0:T(8,128)S(1)}, f32[128,128]{1,0:T(8,128)S(1)}, u32[]{:S(2)}, u32[]{:S(2)}) %collective-permute-start.7) | collective-permute-done | bytes 65568 | tf_op jit(solution)/shard_map/ppermute | solution.py:84
  29.6 0.9 %collective-permute-done.8.refs_2_ = f32[128,128]{1,0:T(8,128)S(1)} collective-permute-done((f32[128,128]{1,0:T(8,128)S(1)}, f32[128,128]{1,0:T(8,128)S(1)}, u32[]{:S(2)}, u32[]{:S(2)}) %collective-permute-start.8) | collective-permute-done | bytes 65568 | tf_op jit(solution)/shard_map/ppermute | solution.py:84
  30.5 2.4 %collective-permute-done.9.refs_3_ = f32[128,128]{1,0:T(8,128)S(1)} collective-permute-done((f32[128,128]{1,0:T(8,128)S(1)}, f32[128,128]{1,0:T(8,128)S(1)}, u32[]{:S(2)}, u32[]{:S(2)}) %collective-permute-start.9) | collective-permute-done | bytes 65568 | tf_op jit(solution)/shard_map/ppermute | solution.py:84
  34.2 2.3 %collective-permute-start.12 = (f32[128,128]{1,0:T(8,128)S(1)}, f32[128,128]{1,0:T(8,128)S(1)}, u32[]{:S(2)}, u32[]{:S(2)}) collective-permute-start(f32[128,128]{1,0:T(8,128)S(1)} %get-tuple-element.52), channel_id=1, source_target_pairs={{0,24},{1,25},{2,26},{3,27},{4,28},{5,29},{6,30},{7,31},{8,16},{9,... | collective-permute-start | bytes 196616 | tf_op jit(solution)/shard_map/ppermute | solution.py:84
  36.6 0.8 %collective-permute-done.10.refs_1_ = f32[128,128]{1,0:T(8,128)S(1)} collective-permute-done((f32[128,128]{1,0:T(8,128)S(1)}, f32[128,128]{1,0:T(8,128)S(1)}, u32[]{:S(2)}, u32[]{:S(2)}) %collective-permute-start.10) | collective-permute-done | bytes 65568 | tf_op jit(solution)/shard_map/ppermute | solution.py:84
  37.4 1.0 %collective-permute-done.11.refs_2_ = f32[128,128]{1,0:T(8,128)S(1)} collective-permute-done((f32[128,128]{1,0:T(8,128)S(1)}, f32[128,128]{1,0:T(8,128)S(1)}, u32[]{:S(2)}, u32[]{:S(2)}) %collective-permute-start.11) | collective-permute-done | bytes 65568 | tf_op jit(solution)/shard_map/ppermute | solution.py:84
  38.3 1.1 %collective-permute-done.12.refs_3_ = f32[128,128]{1,0:T(8,128)S(1)} collective-permute-done((f32[128,128]{1,0:T(8,128)S(1)}, f32[128,128]{1,0:T(8,128)S(1)}, u32[]{:S(2)}, u32[]{:S(2)}) %collective-permute-start.12) | collective-permute-done | bytes 65568 | tf_op jit(solution)/shard_map/ppermute | solution.py:84
  40.2 1.3 %collective-permute-start.18 = (f32[1,80,128]{2,1,0:T(8,128)S(1)}, f32[1,80,128]{2,1,0:T(8,128)S(1)}, u32[]{:S(2)}, u32[]{:S(2)}) collective-permute-start(f32[1,80,128]{2,1,0:T(8,128)S(1)} %get-tuple-element.60), channel_id=1, source_target_pairs={{0,1},{1,0},{2,3},{3,2},{4,5},{5,4},{6,7},{7,6},{8,9},{9,8},{10,11... | collective-permute-start | bytes 122888 | tf_op jit(solution)/shard_map/ppermute | solution.py:433
  41.5 2.6 %collective-permute-start.13 = (f32[2,80,128]{2,1,0:T(8,128)S(1)}, f32[2,80,128]{2,1,0:T(8,128)S(1)}, u32[]{:S(2)}, u32[]{:S(2)}) collective-permute-start(f32[2,80,128]{2,1,0:T(8,128)S(1)} %get-tuple-element.55), channel_id=1, source_target_pairs={{0,6},{1,7},{2,4},{3,5},{4,2},{5,3},{6,0},{7,1},{8,14},{9,15},{10,... | collective-permute-start | bytes 245768 | tf_op jit(solution)/shard_map/ppermute | solution.py:433
  44.1 2.2 %collective-permute-start.15 = (f32[2,80,128]{2,1,0:T(8,128)S(1)}, f32[2,80,128]{2,1,0:T(8,128)S(1)}, u32[]{:S(2)}, u32[]{:S(2)}) collective-permute-start(f32[2,80,128]{2,1,0:T(8,128)S(1)} %get-tuple-element.57), channel_id=1, source_target_pairs={{0,4},{1,5},{2,6},{3,7},{4,0},{5,1},{6,2},{7,3},{8,12},{9,13},{10,... | collective-permute-start | bytes 245768 | tf_op jit(solution)/shard_map/ppermute | solution.py:433
  46.4 1.0 %collective-permute-start.19 = (f32[2,80,128]{2,1,0:T(8,128)S(1)}, f32[2,80,128]{2,1,0:T(8,128)S(1)}, u32[]{:S(2)}, u32[]{:S(2)}) collective-permute-start(f32[2,80,128]{2,1,0:T(8,128)S(1)} %get-tuple-element.61), channel_id=1, source_target_pairs={{0,2},{1,3},{2,0},{3,1},{4,6},{5,7},{6,4},{7,5},{8,10},{9,11},{10,... | collective-permute-start | bytes 245768 | tf_op jit(solution)/shard_map/ppermute | solution.py:433
  48.6 5.4 %collective-permute-done.14.refs_1_ = f32[2,80,128]{2,1,0:T(8,128)S(1)} collective-permute-done((f32[2,80,128]{2,1,0:T(8,128)S(1)}, f32[2,80,128]{2,1,0:T(8,128)S(1)}, u32[]{:S(2)}, u32[]{:S(2)}) %collective-permute-start.14) | collective-permute-done | bytes 81952 | tf_op jit(solution)/shard_map/ppermute | solution.py:433
  54.0 2.1 %collective-permute-done.15.refs_2_ = f32[2,80,128]{2,1,0:T(8,128)S(1)} collective-permute-done((f32[2,80,128]{2,1,0:T(8,128)S(1)}, f32[2,80,128]{2,1,0:T(8,128)S(1)}, u32[]{:S(2)}, u32[]{:S(2)}) %collective-permute-start.15) | collective-permute-done | bytes 81952 | tf_op jit(solution)/shard_map/ppermute | solution.py:433
  56.1 2.1 %shard_map.89 = f32[512,128]{1,0:T(8,128)} custom-call(s32[1,8]{1,0:T(1,128)S(1)} %bitcast.16, s32[1,8]{1,0:T(1,128)S(1)} %bitcast.18, f32[2,80,128]{2,1,0:T(8,128)S(1)} %collective-permute-done.13.refs_0_, f32[2,80,128]{2,1,0:T(8,128)S(1)} %collective-permute-done.14.refs_1_, f32[2,80,128]{2,1,0:T(8,128)S(1)} %collective-permute-done.15.refs_2_, ...), custom_call_target="tpu_custom_call" | custom-call | flops 335544320 | bytes 1638400 | tf_op jit(solution)/shard_map/pallas_call | solution.py:416
  (34 shorter events, 6.4 us)
Async XLA Ops:
  2.0 11.2 %copy-start.1 = (f32[64,4,4]{0,2,1:T(4,128)S(1)}, f32[64,4,4]{0,2,1:T(4,128)}, u32[]{:S(2)}) copy-start(f32[64,4,4]{0,2,1:T(4,128)} %param.13) | copy-start | bytes 12292
  2.0 11.2 %copy-start.2 = (s32[512]{0:T(512)S(1)}, s32[512]{0:T(512)}, u32[]{:S(2)}) copy-start(s32[512]{0:T(512)} %param.14) | copy-start | bytes 6148
  4.1 8.0 %collective-permute-start.4 = (f32[1,80,128]{2,1,0:T(8,128)S(1)}, f32[1,80,128]{2,1,0:T(8,128)S(1)}, u32[]{:S(2)}, u32[]{:S(2)}) collective-permute-start(f32[1,80,128]{2,1,0:T(8,128)S(1)} %get-tuple-element.39), channel_id=1, source_target_pairs={{0,7},{1,2},{2,1},{3,4},{4,3},{5,6},{6,5},{7,0},{8,15},{9,10},{10,... | collective-permute-start | bytes 122888 | tf_op jit(solution)/shard_map/ppermute | solution.py:433
  8.6 4.2 %collective-permute-start.5 = (f32[1,80,128]{2,1,0:T(8,128)S(1)}, f32[1,80,128]{2,1,0:T(8,128)S(1)}, u32[]{:S(2)}, u32[]{:S(2)}) collective-permute-start(f32[1,80,128]{2,1,0:T(8,128)S(1)} %get-tuple-element.40), channel_id=1, source_target_pairs={{0,1},{1,0},{2,3},{3,2},{4,5},{5,4},{6,7},{7,6},{8,9},{9,8},{10,11... | collective-permute-start | bytes 122888 | tf_op jit(solution)/shard_map/ppermute | solution.py:433
  8.6 7.1 %collective-permute-start = (f32[2,80,128]{2,1,0:T(8,128)S(1)}, f32[2,80,128]{2,1,0:T(8,128)S(1)}, u32[]{:S(2)}, u32[]{:S(2)}) collective-permute-start(f32[2,80,128]{2,1,0:T(8,128)S(1)} %get-tuple-element.34), channel_id=1, source_target_pairs={{0,6},{1,7},{2,4},{3,5},{4,2},{5,3},{6,0},{7,1},{8,14},{9,15},{10,... | collective-permute-start | bytes 245768 | tf_op jit(solution)/shard_map/ppermute | solution.py:433
  9.3 11.3 %collective-permute-start.1 = (f32[2,80,128]{2,1,0:T(8,128)S(1)}, f32[2,80,128]{2,1,0:T(8,128)S(1)}, u32[]{:S(2)}, u32[]{:S(2)}) collective-permute-start(f32[2,80,128]{2,1,0:T(8,128)S(1)} %get-tuple-element.35), channel_id=1, source_target_pairs={{0,5},{1,4},{2,7},{3,6},{4,1},{5,0},{6,3},{7,2},{8,13},{9,12},{10,... | collective-permute-start | bytes 245768 | tf_op jit(solution)/shard_map/ppermute | solution.py:433
  9.6 13.6 %collective-permute-start.2 = (f32[2,80,128]{2,1,0:T(8,128)S(1)}, f32[2,80,128]{2,1,0:T(8,128)S(1)}, u32[]{:S(2)}, u32[]{:S(2)}) collective-permute-start(f32[2,80,128]{2,1,0:T(8,128)S(1)} %get-tuple-element.36), channel_id=1, source_target_pairs={{0,4},{1,5},{2,6},{3,7},{4,0},{5,1},{6,2},{7,3},{8,12},{9,13},{10,... | collective-permute-start | bytes 245768 | tf_op jit(solution)/shard_map/ppermute | solution.py:433
  12.0 11.2 %collective-permute-start.3 = (f32[2,80,128]{2,1,0:T(8,128)S(1)}, f32[2,80,128]{2,1,0:T(8,128)S(1)}, u32[]{:S(2)}, u32[]{:S(2)}) collective-permute-start(f32[2,80,128]{2,1,0:T(8,128)S(1)} %get-tuple-element.38), channel_id=1, source_target_pairs={{0,3},{1,6},{2,5},{3,0},{4,7},{5,2},{6,1},{7,4},{8,11},{9,14},{10,... | collective-permute-start | bytes 245768 | tf_op jit(solution)/shard_map/ppermute | solution.py:433
  12.8 10.4 %collective-permute-start.6 = (f32[2,80,128]{2,1,0:T(8,128)S(1)}, f32[2,80,128]{2,1,0:T(8,128)S(1)}, u32[]{:S(2)}, u32[]{:S(2)}) collective-permute-start(f32[2,80,128]{2,1,0:T(8,128)S(1)} %get-tuple-element.41), channel_id=1, source_target_pairs={{0,2},{1,3},{2,0},{3,1},{4,6},{5,7},{6,4},{7,5},{8,10},{9,11},{10,... | collective-permute-start | bytes 245768 | tf_op jit(solution)/shard_map/ppermute | solution.py:433
  13.2 10.0 %copy-start.4 = (s32[1,1,8]{2,1,0:T(1,128)S(1)}, s32[1,1,8]{2,1,0:T(1,128)}, u32[]{:S(2)}) copy-start(s32[1,1,8]{2,1,0:T(1,128)} %param.12) | copy-start | bytes 100
  24.7 4.9 %collective-permute-start.7 = (f32[128,128]{1,0:T(8,128)S(1)}, f32[128,128]{1,0:T(8,128)S(1)}, u32[]{:S(2)}, u32[]{:S(2)}) collective-permute-start(f32[128,128]{1,0:T(8,128)S(1)} %get-tuple-element.45), channel_id=1, source_target_pairs={{0,8},{1,17},{2,10},{3,19},{4,12},{5,21},{6,14},{7,23},{8,0},{9,25... | collective-permute-start | bytes 196616 | tf_op jit(solution)/shard_map/ppermute | solution.py:84
  26.2 4.3 %collective-permute-start.8 = (f32[128,128]{1,0:T(8,128)S(1)}, f32[128,128]{1,0:T(8,128)S(1)}, u32[]{:S(2)}, u32[]{:S(2)}) collective-permute-start(f32[128,128]{1,0:T(8,128)S(1)} %get-tuple-element.46), channel_id=1, source_target_pairs={{0,16},{1,9},{2,18},{3,11},{4,20},{5,13},{6,22},{7,15},{8,24},{9,1... | collective-permute-start | bytes 196616 | tf_op jit(solution)/shard_map/ppermute | solution.py:84
  27.8 5.2 %collective-permute-start.9 = (f32[128,128]{1,0:T(8,128)S(1)}, f32[128,128]{1,0:T(8,128)S(1)}, u32[]{:S(2)}, u32[]{:S(2)}) collective-permute-start(f32[128,128]{1,0:T(8,128)S(1)} %get-tuple-element.47), channel_id=1, source_target_pairs={{0,24},{1,25},{2,26},{3,27},{4,28},{5,29},{6,30},{7,31},{8,16},{9,... | collective-permute-start | bytes 196616 | tf_op jit(solution)/shard_map/ppermute | solution.py:84
  33.0 14.3 %copy-start = (f32[1,1,512,512]{3,2,1,0:T(8,128)S(1)}, f32[1,1,512,512]{3,2,1,0:T(8,128)}, u32[]{:S(2)}) copy-start(f32[1,1,512,512]{3,2,1,0:T(8,128)} %param.8) | copy-start | bytes 3145732
  33.0 4.3 %collective-permute-start.10 = (f32[128,128]{1,0:T(8,128)S(1)}, f32[128,128]{1,0:T(8,128)S(1)}, u32[]{:S(2)}, u32[]{:S(2)}) collective-permute-start(f32[128,128]{1,0:T(8,128)S(1)} %get-tuple-element.50), channel_id=1, source_target_pairs={{0,8},{1,17},{2,10},{3,19},{4,12},{5,21},{6,14},{7,23},{8,0},{9,25... | collective-permute-start | bytes 196616 | tf_op jit(solution)/shard_map/ppermute | solution.py:84
  33.6 4.7 %collective-permute-start.11 = (f32[128,128]{1,0:T(8,128)S(1)}, f32[128,128]{1,0:T(8,128)S(1)}, u32[]{:S(2)}, u32[]{:S(2)}) collective-permute-start(f32[128,128]{1,0:T(8,128)S(1)} %get-tuple-element.51), channel_id=1, source_target_pairs={{0,16},{1,9},{2,18},{3,11},{4,20},{5,13},{6,22},{7,15},{8,24},{9,1... | collective-permute-start | bytes 196616 | tf_op jit(solution)/shard_map/ppermute | solution.py:84
  34.2 5.2 %collective-permute-start.12 = (f32[128,128]{1,0:T(8,128)S(1)}, f32[128,128]{1,0:T(8,128)S(1)}, u32[]{:S(2)}, u32[]{:S(2)}) collective-permute-start(f32[128,128]{1,0:T(8,128)S(1)} %get-tuple-element.52), channel_id=1, source_target_pairs={{0,24},{1,25},{2,26},{3,27},{4,28},{5,29},{6,30},{7,31},{8,16},{9,... | collective-permute-start | bytes 196616 | tf_op jit(solution)/shard_map/ppermute | solution.py:84
  40.1 6.3 %collective-permute-start.17 = (f32[1,80,128]{2,1,0:T(8,128)S(1)}, f32[1,80,128]{2,1,0:T(8,128)S(1)}, u32[]{:S(2)}, u32[]{:S(2)}) collective-permute-start(f32[1,80,128]{2,1,0:T(8,128)S(1)} %get-tuple-element.59), channel_id=1, source_target_pairs={{0,7},{1,2},{2,1},{3,4},{4,3},{5,6},{6,5},{7,0},{8,15},{9,10},{10,... | collective-permute-start | bytes 122888 | tf_op jit(solution)/shard_map/ppermute | solution.py:433
  40.2 6.2 %collective-permute-start.18 = (f32[1,80,128]{2,1,0:T(8,128)S(1)}, f32[1,80,128]{2,1,0:T(8,128)S(1)}, u32[]{:S(2)}, u32[]{:S(2)}) collective-permute-start(f32[1,80,128]{2,1,0:T(8,128)S(1)} %get-tuple-element.60), channel_id=1, source_target_pairs={{0,1},{1,0},{2,3},{3,2},{4,5},{5,4},{6,7},{7,6},{8,9},{9,8},{10,11... | collective-permute-start | bytes 122888 | tf_op jit(solution)/shard_map/ppermute | solution.py:433
  41.5 7.1 %collective-permute-start.13 = (f32[2,80,128]{2,1,0:T(8,128)S(1)}, f32[2,80,128]{2,1,0:T(8,128)S(1)}, u32[]{:S(2)}, u32[]{:S(2)}) collective-permute-start(f32[2,80,128]{2,1,0:T(8,128)S(1)} %get-tuple-element.55), channel_id=1, source_target_pairs={{0,6},{1,7},{2,4},{3,5},{4,2},{5,3},{6,0},{7,1},{8,14},{9,15},{10,... | collective-permute-start | bytes 245768 | tf_op jit(solution)/shard_map/ppermute | solution.py:433
  44.1 9.9 %collective-permute-start.14 = (f32[2,80,128]{2,1,0:T(8,128)S(1)}, f32[2,80,128]{2,1,0:T(8,128)S(1)}, u32[]{:S(2)}, u32[]{:S(2)}) collective-permute-start(f32[2,80,128]{2,1,0:T(8,128)S(1)} %get-tuple-element.56), channel_id=1, source_target_pairs={{0,5},{1,4},{2,7},{3,6},{4,1},{5,0},{6,3},{7,2},{8,13},{9,12},{10,... | collective-permute-start | bytes 245768 | tf_op jit(solution)/shard_map/ppermute | solution.py:433
  44.1 12.0 %collective-permute-start.15 = (f32[2,80,128]{2,1,0:T(8,128)S(1)}, f32[2,80,128]{2,1,0:T(8,128)S(1)}, u32[]{:S(2)}, u32[]{:S(2)}) collective-permute-start(f32[2,80,128]{2,1,0:T(8,128)S(1)} %get-tuple-element.57), channel_id=1, source_target_pairs={{0,4},{1,5},{2,6},{3,7},{4,0},{5,1},{6,2},{7,3},{8,12},{9,13},{10,... | collective-permute-start | bytes 245768 | tf_op jit(solution)/shard_map/ppermute | solution.py:433
  46.4 9.7 %collective-permute-start.16 = (f32[2,80,128]{2,1,0:T(8,128)S(1)}, f32[2,80,128]{2,1,0:T(8,128)S(1)}, u32[]{:S(2)}, u32[]{:S(2)}) collective-permute-start(f32[2,80,128]{2,1,0:T(8,128)S(1)} %get-tuple-element.58), channel_id=1, source_target_pairs={{0,3},{1,6},{2,5},{3,0},{4,7},{5,2},{6,1},{7,4},{8,11},{9,14},{10,... | collective-permute-start | bytes 245768 | tf_op jit(solution)/shard_map/ppermute | solution.py:433
  46.4 9.7 %collective-permute-start.19 = (f32[2,80,128]{2,1,0:T(8,128)S(1)}, f32[2,80,128]{2,1,0:T(8,128)S(1)}, u32[]{:S(2)}, u32[]{:S(2)}) collective-permute-start(f32[2,80,128]{2,1,0:T(8,128)S(1)} %get-tuple-element.61), channel_id=1, source_target_pairs={{0,2},{1,3},{2,0},{3,1},{4,6},{5,7},{6,4},{7,5},{8,10},{9,11},{10,... | collective-permute-start | bytes 245768 | tf_op jit(solution)/shard_map/ppermute | solution.py:433
  (1 other events, 10.0 us)

commit v9 on v6

--- a/solution.py
+++ b/solution.py
@@ -1,4 +1,5 @@
 import functools
+import math
 
 import jax
 import jax.numpy as jnp
@@ -13,6 +14,7 @@
 in_vmem = pl.BlockSpec(memory_space=pltpu.VMEM)
 in_smem = pl.BlockSpec(memory_space=pltpu.SMEM)
 in_hbm = pl.BlockSpec(memory_space=pltpu.HBM)
+in_any = pl.BlockSpec(memory_space=pl.ANY)
 
 
 def to_hbm(value):
@@ -62,7 +64,7 @@
 def partner(me, step, count):
     if count & (count - 1) == 0:
         return me ^ step, me ^ step
-    return lax.rem(me + step, count), lax.rem(me + count - step, count)
+    return (me + step) % count, (me + count - step) % count
 
 
 def gather_fields(halves):
@@ -84,39 +86,57 @@
 
 
 class Message:
-    def __init__(self, count, reach, step=None, slot=None):
-        self.count, self.reach, self.step, self.slot = count, reach, step, slot
-        if slot is not None:
-            offset = slot - reach if slot < reach else slot - reach + 1
-            self.width = 1
-            self.pairs = [(source, (source - offset) % count) for source in range(count)]
-        else:
-            self.pairs = step_pairs(count, step)
-            self.width = 1
-            for source, dest in self.pairs:
-                ahead = (source - dest) % count
-                if ahead <= reach and count - ahead <= reach:
-                    self.width = 2
+    def __init__(self, count, reach, ahead=None, turn=0, slot=None):
+        self.count, self.reach, self.slot = count, reach, slot
+        self.ahead, self.turn = ahead, turn
+        self.width = 1
+        if slot is None and ahead <= reach and count - ahead <= reach:
+            self.width = 2
+        offset = ahead if slot is None else offset_of(slot, reach)
+        self.pairs = [(source, (source - offset) % count) for source in range(count)]
+        if slot is None and turn is not None:
+            self.pairs = [(source, self.mate(source)) for source in range(count)]
+
+    def mate(self, me):
+        upward = 1 - 2 * ((me // math.gcd(self.ahead, self.count) + self.turn) % 2)
+        return (me + upward * self.ahead + self.count) % self.count
+
+    def across(self):
+        half = self.count // 2
+        return self.width * sum((a < half) != (b < half) for a, b in self.pairs)
 
     def slots(self, me, sending):
         if self.slot is not None:
-            return [(self.slot, True)]
+            return [self.slot]
         count, reach = self.count, self.reach
-        dest, source = partner(me, self.step, count)
-        column, row = (me, dest) if sending else (source, me)
-        ahead = lax.rem(column - row + count, count)
-        first = jnp.where(ahead <= reach, ahead + reach - 1, ahead - count + reach)
+        if self.turn is None:
+            ahead = self.ahead
+        else:
+            mate = self.mate(me)
+            ahead = lax.rem((me - mate if sending else mate - me) + count, count)
+        below = ahead - count + reach
         if self.width == 1:
-            return [(first, True)]
-        both = jnp.logical_and(ahead <= reach, count - ahead <= reach)
-        return [(first, True), (jnp.where(both, ahead - count + reach, first), both)]
-
-
-def messages_of(count, slots):
+            return [jnp.where(ahead <= reach, ahead + reach - 1, below)]
+        return [ahead + reach - 1, below]
+
+
+def offset_of(slot, reach):
+    return slot - reach if slot < reach else slot - reach + 1
+
+
+def message_sets_of(count, slots):
     reach = slots // 2
-    if reach < count <= 2 * reach:
-        return [Message(count, reach, step=step) for step in range(count - 1, 0, -1)]
-    return [Message(count, reach, slot=slot) for slot in range(slots)]
+    if not reach < count <= 2 * reach:
+        return [[Message(count, reach, slot=slot) for slot in range(slots)]]
+    messages = []
+    if count & (count - 1) == 0:
+        for ahead in range(1, count // 2 + 1):
+            for turn in range(1 if 2 * ahead == count else 2):
+                messages.append(Message(count, reach, ahead, turn))
+    else:
+        messages = [Message(count, reach, ahead, None) for ahead in range(1, count)]
+    messages.sort(key=lambda message: -message.across())
+    return [messages[: count // 2 - 1], messages[count // 2 - 1 :]]
 
 
 def chunks_of(messages, most=4):
@@ -143,6 +163,7 @@
 
 
 def first_coeff_kernel(messages, fresh, cols_ref, right_ref, *refs):
+    refs = refs if fresh else refs[1:]
     outs, refs = refs[: len(messages)], refs[len(messages) :]
     split_ref = refs[0]
     rank = right_ref.shape[1]
@@ -156,7 +177,7 @@
         right, sems = refs[1:]
     copies = []
     for message in messages:
-        for slot, _ in message.slots(me, True):
+        for slot in message.slots(me, True):
             at = len(copies)
             copies.append(pltpu.make_async_copy(right_ref.at[slot], right.at[at], sems.at[at]))
             copies[-1].start()
@@ -176,7 +197,8 @@
         base = chunk_coefficients(split_ref, base, chunk, messages, rank, both, outs)
 
 
-def first_coefficients(cols, right_tile, messages, fresh):
+def first_coefficients(cols, right_tile, messages, after=None):
+    fresh = after is None
     slots, rank, size = right_tile.shape
     blocks = sum(message.width for message in messages)
     width = cols.shape[1] if fresh else cols.shape[1] // 2
@@ -190,20 +212,19 @@
         functools.partial(first_coeff_kernel, messages, fresh),
         outs,
         [in_vmem] * len(outs),
-        [in_hbm if fresh else in_vmem, in_hbm],
+        [in_hbm, in_hbm] if fresh else [in_vmem, in_hbm, in_any],
         scratch,
         flops=8 * blocks * rank * size * width,
         moved=4 * blocks * rank * (2 * size + width),
-    )(to_hbm(cols) if fresh else cols, to_hbm(right_tile))
+    )(*((to_hbm(cols), to_hbm(right_tile)) if fresh else (cols, to_hbm(right_tile), after)))
     return got[: len(messages)], got[len(messages)], got[-1] if fresh else cols
 
 
-def next_coeff_kernel(message_sets, halves, *refs):
+def mix_coeff_kernel(messages, halves, *refs):
     count = lax.axis_size("kern")
-    fields = refs[: count * halves]
-    weights_ref = refs[count * halves]
-    splits = refs[count * halves + 1 : count * halves + 1 + len(message_sets)]
-    outs, cols_ref = refs[count * halves + 1 + len(message_sets) : -1], refs[-1]
+    fields, refs = refs[: count * halves], refs[count * halves :]
+    weights_ref, split_ref = refs[:2]
+    outs, (cols_ref, both_ref) = refs[2:-2], refs[-2:]
     me = lax.axis_index("kern")
     part = fields[0].shape[0]
     for half in range(halves):
@@ -214,34 +235,52 @@
             term = fields[step * halves + half][...] * weights_ref[source, rows_of]
             total = term if total is None else total + term
         cols_ref[rows_of] = total
-    both = side_by_side(cols_ref[...])
+        both_ref[rows_of] = side_by_side(total)
+    both = both_ref[...]
     rank = outs[0].shape[1]
-    done = 0
-    for messages, split_ref in zip(message_sets, splits):
-        here = outs[done : done + len(messages)]
-        done += len(messages)
-        base = 0
-        for chunk in chunks_of(messages):
-            base = chunk_coefficients(split_ref, base, chunk, messages, rank, both, here)
-
-
-def next_coefficients(fields, weights, splits, message_sets, rank):
+    base = 0
+    for chunk in chunks_of(messages):
+        base = chunk_coefficients(split_ref, base, chunk, messages, rank, both, outs)
+
+
+def mixed_coefficients(fields, weights, split_right, messages, rank):
     halves = len(fields[0])
     part, width = fields[0][0].shape
     size = part * halves
-    outs = [struct(message.width, rank, width) for group in message_sets for message in group]
-    outs.append(struct(size, width))
-    total = sum(split_right.shape[0] for split_right in splits)
+    total = split_right.shape[0]
+    outs = [struct(message.width, rank, width) for message in messages]
+    outs += [struct(size, width), struct(size, 2 * width, dtype=bf16)]
     flat = [half for field in fields for half in field]
     got = call(
-        functools.partial(next_coeff_kernel, message_sets, halves),
+        functools.partial(mix_coeff_kernel, messages, halves),
         outs,
         [in_vmem] * len(outs),
-        [in_vmem] * (len(flat) + 1 + len(splits)),
+        [in_vmem] * (len(flat) + 2),
         flops=4 * total * size * width,
         moved=2 * total * (size + width),
-    )(*flat, weights, *splits)
-    return got[:-1], got[-1]
+    )(*flat, weights, split_right)
+    return got[: len(messages)], got[-2], got[-1]
+
+
+def next_coeff_kernel(messages, both_ref, split_ref, after_ref, *outs):
+    both = both_ref[...]
+    rank = outs[0].shape[1]
+    base = 0
+    for chunk in chunks_of(messages):
+        base = chunk_coefficients(split_ref, base, chunk, messages, rank, both, outs)
+
+
+def next_coefficients(both, split_right, messages, rank, after):
+    size, width = both.shape[0], both.shape[1] // 2
+    total = split_right.shape[0]
+    return call(
+        functools.partial(next_coeff_kernel, messages),
+        [struct(message.width, rank, width) for message in messages],
+        [in_vmem] * len(messages),
+        [in_vmem, in_vmem, in_any],
+        flops=4 * total * size * width,
+        moved=2 * total * (size + width),
+    )(both, split_right, after)
 
 
 def times_diag(diag_ref, cols_ref):
@@ -352,8 +391,8 @@
             picked[pl.ds(pl.multiple_of(term * rank, rank), rank)] = kept
 
     for got, message in zip(gots, messages):
-        for w, (slot, there) in enumerate(message.slots(me, False)):
-            pick(got, w, jnp.where(there, term_of[slot], -1))
+        for w, slot in enumerate(message.slots(me, False)):
+            pick(got, w, term_of[slot])
     both = side_by_side(picked[...])
     part = diag_ref.shape[0] // halves
     sent = []
@@ -415,19 +454,21 @@
     index = block_index[None]
     cols = rhs_field[0]
 
-    messages = messages_of(lax.axis_size("tile"), slots)
-    far = (len(messages) + 1) // 2
-    message_sets = [messages[:far], messages[far:]]
-    gots, splits, given = [], [], cols
-    for group in message_sets:
-        coeffs, split_right, given = first_coefficients(given, right_tile, group, not splits)
+    far, *near = message_sets_of(lax.axis_size("tile"), slots)
+    messages = far + [message for group in near for message in group]
+    coeffs, split_right, both = first_coefficients(cols, right_tile, far)
+    gots, splits = deliver(coeffs, far), [split_right]
+    for group in near:
+        coeffs, split_right, _ = first_coefficients(both, right_tile, group, gots[0])
         gots += deliver(coeffs, group)
         splits.append(split_right)
     diag_part, left_split, weights = prepare(diag_tile, cols, left_rows, table, index, halves)
     first = rows(offsets, ranks, gots, messages, left_split, diag_part, slots, halves, False)
     fields = gather_fields(first)
-    coeffs, cols = next_coefficients(fields, weights, splits, message_sets, rank)
-    gots = deliver(coeffs, messages)
+    coeffs, cols, both = mixed_coefficients(fields, weights, splits[0], far, rank)
+    gots = deliver(coeffs, far)
+    for group, split_right in zip(near, splits[1:]):
+        gots += deliver(next_coefficients(both, split_right, group, rank, gots[0]), group)
     diag_part = diagonal(diag_tile, cols)
     return rows(offsets, ranks, gots, messages, left_split, diag_part, slots, halves, True)[None]
 

time: 56.6 us -> 57.3 us (1.012)
  starting transfers between devices: 25.3 us -> 28.1 us
  waiting for transfers between devices: 20.1 us -> 17.8 us
    ppermute x14, starting transfers between devices: 18.2 us -> 21.7 us  [deliver(): lax.ppermute(sent, 'tile', message.pairs)]
    ppermute x14, waiting for transfers between devices: 14.1 us -> 11.5 us  [deliver(): lax.ppermute(sent, 'tile', message.pairs)]
    ppermute x1, waiting for transfers between devices: 1.32 us -> 0.29 us  [gather_fields(): across_low = lax.ppermute(low, 'kern', across)]
    ppermute x1, waiting for transfers between devices: 0.99 us -> 0.01 us  [gather_fields(): across_high = lax.ppermute(high, 'kern', across)]
    ppermute x1, waiting for transfers between devices: 1.46 us -> 2.3 us  [gather_fields(): last_low = lax.ppermute(near_low, 'kern', across)]
    ppermute x1, waiting for transfers between devices: 1.55 us -> 2.32 us  [gather_fields(): near_low = lax.ppermute(low, 'kern', near)]
    ppermute x1, waiting for transfers between devices: 0.7 us -> 1.34 us  [gather_fields(): last_high = lax.ppermute(across_high, 'kern', near)]
  transfers between devices with their start and end apart: 20 -> 20, of which waited for: 12 -> 10; matrix products, arithmetic and copies ran while one was open for 0% -> 0% of each run, Pallas kernels for 8% -> 9%
where the time goes in v9:
time: 57.3 us; the launch traced here: 57.1 us
  starting transfers between devices  28.1 us (49%)
  waiting for transfers between devices  17.8 us (31%)
  Pallas kernels  11 us (19%)
    ppermute x14, starting transfers between devices, deliver(): lax.ppermute(sent, 'tile', message.pairs)  21.7 us
    ppermute x14, waiting for transfers between devices, deliver(): lax.ppermute(sent, 'tile', message.pairs)  11.5 us
    pallas_call x2, Pallas kernels, first_coefficients(): call(functools.partial(first_coeff_kernel, messages, fresh), outs, [in_vm...  4.01 us
    pallas_call x2, Pallas kernels, rows(): call(functools.partial(row_kernel, messages, halves, final), pltpu.HBM((s...  3.49 us
    ppermute x1, waiting for transfers between devices, gather_fields(): near_low = lax.ppermute(low, 'kern', near)  2.32 us
    ppermute x1, waiting for transfers between devices, gather_fields(): last_low = lax.ppermute(near_low, 'kern', across)  2.3 us
    pallas_call x1, Pallas kernels, prepare(): call(functools.partial(prepare_kernel, halves), [struct(size, width), str...  2.17 us
    ppermute x1, starting transfers between devices, gather_fields(): across_high = lax.ppermute(high, 'kern', across)  1.52 us
  transfers between devices with their start and end apart: 20, of which 10 were waited for; matrix products, arithmetic and copies ran while one was open for 0% of the time, Pallas kernels for 9%

profile of v9, /device:TPU:0, one launch (start us, length us, event | category | flops | bytes accessed | tf_op | source)
XLA Modules:
  0.0 57.1 jit_solution(764936390656376217)
XLA Ops:
  0.0 2.0 %shard_map.82 = (f32[2,80,128]{2,1,0:T(8,128)S(1)}, f32[2,80,128]{2,1,0:T(8,128)S(1)}, f32[2,80,128]{2,1,0:T(8,128)S(1)}, bf16[960,512]{1,0:T(8,128)(2,1)S(1)}, bf16[512,256]{1,0:T(8,128)(2,1)S(1)}) custom-call(f32[512,128]{1,0:T(8,128)} %bitcast.20, f32[12,80,512]{2,1,0:T(8,128)} %bitcast.17), custom_call_target="tpu_custom_call" | custom-call | flops 251658240 | bytes 2211840 | tf_op jit(solution)/shard_map/pallas_call | solution.py:211
  2.0 5.1 %collective-permute-start = (f32[2,80,128]{2,1,0:T(8,128)S(1)}, f32[2,80,128]{2,1,0:T(8,128)S(1)}, u32[]{:S(2)}, u32[]{:S(2)}) collective-permute-start(f32[2,80,128]{2,1,0:T(8,128)S(1)} %get-tuple-element.29), channel_id=1, source_target_pairs={{0,6},{1,7},{2,4},{3,5},{4,2},{5,3},{6,0},{7,1},{8,14},{9,15},{10,... | collective-permute-start | bytes 245768 | tf_op jit(solution)/shard_map/ppermute | solution.py:433
  7.2 2.1 %collective-permute-start.2 = (f32[2,80,128]{2,1,0:T(8,128)S(1)}, f32[2,80,128]{2,1,0:T(8,128)S(1)}, u32[]{:S(2)}, u32[]{:S(2)}) collective-permute-start(f32[2,80,128]{2,1,0:T(8,128)S(1)} %get-tuple-element.31), channel_id=1, source_target_pairs={{0,4},{1,5},{2,6},{3,7},{4,0},{5,1},{6,2},{7,3},{8,12},{9,13},{10,... | collective-permute-start | bytes 245768 | tf_op jit(solution)/shard_map/ppermute | solution.py:433
  9.8 2.0 %shard_map.83 = (f32[2,80,128]{2,1,0:T(8,128)S(1)}, f32[1,80,128]{2,1,0:T(8,128)S(1)}, f32[1,80,128]{2,1,0:T(8,128)S(1)}, f32[2,80,128]{2,1,0:T(8,128)S(1)}, bf16[960,512]{1,0:T(8,128)(2,1)S(1)}) custom-call(bf16[512,256]{1,0:T(8,128)(2,1)S(1)} %get-tuple-element.32.cols_ref, f32[12,80,512]{2,1,0:T(8,128)} %bitcast.18, ...), custom_call_target="tpu_custom_call" | custom-call | flops 251658240 | bytes 2211840 | tf_op jit(solution)/shard_map/pallas_call | solution.py:211
  11.9 5.5 %collective-permute-start.6 = (f32[2,80,128]{2,1,0:T(8,128)S(1)}, f32[2,80,128]{2,1,0:T(8,128)S(1)}, u32[]{:S(2)}, u32[]{:S(2)}) collective-permute-start(f32[2,80,128]{2,1,0:T(8,128)S(1)} %get-tuple-element.36), channel_id=1, source_target_pairs={{0,2},{1,3},{2,0},{3,1},{4,6},{5,7},{6,4},{7,5},{8,10},{9,11},{10,... | collective-permute-start | bytes 245768 | tf_op jit(solution)/shard_map/ppermute | solution.py:433
  17.4 2.3 %collective-permute-start.4 = (f32[1,80,128]{2,1,0:T(8,128)S(1)}, f32[1,80,128]{2,1,0:T(8,128)S(1)}, u32[]{:S(2)}, u32[]{:S(2)}) collective-permute-start(f32[1,80,128]{2,1,0:T(8,128)S(1)} %get-tuple-element.34), channel_id=1, source_target_pairs={{0,7},{1,2},{2,1},{3,4},{4,3},{5,6},{6,5},{7,0},{8,15},{9,10},{10,... | collective-permute-start | bytes 122888 | tf_op jit(solution)/shard_map/ppermute | solution.py:433
  19.8 2.2 %shard_map.84 = (f32[512,128]{1,0:T(8,128)S(1)}, bf16[1024,640]{1,0:T(8,128)(2,1)S(1)}, f32[4,512,128]{2,1,0:T(8,128)S(1)}) custom-call(f32[512,512]{1,0:T(8,128)} %bitcast.9, f32[512,128]{1,0:T(8,128)} %bitcast.21, f32[640,512]{1,0:T(8,128)} %bitcast.19, f32[4,4,64]{2,1,0:T(4,128)S(1)} %bitcast.11, s32[1,512]{1,0:T(1,128)S(1)} %bitcast.12), custom_call_target="tpu_custom_call" | custom-call | flops 268435456 | bytes 4194304 | tf_op jit(solution)/shard_map/pallas_call | solution.py:347
  21.9 2.4 %collective-permute-done.4.refs_4_ = f32[1,80,128]{2,1,0:T(8,128)S(1)} collective-permute-done((f32[1,80,128]{2,1,0:T(8,128)S(1)}, f32[1,80,128]{2,1,0:T(8,128)S(1)}, u32[]{:S(2)}, u32[]{:S(2)}) %collective-permute-start.4) | collective-permute-done | bytes 40992 | tf_op jit(solution)/shard_map/ppermute | solution.py:433
  24.3 1.4 %shard_map.85 = (f32[256,128]{1,0:T(8,128)S(1)}, f32[256,128]{1,0:T(8,128)S(1)}) custom-call(s32[1,8]{1,0:T(1,128)S(1)} %bitcast.13, s32[1,8]{1,0:T(1,128)S(1)} %bitcast.15, f32[2,80,128]{2,1,0:T(8,128)S(1)} %collective-permute-done.refs_0_, f32[2,80,128]{2,1,0:T(8,128)S(1)} %collective-permute-done.1.refs_1_, ...), custom_call_target="tpu_custom_call" | custom-call | flops 335544320 | bytes 1638400 | tf_op jit(solution)/shard_map/pallas_call | solution.py:421
  25.7 1.4 %collective-permute-start.7 = (f32[256,128]{1,0:T(8,128)S(1)}, f32[256,128]{1,0:T(8,128)S(1)}, u32[]{:S(2)}, u32[]{:S(2)}) collective-permute-start(f32[256,128]{1,0:T(8,128)S(1)} %get-tuple-element.39.refs_0_), channel_id=1, source_target_pairs={{0,8},{8,0},{16,24},{24,16},{1,9},{9,1},{17,25},{25,17},{2,10},{10... | collective-permute-start | bytes 393224 | tf_op jit(solution)/shard_map/ppermute | solution.py:75
  27.1 1.5 %collective-permute-start.10 = (f32[256,128]{1,0:T(8,128)S(1)}, f32[256,128]{1,0:T(8,128)S(1)}, u32[]{:S(2)}, u32[]{:S(2)}) collective-permute-start(f32[256,128]{1,0:T(8,128)S(1)} %get-tuple-element.40.refs_1_), channel_id=1, source_target_pairs={{0,16},{8,24},{16,0},{24,8},{1,17},{9,25},{17,1},{25,9},{2,18},{10... | collective-permute-start | bytes 393224 | tf_op jit(solution)/shard_map/ppermute | solution.py:76
  29.1 0.7 %collective-permute-start.8 = (f32[256,128]{1,0:T(8,128)S(1)}, f32[256,128]{1,0:T(8,128)S(1)}, u32[]{:S(2)}, u32[]{:S(2)}) collective-permute-start(f32[256,128]{1,0:T(8,128)S(1)} %get-tuple-element.40.refs_1_), channel_id=1, source_target_pairs={{0,8},{8,0},{16,24},{24,16},{1,9},{9,1},{17,25},{25,17},{2,10},{10... | collective-permute-start | bytes 393224 | tf_op jit(solution)/shard_map/ppermute | solution.py:77
  29.8 2.3 %collective-permute-done.7.refs_2_ = f32[256,128]{1,0:T(8,128)S(1)} collective-permute-done((f32[256,128]{1,0:T(8,128)S(1)}, f32[256,128]{1,0:T(8,128)S(1)}, u32[]{:S(2)}, u32[]{:S(2)}) %collective-permute-start.7) | collective-permute-done | bytes 131104 | tf_op jit(solution)/shard_map/ppermute | solution.py:75
  32.1 1.3 %collective-permute-start.11 = (f32[256,128]{1,0:T(8,128)S(1)}, f32[256,128]{1,0:T(8,128)S(1)}, u32[]{:S(2)}, u32[]{:S(2)}) collective-permute-start(f32[256,128]{1,0:T(8,128)S(1)} %collective-permute-done.7.refs_2_), channel_id=1, source_target_pairs={{0,16},{8,24},{16,0},{24,8},{1,17},{9,25},{17,1},{25,9},{2,18},{10... | collective-permute-start | bytes 393224 | tf_op jit(solution)/shard_map/ppermute | solution.py:79
  33.5 1.0 %collective-permute-start.12 = (f32[256,128]{1,0:T(8,128)S(1)}, f32[256,128]{1,0:T(8,128)S(1)}, u32[]{:S(2)}, u32[]{:S(2)}) collective-permute-start(f32[256,128]{1,0:T(8,128)S(1)} %collective-permute-done.10.refs_5_), channel_id=1, source_target_pairs={{0,8},{8,0},{16,24},{24,16},{1,9},{9,1},{17,25},{25,17},{2,10},{10... | collective-permute-start | bytes 393224 | tf_op jit(solution)/shard_map/ppermute | solution.py:80
  34.8 2.3 %collective-permute-done.11.refs_6_ = f32[256,128]{1,0:T(8,128)S(1)} collective-permute-done((f32[256,128]{1,0:T(8,128)S(1)}, f32[256,128]{1,0:T(8,128)S(1)}, u32[]{:S(2)}, u32[]{:S(2)}) %collective-permute-start.11) | collective-permute-done | bytes 131104 | tf_op jit(solution)/shard_map/ppermute | solution.py:79
  37.1 1.3 %collective-permute-done.12.refs_7_ = f32[256,128]{1,0:T(8,128)S(1)} collective-permute-done((f32[256,128]{1,0:T(8,128)S(1)}, f32[256,128]{1,0:T(8,128)S(1)}, u32[]{:S(2)}, u32[]{:S(2)}) %collective-permute-start.12) | collective-permute-done | bytes 131104 | tf_op jit(solution)/shard_map/ppermute | solution.py:80
  38.9 0.8 %collective-permute-start.13 = (f32[2,80,128]{2,1,0:T(8,128)S(1)}, f32[2,80,128]{2,1,0:T(8,128)S(1)}, u32[]{:S(2)}, u32[]{:S(2)}) collective-permute-start(f32[2,80,128]{2,1,0:T(8,128)S(1)} %get-tuple-element.43), channel_id=1, source_target_pairs={{0,6},{1,7},{2,4},{3,5},{4,2},{5,3},{6,0},{7,1},{8,14},{9,15},{10,... | collective-permute-start | bytes 245768 | tf_op jit(solution)/shard_map/ppermute | solution.py:433
  39.8 1.3 %collective-permute-start.15 = (f32[2,80,128]{2,1,0:T(8,128)S(1)}, f32[2,80,128]{2,1,0:T(8,128)S(1)}, u32[]{:S(2)}, u32[]{:S(2)}) collective-permute-start(f32[2,80,128]{2,1,0:T(8,128)S(1)} %get-tuple-element.45), channel_id=1, source_target_pairs={{0,4},{1,5},{2,6},{3,7},{4,0},{5,1},{6,2},{7,3},{8,12},{9,13},{10,... | collective-permute-start | bytes 245768 | tf_op jit(solution)/shard_map/ppermute | solution.py:433
  41.1 4.3 %collective-permute-done.13.after_ref.refs_0_ = f32[2,80,128]{2,1,0:T(8,128)S(1)} collective-permute-done((f32[2,80,128]{2,1,0:T(8,128)S(1)}, f32[2,80,128]{2,1,0:T(8,128)S(1)}, u32[]{:S(2)}, u32[]{:S(2)}) %collective-permute-start.13) | collective-permute-done | bytes 81952 | tf_op jit(solution)/shard_map/ppermute | solution.py:433
  45.9 1.2 %collective-permute-start.19 = (f32[2,80,128]{2,1,0:T(8,128)S(1)}, f32[2,80,128]{2,1,0:T(8,128)S(1)}, u32[]{:S(2)}, u32[]{:S(2)}) collective-permute-start(f32[2,80,128]{2,1,0:T(8,128)S(1)} %get-tuple-element.51), channel_id=1, source_target_pairs={{0,2},{1,3},{2,0},{3,1},{4,6},{5,7},{6,4},{7,5},{8,10},{9,11},{10,... | collective-permute-start | bytes 245768 | tf_op jit(solution)/shard_map/ppermute | solution.py:433
  47.1 3.2 %collective-permute-start.17 = (f32[1,80,128]{2,1,0:T(8,128)S(1)}, f32[1,80,128]{2,1,0:T(8,128)S(1)}, u32[]{:S(2)}, u32[]{:S(2)}) collective-permute-start(f32[1,80,128]{2,1,0:T(8,128)S(1)} %get-tuple-element.49), channel_id=1, source_target_pairs={{0,7},{1,2},{2,1},{3,4},{4,3},{5,6},{6,5},{7,0},{8,15},{9,10},{10,... | collective-permute-start | bytes 122888 | tf_op jit(solution)/shard_map/ppermute | solution.py:433
  50.9 4.1 %collective-permute-done.17.refs_4_ = f32[1,80,128]{2,1,0:T(8,128)S(1)} collective-permute-done((f32[1,80,128]{2,1,0:T(8,128)S(1)}, f32[1,80,128]{2,1,0:T(8,128)S(1)}, u32[]{:S(2)}, u32[]{:S(2)}) %collective-permute-start.17) | collective-permute-done | bytes 40992 | tf_op jit(solution)/shard_map/ppermute | solution.py:433
  55.0 2.1 %shard_map.89 = f32[512,128]{1,0:T(8,128)} custom-call(s32[1,8]{1,0:T(1,128)S(1)} %bitcast.14, s32[1,8]{1,0:T(1,128)S(1)} %bitcast.16, f32[2,80,128]{2,1,0:T(8,128)S(1)} %collective-permute-done.13.after_ref.refs_0_, f32[2,80,128]{2,1,0:T(8,128)S(1)} %collective-permute-done.14.refs_1_, f32[2,80,128]{2,1,0:T(8,128)S(1)} %collective-permute-done.15.refs_2_, ...), custom_call_target="tpu_custom_call" | custom-call | flops 335544320 | bytes 1638400 | tf_op jit(solution)/shard_map/pallas_call | solution.py:421
  (34 shorter events, 3.1 us)
Async XLA Ops:
  2.0 17.7 %copy-start.1 = (f32[64,4,4]{0,2,1:T(4,128)S(1)}, f32[64,4,4]{0,2,1:T(4,128)}, u32[]{:S(2)}) copy-start(f32[64,4,4]{0,2,1:T(4,128)} %param.13) | copy-start | bytes 12292
  2.0 17.7 %copy-start.2 = (s32[512]{0:T(512)S(1)}, s32[512]{0:T(512)}, u32[]{:S(2)}) copy-start(s32[512]{0:T(512)} %param.14) | copy-start | bytes 6148
  2.0 7.7 %collective-permute-start = (f32[2,80,128]{2,1,0:T(8,128)S(1)}, f32[2,80,128]{2,1,0:T(8,128)S(1)}, u32[]{:S(2)}, u32[]{:S(2)}) collective-permute-start(f32[2,80,128]{2,1,0:T(8,128)S(1)} %get-tuple-element.29), channel_id=1, source_target_pairs={{0,6},{1,7},{2,4},{3,5},{4,2},{5,3},{6,0},{7,1},{8,14},{9,15},{10,... | collective-permute-start | bytes 245768 | tf_op jit(solution)/shard_map/ppermute | solution.py:433
  7.2 12.5 %collective-permute-start.1 = (f32[2,80,128]{2,1,0:T(8,128)S(1)}, f32[2,80,128]{2,1,0:T(8,128)S(1)}, u32[]{:S(2)}, u32[]{:S(2)}) collective-permute-start(f32[2,80,128]{2,1,0:T(8,128)S(1)} %get-tuple-element.30), channel_id=1, source_target_pairs={{0,5},{1,4},{2,7},{3,6},{4,1},{5,0},{6,3},{7,2},{8,13},{9,12},{10,... | collective-permute-start | bytes 245768 | tf_op jit(solution)/shard_map/ppermute | solution.py:433
  7.2 14.8 %collective-permute-start.2 = (f32[2,80,128]{2,1,0:T(8,128)S(1)}, f32[2,80,128]{2,1,0:T(8,128)S(1)}, u32[]{:S(2)}, u32[]{:S(2)}) collective-permute-start(f32[2,80,128]{2,1,0:T(8,128)S(1)} %get-tuple-element.31), channel_id=1, source_target_pairs={{0,4},{1,5},{2,6},{3,7},{4,0},{5,1},{6,2},{7,3},{8,12},{9,13},{10,... | collective-permute-start | bytes 245768 | tf_op jit(solution)/shard_map/ppermute | solution.py:433
  11.8 12.5 %collective-permute-start.3 = (f32[2,80,128]{2,1,0:T(8,128)S(1)}, f32[2,80,128]{2,1,0:T(8,128)S(1)}, u32[]{:S(2)}, u32[]{:S(2)}) collective-permute-start(f32[2,80,128]{2,1,0:T(8,128)S(1)} %get-tuple-element.33), channel_id=1, source_target_pairs={{0,3},{1,6},{2,5},{3,0},{4,7},{5,2},{6,1},{7,4},{8,11},{9,14},{10,... | collective-permute-start | bytes 245768 | tf_op jit(solution)/shard_map/ppermute | solution.py:433
  11.9 12.4 %collective-permute-start.6 = (f32[2,80,128]{2,1,0:T(8,128)S(1)}, f32[2,80,128]{2,1,0:T(8,128)S(1)}, u32[]{:S(2)}, u32[]{:S(2)}) collective-permute-start(f32[2,80,128]{2,1,0:T(8,128)S(1)} %get-tuple-element.36), channel_id=1, source_target_pairs={{0,2},{1,3},{2,0},{3,1},{4,6},{5,7},{6,4},{7,5},{8,10},{9,11},{10,... | collective-permute-start | bytes 245768 | tf_op jit(solution)/shard_map/ppermute | solution.py:433
  17.4 6.9 %collective-permute-start.4 = (f32[1,80,128]{2,1,0:T(8,128)S(1)}, f32[1,80,128]{2,1,0:T(8,128)S(1)}, u32[]{:S(2)}, u32[]{:S(2)}) collective-permute-start(f32[1,80,128]{2,1,0:T(8,128)S(1)} %get-tuple-element.34), channel_id=1, source_target_pairs={{0,7},{1,2},{2,1},{3,4},{4,3},{5,6},{6,5},{7,0},{8,15},{9,10},{10,... | collective-permute-start | bytes 122888 | tf_op jit(solution)/shard_map/ppermute | solution.py:433
  19.7 4.6 %collective-permute-start.5 = (f32[1,80,128]{2,1,0:T(8,128)S(1)}, f32[1,80,128]{2,1,0:T(8,128)S(1)}, u32[]{:S(2)}, u32[]{:S(2)}) collective-permute-start(f32[1,80,128]{2,1,0:T(8,128)S(1)} %get-tuple-element.35), channel_id=1, source_target_pairs={{0,1},{1,0},{2,3},{3,2},{4,5},{5,4},{6,7},{7,6},{8,9},{9,8},{10,11... | collective-permute-start | bytes 122888 | tf_op jit(solution)/shard_map/ppermute | solution.py:433
  19.7 4.6 %copy-start.3 = (s32[1,1,8]{2,1,0:T(1,128)S(1)}, s32[1,1,8]{2,1,0:T(1,128)}, u32[]{:S(2)}) copy-start(s32[1,1,8]{2,1,0:T(1,128)} %param.11) | copy-start | bytes 100
  25.7 6.4 %collective-permute-start.7 = (f32[256,128]{1,0:T(8,128)S(1)}, f32[256,128]{1,0:T(8,128)S(1)}, u32[]{:S(2)}, u32[]{:S(2)}) collective-permute-start(f32[256,128]{1,0:T(8,128)S(1)} %get-tuple-element.39.refs_0_), channel_id=1, source_target_pairs={{0,8},{8,0},{16,24},{24,16},{1,9},{9,1},{17,25},{25,17},{2,10},{10... | collective-permute-start | bytes 393224 | tf_op jit(solution)/shard_map/ppermute | solution.py:75
  27.1 6.4 %collective-permute-start.10 = (f32[256,128]{1,0:T(8,128)S(1)}, f32[256,128]{1,0:T(8,128)S(1)}, u32[]{:S(2)}, u32[]{:S(2)}) collective-permute-start(f32[256,128]{1,0:T(8,128)S(1)} %get-tuple-element.40.refs_1_), channel_id=1, source_target_pairs={{0,16},{8,24},{16,0},{24,8},{1,17},{9,25},{17,1},{25,9},{2,18},{10... | collective-permute-start | bytes 393224 | tf_op jit(solution)/shard_map/ppermute | solution.py:76
  28.6 6.1 %collective-permute-start.9 = (f32[256,128]{1,0:T(8,128)S(1)}, f32[256,128]{1,0:T(8,128)S(1)}, u32[]{:S(2)}, u32[]{:S(2)}) collective-permute-start(f32[256,128]{1,0:T(8,128)S(1)} %get-tuple-element.39.refs_0_), channel_id=1, source_target_pairs={{0,16},{8,24},{16,0},{24,8},{1,17},{9,25},{17,1},{25,9},{2,18},{10... | collective-permute-start | bytes 393224 | tf_op jit(solution)/shard_map/ppermute | solution.py:78
  29.1 5.7 %collective-permute-start.8 = (f32[256,128]{1,0:T(8,128)S(1)}, f32[256,128]{1,0:T(8,128)S(1)}, u32[]{:S(2)}, u32[]{:S(2)}) collective-permute-start(f32[256,128]{1,0:T(8,128)S(1)} %get-tuple-element.40.refs_1_), channel_id=1, source_target_pairs={{0,8},{8,0},{16,24},{24,16},{1,9},{9,1},{17,25},{25,17},{2,10},{10... | collective-permute-start | bytes 393224 | tf_op jit(solution)/shard_map/ppermute | solution.py:77
  32.1 5.0 %collective-permute-start.11 = (f32[256,128]{1,0:T(8,128)S(1)}, f32[256,128]{1,0:T(8,128)S(1)}, u32[]{:S(2)}, u32[]{:S(2)}) collective-permute-start(f32[256,128]{1,0:T(8,128)S(1)} %collective-permute-done.7.refs_2_), channel_id=1, source_target_pairs={{0,16},{8,24},{16,0},{24,8},{1,17},{9,25},{17,1},{25,9},{2,18},{10... | collective-permute-start | bytes 393224 | tf_op jit(solution)/shard_map/ppermute | solution.py:79
  33.5 5.0 %collective-permute-start.12 = (f32[256,128]{1,0:T(8,128)S(1)}, f32[256,128]{1,0:T(8,128)S(1)}, u32[]{:S(2)}, u32[]{:S(2)}) collective-permute-start(f32[256,128]{1,0:T(8,128)S(1)} %collective-permute-done.10.refs_5_), channel_id=1, source_target_pairs={{0,8},{8,0},{16,24},{24,16},{1,9},{9,1},{17,25},{25,17},{2,10},{10... | collective-permute-start | bytes 393224 | tf_op jit(solution)/shard_map/ppermute | solution.py:80
  38.9 11.3 %copy-start = (f32[1,1,512,512]{3,2,1,0:T(8,128)S(1)}, f32[1,1,512,512]{3,2,1,0:T(8,128)}, u32[]{:S(2)}) copy-start(f32[1,1,512,512]{3,2,1,0:T(8,128)} %param.8) | copy-start | bytes 3145732
  38.9 6.4 %collective-permute-start.13 = (f32[2,80,128]{2,1,0:T(8,128)S(1)}, f32[2,80,128]{2,1,0:T(8,128)S(1)}, u32[]{:S(2)}, u32[]{:S(2)}) collective-permute-start(f32[2,80,128]{2,1,0:T(8,128)S(1)} %get-tuple-element.43), channel_id=1, source_target_pairs={{0,6},{1,7},{2,4},{3,5},{4,2},{5,3},{6,0},{7,1},{8,14},{9,15},{10,... | collective-permute-start | bytes 245768 | tf_op jit(solution)/shard_map/ppermute | solution.py:433
  39.8 10.4 %collective-permute-start.14 = (f32[2,80,128]{2,1,0:T(8,128)S(1)}, f32[2,80,128]{2,1,0:T(8,128)S(1)}, u32[]{:S(2)}, u32[]{:S(2)}) collective-permute-start(f32[2,80,128]{2,1,0:T(8,128)S(1)} %get-tuple-element.44), channel_id=1, source_target_pairs={{0,5},{1,4},{2,7},{3,6},{4,1},{5,0},{6,3},{7,2},{8,13},{9,12},{10,... | collective-permute-start | bytes 245768 | tf_op jit(solution)/shard_map/ppermute | solution.py:433
  39.8 11.1 %collective-permute-start.15 = (f32[2,80,128]{2,1,0:T(8,128)S(1)}, f32[2,80,128]{2,1,0:T(8,128)S(1)}, u32[]{:S(2)}, u32[]{:S(2)}) collective-permute-start(f32[2,80,128]{2,1,0:T(8,128)S(1)} %get-tuple-element.45), channel_id=1, source_target_pairs={{0,4},{1,5},{2,6},{3,7},{4,0},{5,1},{6,2},{7,3},{8,12},{9,13},{10,... | collective-permute-start | bytes 245768 | tf_op jit(solution)/shard_map/ppermute | solution.py:433
  45.8 9.2 %collective-permute-start.16 = (f32[2,80,128]{2,1,0:T(8,128)S(1)}, f32[2,80,128]{2,1,0:T(8,128)S(1)}, u32[]{:S(2)}, u32[]{:S(2)}) collective-permute-start(f32[2,80,128]{2,1,0:T(8,128)S(1)} %get-tuple-element.48), channel_id=1, source_target_pairs={{0,3},{1,6},{2,5},{3,0},{4,7},{5,2},{6,1},{7,4},{8,11},{9,14},{10,... | collective-permute-start | bytes 245768 | tf_op jit(solution)/shard_map/ppermute | solution.py:433
  45.9 9.1 %collective-permute-start.19 = (f32[2,80,128]{2,1,0:T(8,128)S(1)}, f32[2,80,128]{2,1,0:T(8,128)S(1)}, u32[]{:S(2)}, u32[]{:S(2)}) collective-permute-start(f32[2,80,128]{2,1,0:T(8,128)S(1)} %get-tuple-element.51), channel_id=1, source_target_pairs={{0,2},{1,3},{2,0},{3,1},{4,6},{5,7},{6,4},{7,5},{8,10},{9,11},{10,... | collective-permute-start | bytes 245768 | tf_op jit(solution)/shard_map/ppermute | solution.py:433
  47.1 7.9 %collective-permute-start.17 = (f32[1,80,128]{2,1,0:T(8,128)S(1)}, f32[1,80,128]{2,1,0:T(8,128)S(1)}, u32[]{:S(2)}, u32[]{:S(2)}) collective-permute-start(f32[1,80,128]{2,1,0:T(8,128)S(1)} %get-tuple-element.49), channel_id=1, source_target_pairs={{0,7},{1,2},{2,1},{3,4},{4,3},{5,6},{6,5},{7,0},{8,15},{9,10},{10,... | collective-permute-start | bytes 122888 | tf_op jit(solution)/shard_map/ppermute | solution.py:433
  50.2 4.8 %collective-permute-start.18 = (f32[1,80,128]{2,1,0:T(8,128)S(1)}, f32[1,80,128]{2,1,0:T(8,128)S(1)}, u32[]{:S(2)}, u32[]{:S(2)}) collective-permute-start(f32[1,80,128]{2,1,0:T(8,128)S(1)} %get-tuple-element.50), channel_id=1, source_target_pairs={{0,1},{1,0},{2,3},{3,2},{4,5},{5,4},{6,7},{7,6},{8,9},{9,8},{10,11... | collective-permute-start | bytes 122888 | tf_op jit(solution)/shard_map/ppermute | solution.py:433
  (1 other events, 4.6 us)
